TPU v7x, 32 devices: a whole 2x2x4 slice. The times are simulated.
32 devices in a mesh: tensor: 4 (over x, core), dp: 2 (over y), context: 4 (over z).
Axes of the slice: x: 2, y: 2, z: 4, core: 2. Of those that a mesh axis runs over, the one named last changes fastest.
Arguments:
- tokens: bfloat16 [2, 2048, 2048], P('dp', 'context'), may hold values from -6 to 6
- segments: int32 [2, 2048], P('dp', 'context'), may hold values from 0 to 2047, as said below
- gain_one: float32 [2048], replicated, may hold values from 0.1 to 1.9
- w_query: bfloat16 [2048, 2048], P(None, 'tensor'), may hold values from -0.125 to 0.125
- w_keyval: bfloat16 [2048, 4, 128], P(None, 'tensor'), may hold values from -0.125 to 0.125
- w_out: bfloat16 [2048, 2048], P('tensor'), may hold values from -1 to 1
- gain_two: float32 [2048], replicated, may hold values from 0.1 to 1.9
- w_gateup: bfloat16 [2048, 2, 5632], P(None, None, 'tensor'), may hold values from -0.125 to 0.125
- w_down: bfloat16 [5632, 2048], P('tensor'), may hold values from -0.078125 to 0.078125
- cotangent: bfloat16 [2, 2048, 2048], P('dp', 'context'), may hold values from -6 to 6
Outputs:
- mixed: bfloat16 [2, 2048, 2048], P('dp', 'context')
- grad_tokens: float32 [2, 2048, 2048], P('dp', 'context')
- grad_gain_one: float32 [2048], P(('dp', 'context'))
- grad_wquery: float32 [2048, 2048], P(('dp', 'context'), 'tensor')
- grad_wkeyval: float32 [2048, 4, 128], P(('dp', 'context'), 'tensor')
- grad_wout: float32 [2048, 2048], P('tensor', ('dp', 'context'))
- grad_gain_two: float32 [2048], P(('dp', 'context'))
- grad_wgateup: float32 [2048, 2, 5632], P(('dp', 'context'), None, 'tensor')
- grad_wdown: float32 [5632, 2048], P('tensor', ('dp', 'context'))
Inputs may be any that keep to these rules, and one draw needn't show every extreme that they name: `segments`: each token holds the index, within its sequence, of its document's first token, so values never fall along a sequence. In each sequence one document begins among the first 512 tokens and ends among the last 512, and the last token begins a document of its own.
All inputs are finite; a program needn't handle non-finite values.
Results may differ from a plain program's by a relative error of at most 0.024.
Values may be sent and summed in bfloat16 or wider, within the bound.
A program may use at most 256 MiB of HBM per device.

v0:
```python
import math

import jax
import jax.numpy as jnp
from jax import lax
from jax.sharding import PartitionSpec as P

HD = 64


epsilon = 1e-05
neg_large = -1e30


def rotate(values, cosine, sine):
    half_width = values.shape[-1] // 2
    first_half = values[..., :half_width]
    second_half = values[..., half_width:]
    return jnp.concatenate(
        [first_half * cosine - second_half * sine, second_half * cosine + first_half * sine], -1
    )


def angles(positions, head_dim):
    freqs = 10000.0 ** (-(jnp.arange(head_dim // 2, dtype=jnp.float32) * 2.0) / head_dim)
    phase = positions.astype(jnp.float32)[:, None] * freqs[None, :]
    return (jnp.cos(phase), jnp.sin(phase))


def norm_back(inputs, inverse, gain, grad_normed):
    grad_gain = jnp.sum(grad_normed * inputs * inverse, 0)
    scaled = grad_normed * gain
    grad_inputs = inverse * scaled - inputs * (inverse * inverse * inverse) * jnp.mean(
        scaled * inputs, -1, keepdims=True
    )
    return (grad_inputs, grad_gain)


def key_blocks_of(keys_all, seg_all, head_dim):
    length = keys_all.shape[0]
    block_len = min(512, length)
    blocks = length // block_len
    key_blocks = keys_all.reshape(blocks, block_len, keys_all.shape[1], 2 * head_dim)
    seg_blocks = seg_all.reshape(blocks, block_len)
    index_blocks = jnp.arange(length, dtype=jnp.int32).reshape(blocks, block_len)
    return (key_blocks, seg_blocks, index_blocks, block_len)


def block_scores(queries, key_part, query_index, query_seg, key_index, key_seg, scale):
    raw = (
        jnp.einsum("qkgd,pkd->kgqp", queries, key_part, preferred_element_type=jnp.float32) * scale
    )
    allowed = (key_index[None, :] <= query_index[:, None]) & (
        key_seg[None, :] == query_seg[:, None]
    )
    return (raw, allowed)


def attend(queries, query_index, query_seg, keys_all, seg_all, head_dim):
    key_blocks, seg_blocks, index_blocks, block_len = key_blocks_of(keys_all, seg_all, head_dim)
    scale = 1.0 / math.sqrt(head_dim)
    heads_kv, group, tok_count = (queries.shape[1], queries.shape[2], queries.shape[0])

    def useful(index_blk, seg_blk):
        return (index_blk[0] <= query_index[-1]) & (seg_blk[-1] >= query_seg[0])

    def keep(carry):
        return carry

    def stats_step(carry, items):
        key_blk, seg_blk, index_blk = items

        def stats_compute(carry):
            running_max, running_sum = carry
            raw, allowed = block_scores(
                queries, key_blk[..., :head_dim], query_index, query_seg, index_blk, seg_blk, scale
            )
            masked = jnp.where(allowed, raw, neg_large)
            new_max = jnp.maximum(running_max, jnp.max(masked, -1))
            weights = jnp.where(allowed, jnp.exp(masked - new_max[..., None]), 0.0)
            return (new_max, running_sum * jnp.exp(running_max - new_max) + jnp.sum(weights, -1))

        return (lax.cond(useful(index_blk, seg_blk), stats_compute, keep, carry), None)

    start_max = jnp.full((heads_kv, group, tok_count), neg_large, jnp.float32)
    start_sum = jnp.zeros((heads_kv, group, tok_count), jnp.float32)
    (final_max, final_sum), unused = lax.scan(
        stats_step, (start_max, start_sum), (key_blocks, seg_blocks, index_blocks)
    )
    log_total = final_max + jnp.log(final_sum)

    def output_step(accum, items):
        key_blk, seg_blk, index_blk = items

        def output_compute(accum):
            raw, allowed = block_scores(
                queries, key_blk[..., :head_dim], query_index, query_seg, index_blk, seg_blk, scale
            )
            probs = jnp.where(allowed, jnp.exp(raw - log_total[..., None]), 0.0).astype(
                jnp.bfloat16
            )
            return accum + jnp.einsum(
                "kgqp,pkd->qkgd", probs, key_blk[..., head_dim:], preferred_element_type=jnp.float32
            )

        return (lax.cond(useful(index_blk, seg_blk), output_compute, keep, accum), None)

    start_out = jnp.zeros((tok_count, heads_kv, group, head_dim), jnp.float32)
    attended, unused = lax.scan(output_step, start_out, (key_blocks, seg_blocks, index_blocks))
    return (attended, log_total)


def attend_back(
    queries, query_index, query_seg, keys_all, seg_all, grad_attended, attended, log_total, head_dim
):
    key_blocks, seg_blocks, index_blocks, block_len = key_blocks_of(keys_all, seg_all, head_dim)
    scale = 1.0 / math.sqrt(head_dim)
    heads_kv = queries.shape[1]
    delta = jnp.transpose(jnp.sum(grad_attended.astype(jnp.float32) * attended, -1), (1, 2, 0))

    def back_step(grad_q, items):
        key_blk, seg_blk, index_blk = items

        def back_compute(grad_q):
            raw, allowed = block_scores(
                queries, key_blk[..., :head_dim], query_index, query_seg, index_blk, seg_blk, scale
            )
            probs = jnp.where(allowed, jnp.exp(raw - log_total[..., None]), 0.0)
            grad_probs = jnp.einsum(
                "qkgd,pkd->kgqp",
                grad_attended,
                key_blk[..., head_dim:],
                preferred_element_type=jnp.float32,
            )
            grad_raw = (probs * (grad_probs - delta[..., None])).astype(jnp.bfloat16)
            grad_q = (
                grad_q
                + jnp.einsum(
                    "kgqp,pkd->qkgd",
                    grad_raw,
                    key_blk[..., :head_dim],
                    preferred_element_type=jnp.float32,
                )
                * scale
            )
            grad_key = (
                jnp.einsum("kgqp,qkgd->pkd", grad_raw, queries, preferred_element_type=jnp.float32)
                * scale
            )
            grad_value = jnp.einsum(
                "kgqp,qkgd->pkd",
                probs.astype(jnp.bfloat16),
                grad_attended,
                preferred_element_type=jnp.float32,
            )
            return (grad_q, jnp.concatenate([grad_key, grad_value], -1))

        def skip(grad_q):
            return (grad_q, jnp.zeros((block_len, heads_kv, 2 * head_dim), jnp.float32))

        return lax.cond(
            (index_blk[0] <= query_index[-1]) & (seg_blk[-1] >= query_seg[0]),
            back_compute,
            skip,
            grad_q,
        )

    grad_q, grad_blocks = lax.scan(
        back_step, jnp.zeros(queries.shape, jnp.float32), (key_blocks, seg_blocks, index_blocks)
    )
    return (grad_q, grad_blocks.reshape(keys_all.shape[0], heads_kv, 2 * head_dim))


def shards(
    tokens, segments, gain_one, w_query, w_keyval, w_out, gain_two, w_gateup, w_down, cotangent
):
    num_seqs, tok_count, model_width = tokens.shape
    row_count = num_seqs * tok_count
    head_dim = HD
    heads_kv = w_keyval.shape[1]
    group = w_query.shape[1] // head_dim // heads_kv
    x_float = tokens.reshape(row_count, model_width).astype(jnp.float32)
    inverse_one = lax.rsqrt(jnp.mean(x_float * x_float, -1, keepdims=True) + epsilon)
    normed_one = (x_float * inverse_one * gain_one).astype(jnp.bfloat16)
    queries = jnp.dot(normed_one, w_query, preferred_element_type=jnp.float32).reshape(
        row_count, heads_kv, group, head_dim
    )
    key_value = jnp.einsum("rd,dhe->rhe", normed_one, w_keyval, preferred_element_type=jnp.float32)
    query_index = lax.axis_index("context") * tok_count + jnp.arange(tok_count, dtype=jnp.int32)
    positions = (query_index[None, :] - segments).reshape(row_count)
    cosine, sine = angles(positions, head_dim)
    cos_q = cosine[:, None, None, :]
    sin_q = sine[:, None, None, :]
    cos_k = cosine[:, None, :]
    sin_k = sine[:, None, :]
    rot_q = rotate(queries, cos_q, sin_q).astype(jnp.bfloat16)
    rot_kv = jnp.concatenate(
        [rotate(key_value[..., :head_dim], cos_k, sin_k), key_value[..., head_dim:]], -1
    ).astype(jnp.bfloat16)
    keys_all, seg_all = (
        lax.all_gather(
            rot_kv.reshape(num_seqs, tok_count, heads_kv, 2 * head_dim),
            "context",
            axis=1,
            tiled=True,
        ),
        lax.all_gather(segments, "context", axis=1, tiled=True),
    )
    queries_seq = rot_q.reshape(num_seqs, tok_count, heads_kv, group, head_dim)
    seq_index = 0
    attended_one, total_one = attend(
        queries_seq[seq_index],
        query_index,
        segments[seq_index],
        keys_all[seq_index],
        seg_all[seq_index],
        head_dim,
    )
    attended_list = [attended_one]
    total_list = [total_one]
    attended = jnp.stack(attended_list)
    attended_low = attended.reshape(row_count, heads_kv * group * head_dim).astype(jnp.bfloat16)
    branch = jnp.dot(attended_low, w_out, preferred_element_type=jnp.float32)
    resid = x_float + lax.psum(branch.astype(jnp.bfloat16), "tensor").astype(jnp.float32)
    inverse_two = lax.rsqrt(jnp.mean(resid * resid, -1, keepdims=True) + epsilon)
    normed_two = (resid * inverse_two * gain_two).astype(jnp.bfloat16)
    gate_up = jnp.einsum("rd,dcf->rcf", normed_two, w_gateup, preferred_element_type=jnp.float32)
    gate = gate_up[:, 0]
    up_part = gate_up[:, 1]
    sigmoid_gate = jax.nn.sigmoid(gate)
    activated = gate * sigmoid_gate
    hidden = (activated * up_part).astype(jnp.bfloat16)
    down_part = jnp.dot(hidden, w_down, preferred_element_type=jnp.float32)
    output = resid + lax.psum(down_part.astype(jnp.bfloat16), "tensor").astype(jnp.float32)
    mixed = output.astype(jnp.bfloat16).reshape(num_seqs, tok_count, model_width)
    grad_out = cotangent.reshape(row_count, model_width)
    grad_hidden = jnp.einsum("rd,fd->rf", grad_out, w_down, preferred_element_type=jnp.float32)
    grad_wdown = jnp.einsum("rf,rd->fd", hidden, grad_out, preferred_element_type=jnp.float32)
    grad_gate = grad_hidden * up_part * (sigmoid_gate * (1.0 + gate * (1.0 - sigmoid_gate)))
    grad_up = grad_hidden * activated
    grad_gateup = jnp.stack([grad_gate, grad_up], 1).astype(jnp.bfloat16)
    grad_wgateup = jnp.einsum(
        "rd,rcf->dcf", normed_two, grad_gateup, preferred_element_type=jnp.float32
    )
    grad_normed_two = lax.psum(
        jnp.einsum("rcf,dcf->rd", grad_gateup, w_gateup, preferred_element_type=jnp.float32).astype(
            jnp.bfloat16
        ),
        "tensor",
    ).astype(jnp.float32)
    grad_resid_norm, grad_gain_two = norm_back(resid, inverse_two, gain_two, grad_normed_two)
    grad_resid = grad_out.astype(jnp.float32) + grad_resid_norm
    grad_branch = grad_resid.astype(jnp.bfloat16)
    grad_wout = jnp.einsum(
        "ra,rd->ad", attended_low, grad_branch, preferred_element_type=jnp.float32
    )
    grad_attended = jnp.einsum(
        "rd,ad->ra", grad_branch, w_out, preferred_element_type=jnp.float32
    ).astype(jnp.bfloat16)
    grad_attended = grad_attended.reshape(num_seqs, tok_count, heads_kv, group, head_dim)
    seq_index = 0
    grad_q_one, grad_kv_one = attend_back(
        queries_seq[seq_index],
        query_index,
        segments[seq_index],
        keys_all[seq_index],
        seg_all[seq_index],
        grad_attended[seq_index],
        attended[seq_index],
        total_list[seq_index],
        head_dim,
    )
    query_grads = [grad_q_one]
    keyval_grads = [grad_kv_one]
    grad_kv_local = (
        lax.psum_scatter(
            jnp.stack(keyval_grads).astype(jnp.bfloat16), "context", scatter_dimension=1, tiled=True
        )
        .astype(jnp.float32)
        .reshape(row_count, heads_kv, 2 * head_dim)
    )
    grad_rot_q = jnp.stack(query_grads).reshape(row_count, heads_kv, group, head_dim)
    grad_queries = (
        rotate(grad_rot_q, cos_q, -sin_q)
        .reshape(row_count, heads_kv * group * head_dim)
        .astype(jnp.bfloat16)
    )
    grad_keyval = jnp.concatenate(
        [rotate(grad_kv_local[..., :head_dim], cos_k, -sin_k), grad_kv_local[..., head_dim:]], -1
    ).astype(jnp.bfloat16)
    grad_wquery = jnp.einsum(
        "rd,re->de", normed_one, grad_queries, preferred_element_type=jnp.float32
    )
    grad_wkeyval = jnp.einsum(
        "rd,rhe->dhe", normed_one, grad_keyval, preferred_element_type=jnp.float32
    )
    grad_normed_part = jnp.einsum(
        "re,de->rd", grad_queries, w_query, preferred_element_type=jnp.float32
    ) + jnp.einsum("rhe,dhe->rd", grad_keyval, w_keyval, preferred_element_type=jnp.float32)
    grad_normed_one = lax.psum(grad_normed_part.astype(jnp.bfloat16), "tensor").astype(jnp.float32)
    grad_x_norm, grad_gain_one = norm_back(x_float, inverse_one, gain_one, grad_normed_one)
    grad_tokens = (grad_resid + grad_x_norm).reshape(num_seqs, tok_count, model_width)
    sent_wquery, sent_wkeyval, sent_wout, sent_gain_one, sent_wgateup, sent_wdown, sent_gain_two = (
        lax.psum_scatter(
            grad_wquery.astype(jnp.bfloat16), ("dp", "context"), scatter_dimension=0, tiled=True
        ).astype(jnp.float32),
        lax.psum_scatter(
            grad_wkeyval.astype(jnp.bfloat16), ("dp", "context"), scatter_dimension=0, tiled=True
        ).astype(jnp.float32),
        lax.psum_scatter(
            grad_wout.astype(jnp.bfloat16), ("dp", "context"), scatter_dimension=1, tiled=True
        ).astype(jnp.float32),
        lax.psum_scatter(
            grad_gain_one.astype(jnp.bfloat16), ("dp", "context"), scatter_dimension=0, tiled=True
        ).astype(jnp.float32),
        lax.psum_scatter(
            grad_wgateup.astype(jnp.bfloat16), ("dp", "context"), scatter_dimension=0, tiled=True
        ).astype(jnp.float32),
        lax.psum_scatter(
            grad_wdown.astype(jnp.bfloat16), ("dp", "context"), scatter_dimension=1, tiled=True
        ).astype(jnp.float32),
        lax.psum_scatter(
            grad_gain_two.astype(jnp.bfloat16), ("dp", "context"), scatter_dimension=0, tiled=True
        ).astype(jnp.float32),
    )
    return (
        mixed,
        grad_tokens,
        sent_gain_one,
        sent_wquery,
        sent_wkeyval,
        sent_wout,
        sent_gain_two,
        sent_wgateup,
        sent_wdown,
    )


def solution(mesh):
    return jax.shard_map(
        shards,
        mesh=mesh,
        in_specs=(
            P("dp", "context", None),
            P("dp", "context"),
            P(),
            P(None, "tensor"),
            P(None, "tensor", None),
            P("tensor", None),
            P(),
            P(None, None, "tensor"),
            P("tensor", None),
            P("dp", "context", None),
        ),
        out_specs=(
            P("dp", "context", None),
            P("dp", "context", None),
            P(("dp", "context")),
            P(("dp", "context"), "tensor"),
            P(("dp", "context"), "tensor", None),
            P("tensor", ("dp", "context")),
            P(("dp", "context")),
            P(("dp", "context"), None, "tensor"),
            P("tensor", ("dp", "context")),
        ),
        check_vma=False,
    )
```

profile of v0, /device:TPU:24, one launch (start us, length us, event | category | flops | bytes accessed | tf_op | source)
XLA Modules:
  0.0 1001.4 jit_solution(10006894032385933112)
XLA Ops:
  8.6 10.7 %all_gather.6 = s32[1,2048]{1,0:T(1,128)S(1)} all-gather(s32[1,512]{1,0:T(1,128)} %param.23), channel_id=1, replica_groups=mesh['tensor'=4,'dp'=2,'context'=4] {'context'}, dimensions={1}, use_global_device_ids=true | all-gather | bytes 10240 | tf_op jit(solution)/shard_map/all_gather | solution.py:207
  27.1 15.2 %all_gather.7 = bf16[1,2048,1,128]{1,3,2,0:T(8,128)(2,1)S(1)} all-gather(bf16[1,512,1,128]{1,3,2,0:T(8,128)(2,1)S(1)} %pad_maximum_fusion.4), channel_id=1, replica_groups=mesh['tensor'=4,'dp'=2,'context'=4] {'context'}, dimensions={1}, use_global_device_ids=true | all-gather | bytes 655360 | tf_op jit(solution)/shard_map/all_gather | solution.py:201
  52.4 40.2 %while.40 = (s32[]{:T(128)}, f32[1,8,512]{2,1,0:T(8,128)S(1)}, f32[1,8,512]{2,1,0:T(8,128)S(1)}, s32[4,512]{1,0:T(4,128)}, s32[512]{0:T(512)S(1)}, /*index=5*/s3...) while((s32[]{:T(128)}, f32[1,8,512]{2,1,0:T(8,128)S(1)}, ...), condition=%wide.region_6.7_spmd, body=%wide.region_1.6_spmd.sunk | while | flops 286007296 | bytes 18645324 | solution.py:87
  94.3 50.2 %while.41 = (s32[]{:T(128)}, f32[512,1,8,64]{0,3,2,1:T(8,128)}, s32[4,512]{1,0:T(4,128)}, s32[512]{0:T(512)S(1)}, s32[4,512]{1,0:T(4,128)S(1)}, /*index=5*/s32[5...) while((s32[]{:T(128)}, f32[512,1,8,64]{0,3,2,1:T(8,128)}, ...), condition=%wide.region_10.11_spmd, body=%wide.region_7.10_spmd.sunk | while | flops 546308096 | bytes 3588451 | solution.py:109
  100.5 6.4 conditional.7
  102.0 4.8 fusion.15
  113.0 6.4 conditional.7
  125.6 6.4 conditional.7
  127.2 4.8 fusion.15
  138.1 6.4 conditional.7
  149.7 52.0 %all-reduce.8.cloned.1.call-done = bf16[512,2048]{1,0:T(8,128)(2,1)} async-done(((bf16[512,2048]{1,0:T(8,128)(2,1)}), bf16[512,2048]{1,0:T(8,128)(2,1)}) %all-reduce.8.cloned.1.call-update) | async-done | bytes 2097168 | tf_op jit(solution)/shard_map/psum | solution.py:224
  205.2 12.9 %fusion.48 = f32[512,2,1408]{2,0,1:T(8,128)} fusion(bf16[2048,2,1408]{2,1,0:T(2,128)(2,1)} %param.29, bf16[512,2048]{1,0:T(8,128)(2,1)S(1)} %copy-done.6, bf16[1,512,2048]{2,1,0:T(8,128)(2,1)S(1)} %copy-done.2, f32[2048]{0:T(1024)S(1)} %copy-done.26, f32[512]{0:T(512)S(1)} %get-tuple-element.587), kind=kOutput, calls=%fused_computation.70 | convolution fusion | flops 5911871488 | bytes 21506048 | tf_op jit(solution)/shard_map/rd,dcf->rcf/dot_general | solution.py:227
  218.1 7.9 fusion.103
  227.7 7.6 bitcast_convert_fusion
  235.5 51.4 %all-reduce.10.cloned.1.call-done = bf16[512,2048]{1,0:T(8,128)(2,1)} async-done(((bf16[512,2048]{1,0:T(8,128)(2,1)}), bf16[512,2048]{1,0:T(8,128)(2,1)}) %all-reduce.10.cloned.1.call-update) | async-done | bytes 2097168 | tf_op jit(solution)/shard_map/psum | solution.py:245
  297.0 66.7 %while.42 = (s32[]{:T(128)}, f32[512,1,8,64]{0,3,2,1:T(8,128)S(1)}, bf16[4,512,1,128]{1,3,2,0:T(8,128)(2,1)}, s32[4,512]{1,0:T(4,128)}, s32[512]{0:T(512)S(1)}, ...) while((s32[]{:T(128)}, f32[512,1,8,64]{0,3,2,1:T(8,128)S(1)}, ...), condition=%wide.region_20.21_spmd, body=%wide.region_17.20_spmd.sunk | while | flops 1364787200 | bytes 46007160 | solution.py:168
  303.2 9.8 conditional.8
  319.9 9.8 conditional.8
  336.6 9.8 conditional.8
  353.2 9.8 conditional.8
  367.0 9.3 convolution_convert_fusion.5
  376.3 9.3 reduce-scatter.7.cloned.1.call-done
  404.0 9.1 convolution_convert_fusion.1
  413.4 11.5 %convolution_convert_fusion = bf16[2048,2,1408]{2,0,1:T(8,128)(2,1)} fusion(bf16[512,1,1408]{2,0,1:T(8,128)(2,1)} %copy-done.35, bf16[512,1,1408]{2,0,1:T(8,128)(2,1)} %copy-done.34, bf16[512,2048]{1,0:T(8,128)(2,1)} %all-reduce.8.cloned.1.call-done, bf16[1,512,2048]{2,1,0:T(8,128)(2,1)S(1)} %copy-done.4, f32[2048]{0:T(1024)S(1)} %copy-done.26, ...), kind=kOutput, calls=%fused_computation.67 | convolution fusion | flops 5923405824 | bytes 18622464 | tf_op jit(solution)/shard_map/rd,rcf->dcf/dot_general | solution.py:242
  426.8 25.2 %reduce-scatter.11.cloned.1.call-done = bf16[256,1,128]{2,0,1:T(8,128)(2,1)} async-done(((bf16[2048,1,128]{2,0,1:T(8,128)(2,1)}), bf16[256,1,128]{2,0,1:T(8,128)(2,1)}) %reduce-scatter.11.cloned.1.call-update) | async-done | bytes 65552 | tf_op jit(solution)/shard_map/reduce_scatter | solution.py:307
  453.4 87.3 %all-reduce.12.cloned.1.call-done = (bf16[512,2048]{1,0:T(8,128)(2,1)}, bf16[512,2048]{1,0:T(8,128)(2,1)}) async-done(((bf16[512,2048]{1,0:T(8,128)(2,1)}, bf16[512,2048]{1,0:T(8,128)(2,1)}), (bf16[512,2048]{1,0:T(8,128)(2,1)}, bf16[512,2048]{1,0:T(8,128)(2,1)})) %all-reduce.12.cloned.1.call-update) | async-done | bytes 4194320 | tf_op jit(solution)/shard_map/psum | solution.py:234
  543.9 17.8 %all-reduce.2 = (bf16[2048]{0:T(1024)(128)(2,1)S(1)}, bf16[2048]{0:T(1024)(128)(2,1)S(1)}) all-reduce(bf16[2048]{0:T(1024)(128)(2,1)S(1)} %get-tuple-element.489, bf16[2048]{0:T(1024)(128)(2,1)S(1)} %get-tuple-element.487), channel_id=3, replica_groups=mesh['tensor'=4,'dp'=2,'context'=4] {'dp','context'}, use_global_device_ids=true, to_apply=%region_25.26.clone | all-reduce | flops 4096 | bytes 16384
  562.3 7.6 fusion.61
  569.9 41.3 %reduce-scatter.13.cloned.1.call-done = bf16[512,256]{1,0:T(8,128)(2,1)} async-done(((bf16[512,2048]{1,0:T(8,128)(2,1)}), bf16[512,256]{1,0:T(8,128)(2,1)}) %reduce-scatter.13.cloned.1.call-update) | async-done | bytes 262160 | tf_op jit(solution)/shard_map/reduce_scatter | solution.py:310
  613.0 68.7 %reduce-scatter.9.cloned.1.call-done = bf16[256,512]{1,0:T(8,128)(2,1)} async-done(((bf16[2048,512]{1,0:T(8,128)(2,1)}), bf16[256,512]{1,0:T(8,128)(2,1)}) %reduce-scatter.9.cloned.1.call-update) | async-done | bytes 262160 | tf_op jit(solution)/shard_map/reduce_scatter | solution.py:304
  683.5 111.5 %reduce-scatter.17.cloned.1.call-done = bf16[1408,256]{1,0:T(8,128)(2,1)} async-done(((bf16[1408,2048]{1,0:T(8,128)(2,1)}), bf16[1408,256]{1,0:T(8,128)(2,1)}) %reduce-scatter.17.cloned.1.call-update) | async-done | bytes 720912 | tf_op jit(solution)/shard_map/reduce_scatter | solution.py:319
  797.3 192.7 %reduce-scatter.15.cloned.1.call-done = bf16[256,2,1408]{2,0,1:T(8,128)(2,1)} async-done(((bf16[2048,2,1408]{2,0,1:T(8,128)(2,1)}), bf16[256,2,1408]{2,0,1:T(8,128)(2,1)}) %reduce-scatter.15.cloned.1.call-update) | async-done | bytes 1441808 | tf_op jit(solution)/shard_map/reduce_scatter | solution.py:316
  (309 shorter events, 210.9 us)
Async XLA Ops:
  7.2 139.4 %copy-start = (bf16[512,2048]{1,0:T(8,128)(2,1)S(1)}, bf16[512,2048]{1,0:T(8,128)(2,1)}, u32[]{:S(2)}) copy-start(bf16[512,2048]{1,0:T(8,128)(2,1)} %param.27) | copy-start | bytes 6291460
  7.2 194.5 %all-reduce.8.cloned.1.call-start = ((), (), s32[]{:S(2)}) async-start(), calls=%async_computation.6 | async-start | bytes 4194304 | tf_op jit(solution)/shard_map/psum | solution.py:224
  7.3 18.6 %copy-start.31 = (f32[32]{0:T(128)}, f32[32]{0:T(128)S(1)}, u32[]{:S(2)}) copy-start(f32[32]{0:T(128)S(1)} %multiply_power_fusion) | copy-start | bytes 388
  8.6 34.9 %copy-start.24 = (f32[1,512]{1,0:T(1,128)}, f32[1,512]{1,0:T(1,128)S(1)}, u32[]{:S(2)}) copy-start(f32[1,512]{1,0:T(1,128)S(1)} %subtract_convert_fusion.1) | copy-start | bytes 6148
  21.9 5.1 copy-start.27
  25.5 26.6 %copy-start.13 = (f32[512,32]{0,1:T(8,128)}, f32[512,32]{0,1:T(8,128)S(1)}, u32[]{:S(2)}) copy-start(f32[512,32]{0,1:T(8,128)S(1)} %get-tuple-element.583) | copy-start | bytes 196612
  27.0 21.4 %copy-start.28 = (f32[512]{0:T(512)S(1)}, f32[512]{0:T(512)}, u32[]{:S(2)}) copy-start(f32[512]{0:T(512)} %copy-done.27) | copy-start | bytes 6148
  149.2 55.7 %copy-start.26 = (f32[2048]{0:T(1024)S(1)}, f32[2048]{0:T(1024)}, u32[]{:S(2)}) copy-start(f32[2048]{0:T(1024)} %param.28) | copy-start | bytes 24580
  149.2 137.7 %all-reduce.10.cloned.1.call-start = ((), (), s32[]{:S(2)}) async-start(), calls=%async_computation.7 | async-start | bytes 4194304 | tf_op jit(solution)/shard_map/psum | solution.py:245
  205.2 12.9 %copy-start.11 = (bf16[1,512,2048]{2,1,0:T(8,128)(2,1)S(1)}, bf16[1,512,2048]{2,1,0:T(8,128)(2,1)}, u32[]{:S(2)}) copy-start(bf16[1,512,2048]{2,1,0:T(8,128)(2,1)} %param.31) | copy-start | bytes 6291460
  205.2 22.5 %slice-start = ((s8[11534336]{0:T(1024)(128)(4,1)}), s8[4194304]{0:T(1024)(128)(4,1)S(1)}, s32[]{:S(2)}) async-start(s8[11534336]{0:T(1024)(128)(4,1)} %bitcast.419), calls=%async_computation.15 | async-start | bytes 8388608
  205.2 22.5 %slice-start.1 = ((s8[11534336]{0:T(1024)(128)(4,1)}), s8[4194304]{0:T(1024)(128)(4,1)S(1)}, s32[]{:S(2)}) async-start(s8[11534336]{0:T(1024)(128)(4,1)} %bitcast.419), calls=%async_computation.16 | async-start | bytes 8388608
  218.1 9.5 slice-start.2
  235.3 150.3 %reduce-scatter.7.cloned.1.call-start = ((), (), s32[]{:S(2)}) async-start(), calls=%async_computation.8 | async-start | bytes 655360 | tf_op jit(solution)/shard_map/reduce_scatter | solution.py:276
  286.9 4.6 copy-start.3
  286.9 4.6 copy-start.7
  286.9 4.7 copy-start.10
  366.7 20.7 %copy-start.25 = (f32[1,512]{1,0:T(1,128)S(1)}, f32[1,512]{1,0:T(1,128)}, u32[]{:S(2)}) copy-start(f32[1,512]{1,0:T(1,128)} %copy-done.24) | copy-start | bytes 6148
  366.7 20.7 %copy-start.32 = (f32[32]{0:T(128)S(1)}, f32[32]{0:T(128)}, u32[]{:S(2)}) copy-start(f32[32]{0:T(128)} %copy-done.31) | copy-start | bytes 388
  366.7 21.0 %copy-start.4 = (bf16[1,512,2048]{2,1,0:T(8,128)(2,1)S(1)}, bf16[1,512,2048]{2,1,0:T(8,128)(2,1)}, u32[]{:S(2)}) copy-start(bf16[1,512,2048]{2,1,0:T(8,128)(2,1)} %param.22) | copy-start | bytes 6291460
  366.8 21.0 %copy-start.23 = (f32[2048]{0:T(1024)S(1)}, f32[2048]{0:T(1024)}, u32[]{:S(2)}) copy-start(f32[2048]{0:T(1024)} %param.24) | copy-start | bytes 24580
  366.8 21.0 %copy-start.29 = (f32[512]{0:T(512)S(1)}, f32[512]{0:T(512)}, u32[]{:S(2)}) copy-start(f32[512]{0:T(512)} %copy-done.27) | copy-start | bytes 6148
  366.8 85.2 %reduce-scatter.11.cloned.1.call-start = ((), (), s32[]{:S(2)}) async-start(), calls=%async_computation.10 | async-start | bytes 589824 | tf_op jit(solution)/shard_map/reduce_scatter | solution.py:307
  376.3 13.4 %copy-start.14 = (f32[512,32]{0,1:T(8,128)S(1)}, f32[512,32]{0,1:T(8,128)}, u32[]{:S(2)}) copy-start(f32[512,32]{0,1:T(8,128)} %copy-done.13) | copy-start | bytes 196612
  376.3 13.4 %copy-start.20 = (f32[512,32]{0,1:T(8,128)S(1)}, f32[512,32]{0,1:T(8,128)}, u32[]{:S(2)}) copy-start(f32[512,32]{0,1:T(8,128)} %get-tuple-element.581) | copy-start | bytes 196612
  389.6 151.1 %all-reduce.12.cloned.1.call-start = ((), (), s32[]{:S(2)}) async-start(), calls=%async_computation.14 | async-start | bytes 8388608 | tf_op jit(solution)/shard_map/psum | solution.py:234
  396.2 215.0 %reduce-scatter.13.cloned.1.call-start = ((), (), s32[]{:S(2)}) async-start(), calls=%async_computation.11 | async-start | bytes 2359296 | tf_op jit(solution)/shard_map/reduce_scatter | solution.py:310
  401.0 280.7 %reduce-scatter.9.cloned.1.call-start = ((), (), s32[]{:S(2)}) async-start(), calls=%async_computation.9 | async-start | bytes 2359296 | tf_op jit(solution)/shard_map/reduce_scatter | solution.py:304
  404.0 391.0 %reduce-scatter.17.cloned.1.call-start = ((), (), s32[]{:S(2)}) async-start(), calls=%async_computation.13 | async-start | bytes 6488064 | tf_op jit(solution)/shard_map/reduce_scatter | solution.py:319
  413.1 576.9 %reduce-scatter.15.cloned.1.call-start = ((), (), s32[]{:S(2)}) async-start(), calls=%async_computation.12 | async-start | bytes 12976128 | tf_op jit(solution)/shard_map/reduce_scatter | solution.py:316
  424.9 137.4 %copy-start.30 = (f32[512]{0:T(512)S(1)}, f32[512]{0:T(512)}, u32[]{:S(2)}) copy-start(f32[512]{0:T(512)} %get-tuple-element.584) | copy-start | bytes 6148
  562.3 432.2 %copy-start.1 = (bf16[512,2048]{1,0:T(8,128)(2,1)S(1)}, bf16[512,2048]{1,0:T(8,128)(2,1)}, u32[]{:S(2)}) copy-start(bf16[512,2048]{1,0:T(8,128)(2,1)} %param.27) | copy-start | bytes 6291460
  (25 other events, 37.7 us)
Sparse Core Ops, SparseCore 0:
  149.3 52.3 all-reduce.7
  235.4 51.4 all-reduce.9
  366.8 18.7 reduce-scatter.6
  389.7 62.1 reduce-scatter.10
  454.9 85.7 all-reduce.11
  544.1 67.0 reduce-scatter.12
  614.7 66.9 reduce-scatter.8
  685.3 109.5 reduce-scatter.16
  798.5 191.4 reduce-scatter.14
where the time goes:
time: 1020 us; the launch traced here: 1000 us
  waiting for transfers between devices  639 us (63%)
  matrix products  146 us (14%)
  local copies, waits for them, and re-layouts  69 us (7%)
  other arithmetic  54.8 us (5%)
  blocking collectives  43.7 us (4%)
  loops' own time  31.9 us (3%)
  between operations  15.5 us (2%)
    reduce_scatter x1, waiting for transfers between devices, shards(): lax.psum_scatter(grad_wgateup.astype(jnp.bfloat16), ('dp', 'context'), sc...  193 us
    reduce_scatter x1, waiting for transfers between devices, shards(): lax.psum_scatter(grad_wdown.astype(jnp.bfloat16), ('dp', 'context'), scat...  111 us
    psum x1, waiting for transfers between devices, shards(): lax.psum(down_part.astype(jnp.bfloat16), 'tensor').astype(jnp.float32)  87.3 us
    reduce_scatter x1, waiting for transfers between devices, shards(): lax.psum_scatter(grad_wquery.astype(jnp.bfloat16), ('dp', 'context'), sca...  68.7 us
    psum x1, waiting for transfers between devices, shards(): lax.psum(branch.astype(jnp.bfloat16), 'tensor').astype(jnp.float32)  52 us
    psum x1, waiting for transfers between devices, shards(): lax.psum(jnp.einsum('rcf,dcf->rd', grad_gateup, w_gateup, preferred_eleme...  51.4 us
    reduce_scatter x1, waiting for transfers between devices, shards(): lax.psum_scatter(grad_wout.astype(jnp.bfloat16), ('dp', 'context'), scatt...  41.3 us
    reduce_scatter x1, waiting for transfers between devices, shards(): lax.psum_scatter(grad_wkeyval.astype(jnp.bfloat16), ('dp', 'context'), sc...  25.2 us
  transfers between devices with their start and end apart: 9, of which 9 were waited for; matrix products, arithmetic and copies ran while one was open for 6% of the time, Pallas kernels for 0%

commit v1 on v0

v1 whole, which is shorter than its diff:
```python
import math

import jax
import jax.numpy as jnp
from jax import lax
from jax.experimental import pallas as pl
from jax.experimental.pallas import tpu as pltpu
from jax.sharding import PartitionSpec as P

HD = 64


epsilon = 1e-05
neg_large = -1e30


def rotate(values, cosine, sine):
    half_width = values.shape[-1] // 2
    first_half = values[..., :half_width]
    second_half = values[..., half_width:]
    return jnp.concatenate(
        [first_half * cosine - second_half * sine, second_half * cosine + first_half * sine], -1
    )


def angles(positions, head_dim):
    freqs = 10000.0 ** (-(jnp.arange(head_dim // 2, dtype=jnp.float32) * 2.0) / head_dim)
    phase = positions.astype(jnp.float32)[:, None] * freqs[None, :]
    return (jnp.cos(phase), jnp.sin(phase))


def norm_back(inputs, inverse, gain, grad_normed):
    grad_gain = jnp.sum(grad_normed * inputs * inverse, 0)
    scaled = grad_normed * gain
    grad_inputs = inverse * scaled - inputs * (inverse * inverse * inverse) * jnp.mean(
        scaled * inputs, -1, keepdims=True
    )
    return (grad_inputs, grad_gain)


MESH = pl.DeviceIdType.MESH
MIB = 1 << 20


def dot(left, right):
    return jnp.dot(left, right, preferred_element_type=jnp.float32)


def dot_t(left, right):
    return lax.dot_general(left, right, (((1,), (1,)), ((), ())), preferred_element_type=jnp.float32)


def lanes(shape):
    return lax.broadcasted_iota(jnp.int32, shape, len(shape) - 1)


def turn(values, cosine, sine):
    low_half = lax.rem(lanes(values.shape), 64) < 32
    swapped = jnp.where(low_half, pltpu.roll(values, 96, 1), pltpu.roll(values, 32, 1))
    return values * cosine + swapped * sine


def aligned(index, size):
    return pl.ds(pl.multiple_of(index * size, size), size)


def forward_kernel(
    x_hbm, seg_ref, cos_ref, sin_ref, gain_one_ref, gain_two_ref, wq_hbm, wkv_hbm, wout_hbm, raw_hbm,
    wdown_hbm, g_hbm,
    q_out, kv_out, att_out, lse_out, n1_out, n2_out, resid_out, hid_out, gg_out, wgu_out,
    x, n1, wq, wkv, wout, raw, wdown, g, wgu, q, kv, keys, vals_t, run_max, run_sum, acc, att_low,
    own, stage_core, got_core, stage_x, got_x, resid, n2, gh, hid, gg,
    load_sem, store_sem, kv_send, kv_recv, core_send, core_recv, x_send, x_recv, ag_send, ag_recv,
):
    rows, width = x.shape
    quarter = rows // 4
    units = gh.shape[1]
    tensor = lax.axis_index("tensor")
    place = lax.axis_index("context")
    core, chip = lax.rem(tensor, 2), lax.div(tensor, 2)
    core_mate = {"tensor": chip * 2 + 1 - core}
    chip_mate = {"tensor": (1 - chip) * 2 + core}

    barrier = pltpu.get_barrier_semaphore()
    for mate in (core_mate, chip_mate, *({"context": lax.rem(place + k, 4)} for k in (1, 2, 3))):
        pl.semaphore_signal(barrier, inc=1, device_id=mate, device_id_type=MESH)

    loads = [
        pltpu.make_async_copy(src, dst, load_sem.at[i])
        for i, (src, dst) in enumerate(
            [(x_hbm, x), (wkv_hbm, wkv), (wq_hbm, wq), (raw_hbm, raw), (wout_hbm, wout), (g_hbm, g),
             (wdown_hbm, wdown)]
        )
    ]
    for load in loads:
        load.start()
    load_x, load_wkv, load_wq, load_raw, load_wout, load_g, load_wdown = loads
    stores = []

    def store(src, dst):
        copy = pltpu.make_async_copy(src, dst, store_sem.at[len(stores)])
        copy.start()
        stores.append(copy)

    load_x.wait()

    @pl.loop(0, rows // 64)
    def _(i):
        at = aligned(i, 64)
        values = x[at, :].astype(jnp.float32)
        inverse = lax.rsqrt(jnp.mean(values * values, -1, keepdims=True) + epsilon)
        n1[at, :] = (values * inverse * gain_one_ref[...]).astype(jnp.bfloat16)

    store(n1, n1_out)

    load_wkv.wait()
    key_lane = lanes((rows, 128)) < 64
    kv[0] = turn(
        dot(n1[...], wkv[...]),
        jnp.where(key_lane, cos_ref[...], 1.0),
        jnp.where(key_lane, sin_ref[...], 0.0),
    ).astype(jnp.bfloat16)
    pl.semaphore_wait(barrier, 5)

    def kv_copy(k):
        return pltpu.make_async_remote_copy(
            src_ref=kv.at[0], dst_ref=kv.at[k], send_sem=kv_send.at[k], recv_sem=kv_recv.at[k],
            device_id={"context": lax.rem(place + k, 4)}, device_id_type=MESH,
        )

    for k in (1, 2, 3):
        pl.when(place + k < 4)(kv_copy(k).start)

    load_wq.wait()

    @pl.loop(0, q.shape[1] // 256)
    def _(i):
        wide = dot(n1[...], wq[:, aligned(i, 256)])
        for half in range(2):
            turned = turn(wide[:, 128 * half : 128 * half + 128], cos_ref[...], sin_ref[...])
            at = pl.ds(pl.multiple_of(i * 256 + 128 * half, 128), 128)
            q[:, at] = (turned * 0.125).astype(jnp.bfloat16)

    store(q, q_out)

    def attend_block(k, first):
        block = kv[k].astype(jnp.float32)
        keys[0] = jnp.where(key_lane, block, 0.0).astype(jnp.bfloat16)
        keys[1] = jnp.where(key_lane, 0.0, pltpu.roll(block, 64, 1)).astype(jnp.bfloat16)
        vals_t[...] = block.T[64:].astype(jnp.bfloat16)

        @pl.loop(0, q.shape[1] // 128)
        def _(pair):
            pair_q = q[:, aligned(pair, 128)]
            for e in range(2):
                head = pair * 2 + e
                scores = dot_t(keys[e], pair_q)
                key_index = (place - k) * rows + lax.broadcasted_iota(jnp.int32, (rows, rows), 0)
                allowed = key_index >= seg_ref[...]
                if first:
                    query_index = place * rows + lax.broadcasted_iota(jnp.int32, (rows, rows), 1)
                    allowed = allowed & (key_index <= query_index)
                scores = jnp.where(allowed, scores, neg_large)
                top = jnp.max(scores, 0, keepdims=True)
                at = aligned(head, 64)
                if first:
                    weights = jnp.exp(scores - top)
                    run_sum[head] = jnp.sum(weights, 0, keepdims=True)
                    acc[at, :] = dot(vals_t[...], weights.astype(jnp.bfloat16))
                else:
                    old = run_max[head]
                    top = jnp.maximum(top, old)
                    fade = jnp.exp(old - top)
                    weights = jnp.exp(scores - top)
                    run_sum[head] = run_sum[head] * fade + jnp.sum(weights, 0, keepdims=True)
                    acc[at, :] = acc[at, :] * fade + dot(
                        vals_t[...], weights.astype(jnp.bfloat16)
                    )
                run_max[head] = top

    attend_block(0, True)

    load_raw.wait()
    row = lax.broadcasted_iota(jnp.int32, (256, 256), 0)
    column = lax.broadcasted_iota(jnp.int32, (256, 256), 1)
    source = jnp.where(row < 128, 2 * row, 2 * row - 255)
    order = (column == source).astype(jnp.bfloat16)

    @pl.loop(0, width // 128)
    def _(i):
        at = aligned(i, 128)
        split = dot(order, raw[at].reshape(256, units)).astype(jnp.bfloat16)
        for b in range(units // 128):
            wgu[at, 256 * b : 256 * b + 128] = split[:128, 128 * b : 128 * b + 128]
            wgu[at, 256 * b + 128 : 256 * b + 256] = split[128:, 128 * b : 128 * b + 128]

    store(wgu, wgu_out)

    @pl.loop(1, place + 1)
    def _(k):
        kv_copy(k).wait_recv()
        attend_block(k, False)

    for k in (1, 2, 3):
        pl.when(place + k < 4)(kv_copy(k).wait_send)
    store(kv, kv_out)

    @pl.loop(0, q.shape[1] // 128)
    def _(pair):
        for e in range(2):
            head = pair * 2 + e
            at = aligned(head, 64)
            acc[at, :] = acc[at, :] * (1.0 / run_sum[head])
            run_max[head] = run_max[head] + jnp.log(run_sum[head])
        at = aligned(pair, 128)
        att_low[:, at] = acc[at, :].T.astype(jnp.bfloat16)

    store(acc, att_out)
    store(run_max, lse_out)

    load_wout.wait()
    chunks = own.shape[1]
    span = own.shape[3]

    def core_copy(i, c):
        return pltpu.make_async_remote_copy(
            src_ref=stage_core.at[i, c], dst_ref=got_core.at[i, c], send_sem=core_send.at[i, c],
            recv_sem=core_recv.at[i, c], device_id=core_mate, device_id_type=MESH,
        )

    def x_copy(c):
        return pltpu.make_async_remote_copy(
            src_ref=stage_x.at[c], dst_ref=got_x.at[c], send_sem=x_send.at[c],
            recv_sem=x_recv.at[c], device_id=chip_mate, device_id_type=MESH,
        )

    for i in range(2):
        half = 1 - chip if i == 0 else chip
        theirs = aligned(half * 2 + 1 - core, quarter)
        mine = aligned(half * 2 + core, quarter)
        for c in range(chunks):

            @pl.loop(0, span // 256)
            def _(tile):
                left = jnp.concatenate([att_low[theirs, :], att_low[mine, :]], 0)
                at = aligned(tile, 256)
                out_at = pl.ds(pl.multiple_of(c * span + tile * 256, 256), 256)
                both = dot(left, wout[:, out_at])
                stage_core[i, c, :, at] = both[:quarter].astype(jnp.bfloat16)
                own[i, c, :, at] = both[quarter:]

            core_copy(i, c).start()
        if i == 0:
            for c in range(chunks):
                core_copy(0, c).wait_recv()
                stage_x[c] = (own[0, c] + got_core[0, c].astype(jnp.float32)).astype(jnp.bfloat16)
                x_copy(c).start()

    load_g.wait()
    load_wdown.wait()

    @pl.loop(0, units // 128)
    def _(b):
        at = aligned(b, 128)
        gh[:, at] = dot_t(g[...], wdown[at, :])

    mine = aligned(tensor, quarter)
    square = jnp.zeros((quarter, 1), jnp.float32)
    for c in range(chunks):
        core_copy(1, c).wait_recv()
        x_copy(c).wait_recv()
        at = slice(c * span, (c + 1) * span)
        part = own[1, c] + got_core[1, c].astype(jnp.float32) + got_x[c].astype(jnp.float32)
        part = part + x[mine, at].astype(jnp.float32)
        resid[:, at] = part
        square = square + jnp.sum(part * part, -1, keepdims=True)
    inverse = lax.rsqrt(square / width + epsilon)
    n2[mine, :] = (resid[...] * inverse * gain_two_ref[...]).astype(jnp.bfloat16)
    store(resid, resid_out)

    def ag_copy(slot, owner, mate):
        at = aligned(owner, quarter)
        return pltpu.make_async_remote_copy(
            src_ref=n2.at[at, :], dst_ref=n2.at[at, :], send_sem=ag_send.at[slot],
            recv_sem=ag_recv.at[slot], device_id=mate, device_id_type=MESH,
        )

    to_chip = ag_copy(0, tensor, chip_mate)
    to_core = ag_copy(1, tensor, core_mate)
    onward = ag_copy(2, chip_mate["tensor"], core_mate)
    to_chip.start()
    to_core.start()

    def feed_forward(half):
        at = aligned(half, 2 * quarter)

        @pl.loop(0, units // 128)
        def _(b):
            wide = dot(n2[at, :], wgu[:, aligned(b, 256)])
            gate, up = wide[:, :128], wide[:, 128:]
            grad = gh[at, aligned(b, 128)]
            sigmoid = 1.0 / (1.0 + jnp.exp(-gate))
            active = gate * sigmoid
            hid[at, aligned(b, 128)] = (active * up).astype(jnp.bfloat16)
            grad_gate = grad * up * (sigmoid * (1.0 + gate * (1.0 - sigmoid)))
            both = jnp.concatenate([grad_gate, grad * active], 1).astype(jnp.bfloat16)
            gg[at, aligned(b, 256)] = both

    to_core.wait_recv()
    feed_forward(chip)
    to_chip.wait_recv()
    onward.start()
    onward.wait_recv()
    feed_forward(1 - chip)
    store(n2, n2_out)
    store(hid, hid_out)
    store(gg, gg_out)
    for copy in (to_chip, to_core, onward):
        copy.wait_send()
    for c in range(chunks):
        x_copy(c).wait_send()
        for i in range(2):
            core_copy(i, c).wait_send()
    for copy in stores:
        copy.wait()


def forward(x, segments, cosine, sine, gain_one, gain_two, w_query, w_keyval, w_out, w_gateup, w_down, g):
    rows, width = x.shape
    units = w_down.shape[0]
    heads = w_query.shape[1] // HD
    quarter = rows // 4
    chunks = 2
    bf16, f32 = jnp.bfloat16, jnp.float32
    anywhere = pl.BlockSpec(memory_space=pl.ANY)
    inside = pl.BlockSpec(memory_space=pltpu.VMEM)
    outs = [
        ((rows, heads * HD), bf16),
        ((4, rows, 2 * HD), bf16),
        ((heads * HD, rows), f32),
        ((heads, 1, rows), f32),
        ((rows, width), bf16),
        ((rows, width), bf16),
        ((quarter, width), f32),
        ((rows, units), bf16),
        ((rows, 2 * units), bf16),
        ((width, 2 * units), bf16),
    ]
    dma = pltpu.SemaphoreType.DMA
    return pl.pallas_call(
        forward_kernel,
        out_shape=[jax.ShapeDtypeStruct(*out) for out in outs],
        in_specs=[anywhere] + [inside] * 5 + [anywhere] * 6,
        out_specs=[anywhere] * len(outs),
        scratch_shapes=[
            pltpu.VMEM((rows, width), bf16),
            pltpu.VMEM((rows, width), bf16),
            pltpu.VMEM(w_query.shape, bf16),
            pltpu.VMEM(w_keyval.shape, bf16),
            pltpu.VMEM(w_out.shape, bf16),
            pltpu.VMEM(w_gateup.shape, bf16),
            pltpu.VMEM(w_down.shape, bf16),
            pltpu.VMEM((rows, width), bf16),
            pltpu.VMEM((width, 2 * units), bf16),
            pltpu.VMEM((rows, heads * HD), bf16),
            pltpu.VMEM((4, rows, 2 * HD), bf16),
            pltpu.VMEM((2, rows, 2 * HD), bf16),
            pltpu.VMEM((HD, rows), bf16),
            pltpu.VMEM((heads, 1, rows), f32),
            pltpu.VMEM((heads, 1, rows), f32),
            pltpu.VMEM((heads * HD, rows), f32),
            pltpu.VMEM((rows, heads * HD), bf16),
            pltpu.VMEM((2, chunks, quarter, width // chunks), f32),
            pltpu.VMEM((2, chunks, quarter, width // chunks), bf16),
            pltpu.VMEM((2, chunks, quarter, width // chunks), bf16),
            pltpu.VMEM((chunks, quarter, width // chunks), bf16),
            pltpu.VMEM((chunks, quarter, width // chunks), bf16),
            pltpu.VMEM((quarter, width), f32),
            pltpu.VMEM((rows, width), bf16),
            pltpu.VMEM((rows, units), f32),
            pltpu.VMEM((rows, units), bf16),
            pltpu.VMEM((rows, 2 * units), bf16),
            dma((7,)),
            dma((len(outs),)),
            dma((4,)),
            dma((4,)),
            dma((2, chunks)),
            dma((2, chunks)),
            dma((chunks,)),
            dma((chunks,)),
            dma((3,)),
            dma((3,)),
        ],
        compiler_params=pltpu.CompilerParams(
            collective_id=0, has_side_effects=True, vmem_limit_bytes=60 * MIB
        ),
        name="forward",
    )(x, segments, cosine, sine, gain_one, gain_two, w_query, w_keyval, w_out, w_gateup, w_down, g)


def core_swap(array):
    return lax.ppermute(array, "tensor", [(0, 1), (1, 0), (2, 3), (3, 2)])


def chip_swap(array):
    return lax.ppermute(array, "tensor", [(0, 2), (2, 0), (1, 3), (3, 1)])


def pick(array, index, axis):
    return lax.dynamic_index_in_dim(array, index, axis, keepdims=False)


def sum_scatter(part):
    core, chip = lax.axis_index("tensor") % 2, lax.axis_index("tensor") // 2
    rows, width = part.shape
    quarters = part.reshape(2, 2, rows // 4, width)
    got = core_swap(pick(quarters, 1 - core, 1).astype(jnp.bfloat16))
    pair = pick(quarters, core, 1) + got.astype(jnp.float32)
    got = chip_swap(pick(pair, 1 - chip, 0).astype(jnp.bfloat16))
    return pick(pair, chip, 0) + got.astype(jnp.float32)


def gather_rows(quarter):
    core, chip = lax.axis_index("tensor") % 2, lax.axis_index("tensor") // 2
    rows, width = quarter.shape
    other = chip_swap(quarter)
    pair = jnp.where(chip == 0, jnp.stack([quarter, other]), jnp.stack([other, quarter]))
    other = core_swap(pair)
    whole = jnp.where(core == 0, jnp.stack([pair, other], 1), jnp.stack([other, pair], 1))
    return whole.reshape(4 * rows, width)


def line_sum(part):
    place = lax.axis_index("context")
    order = jnp.array([[3, 2, 1, 0], [3, 2, 0, 1], [0, 1, 3, 2], [0, 1, 2, 3]], jnp.int32)[place]
    first, second, third, own = (part(order[i]) for i in range(4))

    def inward(array):
        return lax.ppermute(array.astype(jnp.bfloat16), "context", [(0, 1), (3, 2)])

    def across(array):
        return lax.ppermute(array.astype(jnp.bfloat16), "context", [(1, 2), (2, 1)])

    def outward(array):
        return lax.ppermute(array.astype(jnp.bfloat16), "context", [(1, 0), (2, 3)])

    in_one, in_two, in_three = inward(first), inward(second), inward(third)
    over_two = across(first + in_one.astype(jnp.float32))
    over_three = across(second + in_two.astype(jnp.float32))
    out_three = outward(third + over_two.astype(jnp.float32))
    return (
        own
        + in_three.astype(jnp.float32)
        + over_three.astype(jnp.float32)
        + out_three.astype(jnp.float32)
    )


def weight_grad(left, right, split_left):
    parts_dp = lax.axis_size("dp")
    index = lax.axis_index("dp")
    cut, kept = (left, right) if split_left else (right, left)
    if parts_dp == 2:
        halves = cut.reshape(cut.shape[0], 2, cut.shape[1] // 2)
        swap = [(0, 1), (1, 0)]
        cut_rows = jnp.concatenate(
            [pick(halves, index, 1), lax.ppermute(pick(halves, 1 - index, 1), "dp", swap)]
        )
        kept_rows = jnp.concatenate([kept, lax.ppermute(kept, "dp", swap)])
        step = cut_rows.shape[1] // 4

        def part(chunk):
            columns = lax.dynamic_slice_in_dim(cut_rows, chunk * step, step, 1)
            pair = (columns, kept_rows) if split_left else (kept_rows, columns)
            return jnp.einsum("ta,tb->ab", *pair, preferred_element_type=jnp.float32)

        return line_sum(part)
    whole = jnp.einsum("ta,tb->ab", left, right, preferred_element_type=jnp.float32)
    axis = 0 if split_left else 1
    mine = lax.psum_scatter(
        whole.astype(jnp.bfloat16), "dp", scatter_dimension=axis, tiled=True
    )
    step = mine.shape[axis] // 4
    return line_sum(
        lambda chunk: lax.dynamic_slice_in_dim(mine, chunk * step, step, axis).astype(jnp.float32)
    )


def gain_grad(partial):
    partial = partial + core_swap(partial)
    partial = partial + chip_swap(partial)
    return lax.psum_scatter(partial, ("dp", "context"), scatter_dimension=1, tiled=True)


def tables(positions):
    cosine, sine = angles(positions, HD)
    return jnp.concatenate([cosine] * 4, 1), jnp.concatenate([-sine, sine] * 2, 1)


def shards(
    tokens, segments, gain_one, w_query, w_keyval, w_out, gain_two, w_gateup, w_down, cotangent
):
    num_seqs, tok_count, model_width = tokens.shape
    head_dim = HD
    heads_kv = w_keyval.shape[1]
    heads = w_query.shape[1] // head_dim
    units = w_down.shape[0]
    place = lax.axis_index("context")
    tensor = lax.axis_index("tensor")
    quarter = tok_count // 4

    def own_rows(array):
        return lax.dynamic_slice_in_dim(array, tensor * quarter, quarter, 0)

    tokens_flat = tokens.reshape(tok_count, model_width)
    grad_out = cotangent.reshape(tok_count, model_width)
    query_index = place * tok_count + jnp.arange(tok_count, dtype=jnp.int32)
    cosine, sine = tables(query_index - segments[0])
    w_kv = w_keyval.reshape(model_width, 2 * head_dim)
    (
        rot_q, kv, attended_t, log_total, normed_one, normed_two, resid, hidden, grad_gateup, w_gu
    ) = forward(
        tokens_flat, segments, cosine, sine, gain_one[None], gain_two[None], w_query, w_kv, w_out,
        w_gateup, w_down, grad_out,
    )
    inverse_two = lax.rsqrt(jnp.mean(resid * resid, -1, keepdims=True) + epsilon)
    grad_normed_two = sum_scatter(
        jnp.einsum("rf,df->rd", grad_gateup, w_gu, preferred_element_type=jnp.float32)
    )
    grad_resid_norm, gain_two_part = norm_back(resid, inverse_two, gain_two, grad_normed_two)
    grad_resid = own_rows(grad_out).astype(jnp.float32) + grad_resid_norm
    grad_branch = gather_rows(grad_resid.astype(jnp.bfloat16))
    down_part = jnp.dot(hidden, w_down, preferred_element_type=jnp.float32)
    mixed = gather_rows((resid + sum_scatter(down_part)).astype(jnp.bfloat16))
    sent_wdown = weight_grad(hidden, grad_out, False)
    sent_gateup = weight_grad(normed_two, grad_gateup, True)
    attended = attended_t.T
    sent_wout = weight_grad(attended.astype(jnp.bfloat16), grad_branch, False)
    grad_attended = jnp.einsum(
        "rd,ad->ra", grad_branch, w_out, preferred_element_type=jnp.float32
    ).astype(jnp.bfloat16)
    delta = jnp.sum(
        (grad_attended.astype(jnp.float32) * attended).reshape(tok_count, heads, head_dim), -1
    ).T
    queries = rot_q.reshape(tok_count, heads, head_dim)
    grad_heads = grad_attended.reshape(tok_count, heads, head_dim)
    grad_rot_q = jnp.zeros((tok_count, heads, head_dim), jnp.float32)
    grad_blocks = []
    for back in range(4):
        keys, values = kv[back][:, :head_dim], kv[back][:, head_dim:]
        index = (place - back) * tok_count + jnp.arange(tok_count, dtype=jnp.int32)
        allowed = (index[None, :] <= query_index[:, None]) & (
            index[None, :] >= segments[0][:, None]
        )
        raw = jnp.einsum("qhd,pd->hqp", queries, keys, preferred_element_type=jnp.float32)
        probs = jnp.where(allowed, jnp.exp(jnp.where(allowed, raw, neg_large) - log_total.reshape(heads, tok_count, 1)), 0.0)
        grad_probs = jnp.einsum("qhd,pd->hqp", grad_heads, values, preferred_element_type=jnp.float32)
        grad_raw = (probs * (grad_probs - delta[..., None])).astype(jnp.bfloat16)
        grad_raw = jnp.where(allowed, grad_raw, 0)
        grad_rot_q = grad_rot_q + 0.125 * jnp.einsum("hqp,pd->qhd", grad_raw, keys, preferred_element_type=jnp.float32)
        grad_key = jnp.einsum("hqp,qhd->pd", grad_raw, queries, preferred_element_type=jnp.float32)
        grad_value = jnp.einsum("hqp,qhd->pd", probs.astype(jnp.bfloat16), grad_heads, preferred_element_type=jnp.float32)
        grad_blocks.append(jnp.concatenate([grad_key, grad_value], -1))
    grad_kv = grad_blocks[0]
    for back in range(1, 4):
        grad_kv = grad_kv + lax.ppermute(
            grad_blocks[back].astype(jnp.bfloat16),
            "context",
            [(i + back, i) for i in range(4 - back)],
        ).astype(jnp.float32)
    cos, sin = angles(query_index - segments[0], head_dim)
    grad_queries = (
        rotate(grad_rot_q, cos[:, None, :], -sin[:, None, :]).reshape(tok_count, -1).astype(jnp.bfloat16)
    )
    grad_keyval = jnp.concatenate(
        [rotate(grad_kv[..., :head_dim], cos, -sin), grad_kv[..., head_dim:]], -1
    ).astype(jnp.bfloat16)
    grad_normed_part = jnp.einsum(
        "re,de->rd", grad_queries, w_query, preferred_element_type=jnp.float32
    ) + jnp.einsum("re,de->rd", grad_keyval, w_kv, preferred_element_type=jnp.float32)
    sent_wqkv = weight_grad(
        normed_one, jnp.concatenate([grad_queries, grad_keyval], 1), True
    )
    grad_normed_one = sum_scatter(grad_normed_part)
    x_own = own_rows(tokens_flat).astype(jnp.float32)
    inverse_one = lax.rsqrt(jnp.mean(x_own * x_own, -1, keepdims=True) + epsilon)
    grad_x_norm, gain_one_part = norm_back(x_own, inverse_one, gain_one, grad_normed_one)
    grad_tokens = gather_rows((grad_resid + grad_x_norm).astype(jnp.bfloat16))
    gains = gain_grad(jnp.stack([gain_one_part, gain_two_part]))
    width_q = w_query.shape[1]
    return (
        mixed.reshape(num_seqs, tok_count, model_width),
        grad_tokens.astype(jnp.float32).reshape(num_seqs, tok_count, model_width),
        gains[0],
        sent_wqkv[:, :width_q],
        sent_wqkv[:, width_q:].reshape(-1, heads_kv, 2 * head_dim),
        sent_wout,
        gains[1],
        sent_gateup.reshape(-1, units // 128, 2, 128).transpose(0, 2, 1, 3).reshape(-1, 2, units),
        sent_wdown,
    )


def solution(mesh):
    return jax.shard_map(
        shards,
        mesh=mesh,
        in_specs=(
            P("dp", "context", None),
            P("dp", "context"),
            P(),
            P(None, "tensor"),
            P(None, "tensor", None),
            P("tensor", None),
            P(),
            P(None, None, "tensor"),
            P("tensor", None),
            P("dp", "context", None),
        ),
        out_specs=(
            P("dp", "context", None),
            P("dp", "context", None),
            P(("dp", "context")),
            P(("dp", "context"), "tensor"),
            P(("dp", "context"), "tensor", None),
            P("tensor", ("dp", "context")),
            P(("dp", "context")),
            P(("dp", "context"), None, "tensor"),
            P("tensor", ("dp", "context")),
        ),
        check_vma=False,
    )
```

time: 1020 us -> 671 us (0.66)
  waiting for transfers between devices: 639 us -> 155 us
  starting transfers between devices: 1.47 us -> 130 us
  Pallas kernels: 0 us -> 72.1 us
  local copies, waits for them, and re-layouts: 69 us -> 113 us
  blocking collectives: 43.7 us -> 0 us
  loops' own time: 31.9 us -> 0 us
  other arithmetic: 54.8 us -> 37.5 us
    reduce_scatter x6 -> x0, waiting for transfers between devices: 449 us -> none  [the longest x1 193 us: shards(): lax.psum_scatter(grad_wgateup.astype(jnp.bfloat16), ('dp', 'context'), sc...]
    psum x3 -> x0, waiting for transfers between devices: 191 us -> none  [the longest x1 87.3 us: shards(): lax.psum(down_part.astype(jnp.bfloat16), 'tensor').astype(jnp.float32)]
    ppermute x0 -> x49, starting transfers between devices: none -> 130 us  [the longest x12 72.8 us: inward(): return lax.ppermute(array.astype(jnp.bfloat16), 'context', [(0, 1), (3, 2)])]
    ppermute x0 -> x49, waiting for transfers between devices: none -> 110 us  [the longest x12 52 us: inward(): return lax.ppermute(array.astype(jnp.bfloat16), 'context', [(0, 1), (3, 2)])]
    pallas_call x0 -> x1, Pallas kernels: none -> 72.1 us  [forward(): pl.pallas_call(forward_kernel, out_shape=[jax.ShapeDtypeStruct(*out) for...]
    unnamed x9 -> x2, waiting for transfers between devices: 0.15 us -> 44.8 us
    another operation x15 -> x0, loops' own time: 31.9 us -> none  [the longest x1 10.5 us: attend(): lax.scan(stats_step, (start_max, start_sum), (key_blocks, seg_blocks, ind...]
    slice x48 -> x6, local copies, waits for them, and re-layouts: 34.4 us -> 3.45 us  [the longest x1 1.07 us: shards(): gains[1]]
  transfers between devices with their start and end apart: 9 -> 50, of which waited for: 9 -> 14; matrix products, arithmetic and copies ran while one was open for 6% -> 37% of each run, Pallas kernels for 0% -> 11%
where the time goes in v1:
time: 671 us; the launch traced here: 661 us
  waiting for transfers between devices  155 us (23%)
  matrix products  136 us (20%)
  starting transfers between devices  130 us (19%)
  local copies, waits for them, and re-layouts  113 us (17%)
  Pallas kernels  72.1 us (11%)
  other arithmetic  37.5 us (6%)
  between operations  18.3 us (3%)
    ppermute x12, starting transfers between devices, inward(): return lax.ppermute(array.astype(jnp.bfloat16), 'context', [(0, 1), (3, 2)])  72.8 us
    pallas_call x1, Pallas kernels, forward(): pl.pallas_call(forward_kernel, out_shape=[jax.ShapeDtypeStruct(*out) for...  72.1 us
    ppermute x12, waiting for transfers between devices, inward(): return lax.ppermute(array.astype(jnp.bfloat16), 'context', [(0, 1), (3, 2)])  52 us
    dot_general x16, matrix products, part(): return jnp.einsum('ta,tb->ab', *pair, preferred_element_type=jnp.float32)  46 us
    unnamed x2, waiting for transfers between devices  44.8 us
    unnamed x190, local copies, waits for them, and re-layouts  37.6 us
    ppermute x7, waiting for transfers between devices, chip_swap(): return lax.ppermute(array, 'tensor', [(0, 2), (2, 0), (1, 3), (3, 1)])  34 us
    dynamic_slice x6, local copies, waits for them, and re-layouts, pick(): return lax.dynamic_index_in_dim(array, index, axis, keepdims=False)  27.8 us
  transfers between devices with their start and end apart: 50, of which 14 were waited for; matrix products, arithmetic and copies ran while one was open for 37% of the time, Pallas kernels for 11%

profile of v1, /device:TPU:24, one launch (start us, length us, event | category | flops | bytes accessed | tf_op | source)
XLA Modules:
  0.0 661.1 jit_solution(5746551335179576796)
XLA Ops:
  18.7 72.1 %forward.1 = (bf16[512,512]{1,0:T(8,128)(2,1)}, bf16[4,512,128]{2,1,0:T(8,128)(2,1)}, f32[512,512]{1,0:T(8,128)}, f32[8,1,512]{2,1,0:T(1,128)}, bf16[512,2048]{1...) custom-call(bf16[512,2048]{1,0:T(8,128)(2,1)} %bitcast.403, ...), custom_call_target="tpu_custom_call" | custom-call | tf_op jit(solution)/shard_map/forward/pallas_call | solution.py:350
  91.4 11.2 %fusion.208 = f32[512,2048]{1,0:T(8,128)} fusion(bf16[512,2816]{1,0:T(8,128)(2,1)} %get-tuple-element.21, bf16[2048,2816]{1,0:T(8,128)(2,1)} %get-tuple-element.22), kind=kOutput, calls=%fused_computation.338 | convolution fusion | flops 5905580032 | bytes 18612224 | tf_op jit(solution)/shard_map/rf,df->rd/dot_general | solution.py:528
  107.5 5.8 fusion.207
  131.6 4.6 reshape.511
  136.3 8.5 %constant_dynamic-slice_fusion.1 = (bf16[512,1,1024]{2,1,0:T(2,128)(2,1)}, bf16[512,1,1024]{2,1,0:T(2,128)(2,1)}) fusion(bf16[512,2,1024]{2,1,0:T(2,128)(2,1)} %reshape.511, s32[]{:T(128)S(6)} %select_n.279, s32[]{:T(128)S(6)} %select_n.278), kind=kLoop, calls=%fused_computation.259 | loop fusion | bytes 4194312 | tf_op jit(solution)/shard_map/jit(dynamic_index_in_dim)/dynamic_slice | solution.py:410
  149.3 4.6 fusion.146
  153.9 4.5 fusion.145
  158.4 4.6 fusion.143
  166.4 8.6 %constant_dynamic-slice_fusion.7 = (bf16[512,1,1024]{2,1,0:T(2,128)(2,1)}, bf16[512,1,1024]{2,1,0:T(2,128)(2,1)}) fusion(bf16[512,2,1024]{2,1,0:T(2,128)(2,1)} %reshape.509, s32[]{:T(128)S(6)} %select_n.279, s32[]{:T(128)S(6)} %select_n.278), kind=kLoop, calls=%fused_computation.277 | loop fusion | bytes 4194312 | tf_op jit(solution)/shard_map/jit(dynamic_index_in_dim)/dynamic_slice | solution.py:410
  197.9 9.4 %collective-permute-done.5 = bf16[128,2048]{1,0:T(8,128)(2,1)S(1)} collective-permute-done((bf16[128,2048]{1,0:T(8,128)(2,1)S(1)}, bf16[128,2048]{1,0:T(8,128)(2,1)S(1)}, u32[]{:S(2)}, u32[]{:S(2)}) %collective-permute-start.5) | collective-permute-done | bytes 524320 | tf_op jit(solution)/shard_map/ppermute | solution.py:406
  208.9 8.8 %collective-permute-done.1 = bf16[128,2048]{1,0:T(8,128)(2,1)S(1)} collective-permute-done((bf16[128,2048]{1,0:T(8,128)(2,1)S(1)}, bf16[128,2048]{1,0:T(8,128)(2,1)S(1)}, u32[]{:S(2)}, u32[]{:S(2)}) %collective-permute-start.1) | collective-permute-done | bytes 524320 | tf_op jit(solution)/shard_map/ppermute | solution.py:406
  226.3 8.9 %collective-permute-done.2 = bf16[128,2048]{1,0:T(8,128)(2,1)S(1)} collective-permute-done((bf16[128,2048]{1,0:T(8,128)(2,1)S(1)}, bf16[128,2048]{1,0:T(8,128)(2,1)S(1)}, u32[]{:S(2)}, u32[]{:S(2)}) %collective-permute-start.2) | collective-permute-done | bytes 524320 | tf_op jit(solution)/shard_map/ppermute | solution.py:406
  238.8 6.0 collective-permute-done.6
  246.6 6.4 collective-permute-done.46
  253.3 11.4 %collective-permute-done.44 = bf16[1408,256]{1,0:T(8,128)(2,1)S(1)} collective-permute-done((bf16[1408,256]{1,0:T(8,128)(2,1)S(1)}, bf16[1408,256]{1,0:T(8,128)(2,1)S(1)}, u32[]{:S(2)}, u32[]{:S(2)}) %collective-permute-start.44) | collective-permute-done | bytes 720928 | tf_op jit(solution)/shard_map/ppermute | solution.py:439
  291.6 6.3 fusion.63
  303.9 4.6 fusion.26
  310.8 4.7 fusion.25
  315.5 6.4 constant_dynamic-slice_fusion.4
  330.8 18.1 %collective-permute-start.9 = (bf16[512,128]{1,0:T(8,128)(2,1)}, bf16[512,128]{1,0:T(8,128)(2,1)}, u32[]{:S(2)}, u32[]{:S(2)}) collective-permute-start(bf16[512,128]{1,0:T(8,128)(2,1)} %pad_maximum_fusion.7), channel_id=1, source_target_pairs={{2,0},{3,1},{6,4},{7,5},{10,8},{11,9},{14,12},{15,13},{18,16},{19,... | collective-permute-start | bytes 393224 | tf_op jit(solution)/shard_map/ppermute | solution.py:566
  354.0 5.9 fusion.24
  410.8 17.3 %collective-permute-done.18 = bf16[512,640]{0,1:T(8,128)(2,1)S(1)} collective-permute-done((bf16[512,640]{0,1:T(8,128)(2,1)S(1)}, bf16[512,640]{0,1:T(8,128)(2,1)S(1)}, u32[]{:S(2)}, u32[]{:S(2)}) %collective-permute-start.18) | collective-permute-done | bytes 655392 | tf_op jit(solution)/shard_map/ppermute | solution.py:469
  430.0 5.2 collective-permute-start.20
  441.9 33.4 %collective-permute-done.20 = bf16[256,640]{1,0:T(8,128)(2,1)S(1)} collective-permute-done((bf16[256,640]{1,0:T(8,128)(2,1)S(1)}, bf16[256,640]{1,0:T(8,128)(2,1)S(1)}, u32[]{:S(2)}, u32[]{:S(2)}) %collective-permute-start.20) | collective-permute-done | bytes 327712 | tf_op jit(solution)/shard_map/ppermute | solution.py:439
  499.2 37.0 %collective-permute-start.19 = (bf16[256,640]{1,0:T(8,128)(2,1)}, bf16[256,640]{1,0:T(8,128)(2,1)}, u32[]{:S(2)}, u32[]{:S(2)}) collective-permute-start(bf16[256,640]{1,0:T(8,128)(2,1)} %get-tuple-element.95), channel_id=1, source_target_pairs={{0,1},{3,2},{4,5},{7,6},{8,9},{11,10},{12,13},{15,14},{16,17},{19,... | collective-permute-start | bytes 983048 | tf_op jit(solution)/shard_map/ppermute | solution.py:439
  549.6 6.3 fusion.193
  557.9 6.7 %collective-permute-start.27 = (bf16[512,256]{1,0:T(8,128)(2,1)}, bf16[512,256]{1,0:T(8,128)(2,1)}, u32[]{:S(2)}, u32[]{:S(2)}) collective-permute-start(bf16[512,256]{1,0:T(8,128)(2,1)} %get-tuple-element.97), channel_id=1, source_target_pairs={{0,1},{3,2},{4,5},{7,6},{8,9},{11,10},{12,13},{15,14},{16,17},{19,... | collective-permute-start | bytes 786440 | tf_op jit(solution)/shard_map/ppermute | solution.py:439
  569.4 44.8 %reduce-scatter.4.cloned.1.call-done = f32[256,2]{1,0:T(8,128)} async-done(((f32[2048,2]{1,0:T(8,128)}), f32[256,2]{1,0:T(8,128)}) %reduce-scatter.4.cloned.1.call-update) | async-done | bytes 2064
  632.3 5.8 fusion.41
  638.2 4.6 reshape.512
  642.8 5.7 copy.292
  648.5 5.5 copy.297
  (398 shorter events, 248.9 us)
Async XLA Ops:
  7.2 607.0 %reduce-scatter.4.cloned.1.call-start = ((), (), s32[]{:S(2)}) async-start(), calls=%async_computation.1 | async-start | bytes 1179648
  14.2 207.6 %collective-permute-start.42 = (bf16[512,1024]{1,0:T(8,128)(2,1)}, bf16[512,1024]{1,0:T(8,128)(2,1)}, u32[]{:S(2)}, u32[]{:S(2)}) collective-permute-start(bf16[512,1024]{1,0:T(8,128)(2,1)} %bitcast.440), channel_id=1, source_target_pairs={{0,4},{4,0},{1,5},{5,1},{2,6},{6,2},{3,7},{7,3},{8,12},{12,8},{9,1... | collective-permute-start | bytes 3145736 | tf_op jit(solution)/shard_map/ppermute | solution.py:467
  90.8 175.7 %collective-permute-start.34 = (bf16[512,2816]{1,0:T(8,128)(2,1)}, bf16[512,2816]{1,0:T(8,128)(2,1)}, u32[]{:S(2)}, u32[]{:S(2)}) collective-permute-start(bf16[512,2816]{1,0:T(8,128)(2,1)} %get-tuple-element.21), channel_id=1, source_target_pairs={{0,4},{4,0},{1,5},{5,1},{2,6},{6,2},{3,7},{7,3},{8,12},{12,8},{9,1... | collective-permute-start | bytes 8650760 | tf_op jit(solution)/shard_map/ppermute | solution.py:469
  105.3 84.0 %collective-permute-start.4 = (bf16[2,128,2048]{2,1,0:T(8,128)(2,1)}, bf16[2,128,2048]{2,1,0:T(8,128)(2,1)}, u32[]{:S(2)}, u32[]{:S(2)}) collective-permute-start(bf16[2,128,2048]{2,1,0:T(8,128)(2,1)} %fusion.83), channel_id=1, source_target_pairs={{0,8},{8,0},{16,24},{24,16},{1,9},{9,1},{17,25},{25,17},{2,10},{10... | collective-permute-start | bytes 3145736 | tf_op jit(solution)/shard_map/ppermute | solution.py:402
  106.0 89.7 %collective-permute-start.41 = (bf16[512,1408]{1,0:T(8,128)(2,1)}, bf16[512,1408]{1,0:T(8,128)(2,1)}, u32[]{:S(2)}, u32[]{:S(2)}) collective-permute-start(bf16[512,1408]{1,0:T(8,128)(2,1)} %get-tuple-element.20), channel_id=1, source_target_pairs={{0,4},{4,0},{1,5},{5,1},{2,6},{6,2},{3,7},{7,3},{8,12},{12,8},{9,1... | collective-permute-start | bytes 4325384 | tf_op jit(solution)/shard_map/ppermute | solution.py:469
  116.5 76.0 %collective-permute-start = (bf16[2,128,2048]{2,1,0:T(8,128)(2,1)}, bf16[2,128,2048]{2,1,0:T(8,128)(2,1)}, u32[]{:S(2)}, u32[]{:S(2)}) collective-permute-start(bf16[2,128,2048]{2,1,0:T(8,128)(2,1)} %fusion.85), channel_id=1, source_target_pairs={{0,8},{8,0},{16,24},{24,16},{1,9},{9,1},{17,25},{25,17},{2,10},{10... | collective-permute-start | bytes 3145736 | tf_op jit(solution)/shard_map/ppermute | solution.py:402
  189.3 84.3 %collective-permute-start.33 = (bf16[512,1024]{1,0:T(8,128)(2,1)}, bf16[512,1024]{1,0:T(8,128)(2,1)S(1)}, u32[]{:S(2)}, u32[]{:S(2)}) collective-permute-start(bf16[512,1024]{1,0:T(8,128)(2,1)} %bitcast.434), channel_id=1, source_target_pairs={{0,4},{4,0},{1,5},{5,1},{2,6},{6,2},{3,7},{7,3},{8,12},{12,8},{9,1... | collective-permute-start | bytes 3145736 | tf_op jit(solution)/shard_map/ppermute | solution.py:467
  207.3 202.2 %collective-permute-start.17 = (bf16[512,1024]{1,0:T(8,128)(2,1)}, bf16[512,1024]{1,0:T(8,128)(2,1)}, u32[]{:S(2)}, u32[]{:S(2)}) collective-permute-start(bf16[512,1024]{1,0:T(8,128)(2,1)} %bitcast.364), channel_id=1, source_target_pairs={{0,4},{4,0},{1,5},{5,1},{2,6},{6,2},{3,7},{7,3},{8,12},{12,8},{9,1... | collective-permute-start | bytes 3145736 | tf_op jit(solution)/shard_map/ppermute | solution.py:467
  253.1 28.2 %collective-permute-start.7 = (bf16[2,128,2048]{2,1,0:T(8,128)(2,1)S(1)}, bf16[2,128,2048]{2,1,0:T(8,128)(2,1)S(1)}, u32[]{:S(2)}, u32[]{:S(2)}) collective-permute-start(bf16[2,128,2048]{2,1,0:T(8,128)(2,1)S(1)} %maximum_select_fusion.5), channel_id=1, source_target_pairs={{0,8},{8,0},{16,24},{24,16},{1,9},{9,1},{17,25},{25,17},{2,10},{10... | collective-permute-start | bytes 3145736 | tf_op jit(solution)/shard_map/ppermute | solution.py:402
  266.4 109.5 %collective-permute-start.3 = (bf16[2,128,2048]{2,1,0:T(8,128)(2,1)}, bf16[2,128,2048]{2,1,0:T(8,128)(2,1)}, u32[]{:S(2)}, u32[]{:S(2)}) collective-permute-start(bf16[2,128,2048]{2,1,0:T(8,128)(2,1)} %maximum_select_fusion.4), channel_id=1, source_target_pairs={{0,8},{8,0},{16,24},{24,16},{1,9},{9,1},{17,25},{25,17},{2,10},{10... | collective-permute-start | bytes 3145736 | tf_op jit(solution)/shard_map/ppermute | solution.py:402
  268.5 129.0 %collective-permute-start.45 = (bf16[1408,256]{1,0:T(8,128)(2,1)}, bf16[1408,256]{1,0:T(8,128)(2,1)}, u32[]{:S(2)}, u32[]{:S(2)}) collective-permute-start(bf16[1408,256]{1,0:T(8,128)(2,1)} %add_convert_fusion.5), channel_id=1, source_target_pairs={{1,2},{2,1},{5,6},{6,5},{9,10},{10,9},{13,14},{14,13},{17,18},{18,... | collective-permute-start | bytes 2162696 | tf_op jit(solution)/shard_map/ppermute | solution.py:442
  324.3 60.0 %collective-permute-start.10 = (bf16[512,128]{1,0:T(8,128)(2,1)}, bf16[512,128]{1,0:T(8,128)(2,1)}, u32[]{:S(2)}, u32[]{:S(2)}) collective-permute-start(bf16[512,128]{1,0:T(8,128)(2,1)} %pad_maximum_fusion.8), channel_id=1, source_target_pairs={{3,0},{7,4},{11,8},{15,12},{19,16},{23,20},{27,24},{31,28}} | collective-permute-start | bytes 393224 | tf_op jit(solution)/shard_map/ppermute | solution.py:566
  330.8 56.2 %collective-permute-start.9 = (bf16[512,128]{1,0:T(8,128)(2,1)}, bf16[512,128]{1,0:T(8,128)(2,1)}, u32[]{:S(2)}, u32[]{:S(2)}) collective-permute-start(bf16[512,128]{1,0:T(8,128)(2,1)} %pad_maximum_fusion.7), channel_id=1, source_target_pairs={{2,0},{3,1},{6,4},{7,5},{10,8},{11,9},{14,12},{15,13},{18,16},{19,... | collective-permute-start | bytes 393224 | tf_op jit(solution)/shard_map/ppermute | solution.py:566
  388.3 48.6 %collective-permute-start.26 = (bf16[512,1024]{1,0:T(8,128)(2,1)}, bf16[512,1024]{1,0:T(8,128)(2,1)}, u32[]{:S(2)}, u32[]{:S(2)}) collective-permute-start(bf16[512,1024]{1,0:T(8,128)(2,1)} %bitcast.366), channel_id=1, source_target_pairs={{0,4},{4,0},{1,5},{5,1},{2,6},{6,2},{3,7},{7,3},{8,12},{12,8},{9,1... | collective-permute-start | bytes 3145736 | tf_op jit(solution)/shard_map/ppermute | solution.py:467
  397.5 30.6 %collective-permute-start.18 = (bf16[512,640]{0,1:T(8,128)(2,1)S(1)}, bf16[512,640]{0,1:T(8,128)(2,1)S(1)}, u32[]{:S(2)}, u32[]{:S(2)}) collective-permute-start(bf16[512,640]{0,1:T(8,128)(2,1)S(1)} %pad_maximum_fusion.2), channel_id=1, source_target_pairs={{0,4},{4,0},{1,5},{5,1},{2,6},{6,2},{3,7},{7,3},{8,12},{12,8},{9,1... | collective-permute-start | bytes 1966088 | tf_op jit(solution)/shard_map/ppermute | solution.py:469
  397.9 38.9 %collective-permute-start.25 = (bf16[512,512]{0,1:T(8,128)(2,1)S(1)}, bf16[512,512]{0,1:T(8,128)(2,1)S(1)}, u32[]{:S(2)}, u32[]{:S(2)}) collective-permute-start(bf16[512,512]{0,1:T(8,128)(2,1)S(1)} %copy-done.19), channel_id=1, source_target_pairs={{0,4},{4,0},{1,5},{5,1},{2,6},{6,2},{3,7},{7,3},{8,12},{12,8},{9,1... | collective-permute-start | bytes 1572872 | tf_op jit(solution)/shard_map/ppermute | solution.py:469
  401.8 83.3 %collective-permute-start.38 = (bf16[256,2816]{1,0:T(8,128)(2,1)S(1)}, bf16[256,2816]{1,0:T(8,128)(2,1)S(1)}, u32[]{:S(2)}, u32[]{:S(2)}) collective-permute-start(bf16[256,2816]{1,0:T(8,128)(2,1)S(1)} %copy-done.31), channel_id=1, source_target_pairs={{0,1},{3,2},{4,5},{7,6},{8,9},{11,10},{12,13},{15,14},{16,17},{19,... | collective-permute-start | bytes 4325384 | tf_op jit(solution)/shard_map/ppermute | solution.py:439
  409.4 78.4 %collective-permute-start.36 = (bf16[256,2816]{1,0:T(8,128)(2,1)S(1)}, bf16[256,2816]{1,0:T(8,128)(2,1)S(1)}, u32[]{:S(2)}, u32[]{:S(2)}) collective-permute-start(bf16[256,2816]{1,0:T(8,128)(2,1)S(1)} %copy-done.30), channel_id=1, source_target_pairs={{0,1},{3,2},{4,5},{7,6},{8,9},{11,10},{12,13},{15,14},{16,17},{19,... | collective-permute-start | bytes 4325384 | tf_op jit(solution)/shard_map/ppermute | solution.py:439
  430.0 45.3 %collective-permute-start.20 = (bf16[256,640]{1,0:T(8,128)(2,1)S(1)}, bf16[256,640]{1,0:T(8,128)(2,1)S(1)}, u32[]{:S(2)}, u32[]{:S(2)}) collective-permute-start(bf16[256,640]{1,0:T(8,128)(2,1)S(1)} %get-tuple-element.126), channel_id=1, source_target_pairs={{0,1},{3,2},{4,5},{7,6},{8,9},{11,10},{12,13},{15,14},{16,17},{19,... | collective-permute-start | bytes 983048 | tf_op jit(solution)/shard_map/ppermute | solution.py:439
  436.8 53.3 %collective-permute-start.11 = (bf16[2,128,2048]{2,1,0:T(8,128)(2,1)S(1)}, bf16[2,128,2048]{2,1,0:T(8,128)(2,1)S(1)}, u32[]{:S(2)}, u32[]{:S(2)}) collective-permute-start(bf16[2,128,2048]{2,1,0:T(8,128)(2,1)S(1)} %fusion.84), channel_id=1, source_target_pairs={{0,8},{8,0},{16,24},{24,16},{1,9},{9,1},{17,25},{25,17},{2,10},{10... | collective-permute-start | bytes 3145736 | tf_op jit(solution)/shard_map/ppermute | solution.py:402
  436.9 43.6 %collective-permute-start.22 = (bf16[256,640]{1,0:T(8,128)(2,1)S(1)}, bf16[256,640]{1,0:T(8,128)(2,1)S(1)}, u32[]{:S(2)}, u32[]{:S(2)}) collective-permute-start(bf16[256,640]{1,0:T(8,128)(2,1)S(1)} %get-tuple-element.124), channel_id=1, source_target_pairs={{0,1},{3,2},{4,5},{7,6},{8,9},{11,10},{12,13},{15,14},{16,17},{19,... | collective-permute-start | bytes 983048 | tf_op jit(solution)/shard_map/ppermute | solution.py:439
  485.0 70.9 %collective-permute-start.21 = (bf16[256,640]{1,0:T(8,128)(2,1)S(1)}, bf16[256,640]{1,0:T(8,128)(2,1)}, u32[]{:S(2)}, u32[]{:S(2)}) collective-permute-start(bf16[256,640]{1,0:T(8,128)(2,1)S(1)} %add_convert_fusion.8), channel_id=1, source_target_pairs={{1,2},{2,1},{5,6},{6,5},{9,10},{10,9},{13,14},{14,13},{17,18},{18,... | collective-permute-start | bytes 983048 | tf_op jit(solution)/shard_map/ppermute | solution.py:442
  490.1 57.9 %collective-permute-start.39 = (bf16[256,2816]{1,0:T(8,128)(2,1)}, bf16[256,2816]{1,0:T(8,128)(2,1)}, u32[]{:S(2)}, u32[]{:S(2)}) collective-permute-start(bf16[256,2816]{1,0:T(8,128)(2,1)} %add_convert_fusion.1), channel_id=1, source_target_pairs={{1,2},{2,1},{5,6},{6,5},{9,10},{10,9},{13,14},{14,13},{17,18},{18,... | collective-permute-start | bytes 4325384 | tf_op jit(solution)/shard_map/ppermute | solution.py:442
  492.3 46.2 %collective-permute-start.12 = (bf16[128,2048]{1,0:T(8,128)(2,1)S(1)}, bf16[128,2048]{1,0:T(8,128)(2,1)S(1)}, u32[]{:S(2)}, u32[]{:S(2)}) collective-permute-start(bf16[128,2048]{1,0:T(8,128)(2,1)S(1)} %fusion.91), channel_id=1, source_target_pairs={{0,16},{16,0},{8,24},{24,8},{1,17},{17,1},{9,25},{25,9},{2,18},{18... | collective-permute-start | bytes 1572872 | tf_op jit(solution)/shard_map/ppermute | solution.py:406
  494.6 63.2 %collective-permute-start.29 = (bf16[512,256]{1,0:T(8,128)(2,1)}, bf16[512,256]{1,0:T(8,128)(2,1)}, u32[]{:S(2)}, u32[]{:S(2)}) collective-permute-start(bf16[512,256]{1,0:T(8,128)(2,1)} %add_convert_fusion.11), channel_id=1, source_target_pairs={{1,2},{2,1},{5,6},{6,5},{9,10},{10,9},{13,14},{14,13},{17,18},{18,... | collective-permute-start | bytes 786440 | tf_op jit(solution)/shard_map/ppermute | solution.py:442
  499.2 65.3 %collective-permute-start.19 = (bf16[256,640]{1,0:T(8,128)(2,1)}, bf16[256,640]{1,0:T(8,128)(2,1)}, u32[]{:S(2)}, u32[]{:S(2)}) collective-permute-start(bf16[256,640]{1,0:T(8,128)(2,1)} %get-tuple-element.95), channel_id=1, source_target_pairs={{0,1},{3,2},{4,5},{7,6},{8,9},{11,10},{12,13},{15,14},{16,17},{19,... | collective-permute-start | bytes 983048 | tf_op jit(solution)/shard_map/ppermute | solution.py:439
  544.0 25.4 %collective-permute-start.24 = (bf16[256,640]{1,0:T(8,128)(2,1)}, bf16[256,640]{1,0:T(8,128)(2,1)}, u32[]{:S(2)}, u32[]{:S(2)}) collective-permute-start(bf16[256,640]{1,0:T(8,128)(2,1)} %get-tuple-element.96), channel_id=1, source_target_pairs={{1,0},{2,3},{5,4},{6,7},{9,8},{10,11},{13,12},{14,15},{17,16},{18,... | collective-permute-start | bytes 983048 | tf_op jit(solution)/shard_map/ppermute | solution.py:445
  555.9 76.4 %collective-permute-start.37 = (bf16[256,2816]{1,0:T(8,128)(2,1)}, bf16[256,2816]{1,0:T(8,128)(2,1)}, u32[]{:S(2)}, u32[]{:S(2)}) collective-permute-start(bf16[256,2816]{1,0:T(8,128)(2,1)} %add_convert_fusion.2), channel_id=1, source_target_pairs={{1,2},{2,1},{5,6},{6,5},{9,10},{10,9},{13,14},{14,13},{17,18},{18,... | collective-permute-start | bytes 4325384 | tf_op jit(solution)/shard_map/ppermute | solution.py:442
  557.9 58.7 %collective-permute-start.27 = (bf16[512,256]{1,0:T(8,128)(2,1)}, bf16[512,256]{1,0:T(8,128)(2,1)}, u32[]{:S(2)}, u32[]{:S(2)}) collective-permute-start(bf16[512,256]{1,0:T(8,128)(2,1)} %get-tuple-element.97), channel_id=1, source_target_pairs={{0,1},{3,2},{4,5},{7,6},{8,9},{11,10},{12,13},{15,14},{16,17},{19,... | collective-permute-start | bytes 786440 | tf_op jit(solution)/shard_map/ppermute | solution.py:439
  564.6 67.7 %collective-permute-start.35 = (bf16[256,2816]{1,0:T(8,128)(2,1)}, bf16[256,2816]{1,0:T(8,128)(2,1)}, u32[]{:S(2)}, u32[]{:S(2)}) collective-permute-start(bf16[256,2816]{1,0:T(8,128)(2,1)} %get-tuple-element.80), channel_id=1, source_target_pairs={{0,1},{3,2},{4,5},{7,6},{8,9},{11,10},{12,13},{15,14},{16,17},{19,... | collective-permute-start | bytes 4325384 | tf_op jit(solution)/shard_map/ppermute | solution.py:439
  567.0 65.3 %collective-permute-start.40 = (bf16[256,2816]{1,0:T(8,128)(2,1)}, bf16[256,2816]{1,0:T(8,128)(2,1)}, u32[]{:S(2)}, u32[]{:S(2)}) collective-permute-start(bf16[256,2816]{1,0:T(8,128)(2,1)} %get-tuple-element.81), channel_id=1, source_target_pairs={{1,0},{2,3},{5,4},{6,7},{9,8},{10,11},{13,12},{14,15},{17,16},{18,... | collective-permute-start | bytes 4325384 | tf_op jit(solution)/shard_map/ppermute | solution.py:445
  569.4 58.5 %collective-permute-start.14 = (bf16[2,128,2048]{2,1,0:T(8,128)(2,1)}, bf16[2,128,2048]{2,1,0:T(8,128)(2,1)}, u32[]{:S(2)}, u32[]{:S(2)}) collective-permute-start(bf16[2,128,2048]{2,1,0:T(8,128)(2,1)} %maximum_select_fusion.7), channel_id=1, source_target_pairs={{0,8},{8,0},{16,24},{24,16},{1,9},{9,1},{17,25},{25,17},{2,10},{10... | collective-permute-start | bytes 3145736 | tf_op jit(solution)/shard_map/ppermute | solution.py:402
  (106 other events, 1594.6 us)
Sparse Core Ops, SparseCore 0:
  548.1 66.0 reduce-scatter.3

commit v2 on v1

--- a/solution.py
+++ b/solution.py
@@ -1,4 +1,5 @@
-import math
+import functools
+import types
 
 import jax
 import jax.numpy as jnp
@@ -14,30 +15,12 @@
 neg_large = -1e30
 
 
-def rotate(values, cosine, sine):
-    half_width = values.shape[-1] // 2
-    first_half = values[..., :half_width]
-    second_half = values[..., half_width:]
-    return jnp.concatenate(
-        [first_half * cosine - second_half * sine, second_half * cosine + first_half * sine], -1
-    )
-
-
 def angles(positions, head_dim):
     freqs = 10000.0 ** (-(jnp.arange(head_dim // 2, dtype=jnp.float32) * 2.0) / head_dim)
     phase = positions.astype(jnp.float32)[:, None] * freqs[None, :]
     return (jnp.cos(phase), jnp.sin(phase))
 
 
-def norm_back(inputs, inverse, gain, grad_normed):
-    grad_gain = jnp.sum(grad_normed * inputs * inverse, 0)
-    scaled = grad_normed * gain
-    grad_inputs = inverse * scaled - inputs * (inverse * inverse * inverse) * jnp.mean(
-        scaled * inputs, -1, keepdims=True
-    )
-    return (grad_inputs, grad_gain)
-
-
 MESH = pl.DeviceIdType.MESH
 MIB = 1 << 20
 
@@ -65,12 +48,15 @@
 
 
 def forward_kernel(
+    swap,
     x_hbm, seg_ref, cos_ref, sin_ref, gain_one_ref, gain_two_ref, wq_hbm, wkv_hbm, wout_hbm, raw_hbm,
     wdown_hbm, g_hbm,
-    q_out, kv_out, att_out, lse_out, n1_out, n2_out, resid_out, hid_out, gg_out, wgu_out,
+    q_out, kv_out, att_out, lse_out, n1_out, n2_out, resid_out, hid_out, gg_out, wgu_out, low_out,
+    g_other, n1_other, low_other,
     x, n1, wq, wkv, wout, raw, wdown, g, wgu, q, kv, keys, vals_t, run_max, run_sum, acc, att_low,
     own, stage_core, got_core, stage_x, got_x, resid, n2, gh, hid, gg,
     load_sem, store_sem, kv_send, kv_recv, core_send, core_recv, x_send, x_recv, ag_send, ag_recv,
+    dp_send, dp_recv,
 ):
     rows, width = x.shape
     quarter = rows // 4
@@ -81,8 +67,12 @@
     core_mate = {"tensor": chip * 2 + 1 - core}
     chip_mate = {"tensor": (1 - chip) * 2 + core}
 
+    mates = [core_mate, chip_mate, *({"context": lax.rem(place + k, 4)} for k in (1, 2, 3))]
+    if swap:
+        side = lax.axis_index("dp")
+        mates.append({"dp": 1 - side})
     barrier = pltpu.get_barrier_semaphore()
-    for mate in (core_mate, chip_mate, *({"context": lax.rem(place + k, 4)} for k in (1, 2, 3))):
+    for mate in mates:
         pl.semaphore_signal(barrier, inc=1, device_id=mate, device_id_type=MESH)
 
     loads = [
@@ -120,7 +110,23 @@
         jnp.where(key_lane, cos_ref[...], 1.0),
         jnp.where(key_lane, sin_ref[...], 0.0),
     ).astype(jnp.bfloat16)
-    pl.semaphore_wait(barrier, 5)
+    pl.semaphore_wait(barrier, len(mates))
+    swaps = []
+
+    def swap_start(src, dst):
+        if swap:
+            i = len(swaps)
+            copy = pltpu.make_async_remote_copy(
+                src_ref=src, dst_ref=dst, send_sem=dp_send.at[i], recv_sem=dp_recv.at[i],
+                device_id={"dp": 1 - side}, device_id_type=MESH,
+            )
+            copy.start()
+            swaps.append(copy)
+
+    if swap:
+        theirs_cols = aligned(1 - side, width // 2)
+        swap_start(g_hbm.at[:, theirs_cols], g_other)
+        swap_start(n1.at[:, theirs_cols], n1_other)
 
     def kv_copy(k):
         return pltpu.make_async_remote_copy(
@@ -216,6 +222,8 @@
         att_low[:, at] = acc[at, :].T.astype(jnp.bfloat16)
 
     store(acc, att_out)
+    store(att_low, low_out)
+    swap_start(att_low, low_other)
     store(run_max, lse_out)
 
     load_wout.wait()
@@ -321,11 +329,11 @@
         x_copy(c).wait_send()
         for i in range(2):
             core_copy(i, c).wait_send()
-    for copy in stores:
+    for copy in (*stores, *swaps):
         copy.wait()
 
 
-def forward(x, segments, cosine, sine, gain_one, gain_two, w_query, w_keyval, w_out, w_gateup, w_down, g):
+def forward(swap, x, segments, cosine, sine, gain_one, gain_two, w_query, w_keyval, w_out, w_gateup, w_down, g):
     rows, width = x.shape
     units = w_down.shape[0]
     heads = w_query.shape[1] // HD
@@ -345,10 +353,14 @@
         ((rows, units), bf16),
         ((rows, 2 * units), bf16),
         ((width, 2 * units), bf16),
+        ((rows, heads * HD), bf16),
+        ((rows, width // 2), bf16),
+        ((rows, width // 2), bf16),
+        ((rows, heads * HD), bf16),
     ]
     dma = pltpu.SemaphoreType.DMA
     return pl.pallas_call(
-        forward_kernel,
+        functools.partial(forward_kernel, swap),
         out_shape=[jax.ShapeDtypeStruct(*out) for out in outs],
         in_specs=[anywhere] + [inside] * 5 + [anywhere] * 6,
         out_specs=[anywhere] * len(outs),
@@ -390,6 +402,8 @@
             dma((chunks,)),
             dma((3,)),
             dma((3,)),
+            dma((3,)),
+            dma((3,)),
         ],
         compiler_params=pltpu.CompilerParams(
             collective_id=0, has_side_effects=True, vmem_limit_bytes=60 * MIB
@@ -398,36 +412,726 @@
     )(x, segments, cosine, sine, gain_one, gain_two, w_query, w_keyval, w_out, w_gateup, w_down, g)
 
 
-def core_swap(array):
-    return lax.ppermute(array, "tensor", [(0, 1), (1, 0), (2, 3), (3, 2)])
-
-
-def chip_swap(array):
-    return lax.ppermute(array, "tensor", [(0, 2), (2, 0), (1, 3), (3, 1)])
+def backward_kernel(names, swap, *refs):
+    r = types.SimpleNamespace(**dict(zip(names, refs, strict=True)))
+    rows, width = r.gb.shape
+    quarter = rows // 4
+    units = r.hid.shape[1]
+    heads_width = r.q.shape[1]
+    f32, bf16 = jnp.float32, jnp.bfloat16
+    tensor = lax.axis_index("tensor")
+    place = lax.axis_index("context")
+    core, chip = lax.rem(tensor, 2), lax.div(tensor, 2)
+    core_mate = {"tensor": chip * 2 + 1 - core}
+    chip_mate = {"tensor": (1 - chip) * 2 + core}
+    mates = [core_mate, chip_mate, *({"context": lax.rem(place + k, 4)} for k in (1, 2, 3))]
+    if swap:
+        side = lax.axis_index("dp")
+        dp_mate = {"dp": 1 - side}
+        mates.append(dp_mate)
+
+    barrier = pltpu.get_barrier_semaphore()
+    for mate in mates:
+        pl.semaphore_signal(barrier, inc=1, device_id=mate, device_id_type=MESH)
+
+    def remote(src, dst, send, recv, mate):
+        return pltpu.make_async_remote_copy(
+            src_ref=src, dst_ref=dst, send_sem=send, recv_sem=recv, device_id=mate,
+            device_id_type=MESH,
+        )
+
+    def tile_gu(n):
+        slot = lax.rem(n, 3)
+        return pltpu.make_async_copy(
+            r.wgu_hbm.at[aligned(n, 256)], r.w_rows.at[slot], r.w_rows_sem.at[slot]
+        )
+
+    def tile_down(n):
+        slot = lax.rem(n, 3)
+        return pltpu.make_async_copy(
+            r.wdown_hbm.at[:, aligned(n, 256)], r.w_cols.at[slot], r.w_cols_sem.at[slot]
+        )
+
+    def tile_qkv(n):
+        slot = lax.rem(n, 3)
+        at = aligned(n, 256)
+        copies = (
+            pltpu.make_async_copy(
+                r.wq_hbm.at[at], r.w_rows.at[slot, :, 0:heads_width], r.w_rows_sem.at[slot]
+            ),
+            pltpu.make_async_copy(
+                r.wkv_hbm.at[at],
+                r.w_rows.at[slot, :, heads_width : heads_width + 128],
+                r.w_cols_sem.at[slot],
+            ),
+        )
+        return types.SimpleNamespace(
+            start=lambda: [copy.start() for copy in copies],
+            wait=lambda: [copy.wait() for copy in copies],
+        )
+
+    mine = aligned(tensor, quarter)
+    loads = {}
+    for name, src, dst in (
+        ("gg", r.gg_hbm, r.gg),
+        ("hid", r.hid_hbm, r.hid),
+        ("resid", r.resid_hbm, r.resid),
+        ("g_own", r.g_hbm.at[mine, :], r.g_own),
+        ("x_own", r.x_hbm.at[mine, :], r.x_own),
+        ("wout", r.wout_hbm, r.wout),
+        ("q", r.q_hbm, r.q),
+        ("kv", r.kv_hbm, r.kv),
+        ("att", r.att_hbm, r.att),
+    ):
+        loads[name] = pltpu.make_async_copy(src, dst, r.load_sem.at[len(loads)])
+    loads["gg"].start()
+    for n in range(3):
+        tile_gu(n).start()
+    loads["hid"].start()
+    for n in range(3):
+        tile_down(n).start()
+    for name in ("resid", "g_own", "x_own", "wout", "q", "kv", "att"):
+        loads[name].start()
+
+    pl.semaphore_wait(barrier, len(mates))
+
+    if swap:
+        half = width // 2
+        theirs_cols = aligned(1 - side, half)
+        mine_cols = aligned(side, half)
+        lead = r.stage.shape[3]
+
+        def swap_copy(i, src, dst):
+            return remote(src, dst, r.dp_send.at[i], r.dp_recv.at[i], dp_mate)
+
+        swap_hid = swap_copy(0, r.hid_hbm, r.hid_o)
+        swap_n2 = swap_copy(1, r.n2_hbm.at[:, theirs_cols], r.n2_o)
+        swap_gg = [
+            swap_copy(2 + i, r.gg_hbm.at[:, i * lead : (i + 1) * lead], r.gg_o.at[i])
+            for i in range(2)
+        ]
+        swap_gb = swap_copy(4, r.gb.at[:, theirs_cols], r.gb_o)
+        swap_gqkv = swap_copy(5, r.gqkv, r.gqkv_o)
+        for copy in (swap_hid, swap_n2, *swap_gg):
+            copy.start()
+
+    chunks = r.own_fin.shape[1]
+    span = r.own_fin.shape[3]
+
+    def core_copy(b, c):
+        return remote(
+            r.stage_core.at[b, c], r.got_core.at[b, c], r.core_send.at[b, c],
+            r.core_recv.at[b, c], core_mate,
+        )
+
+    def x_copy(b, c):
+        return remote(
+            r.stage_x.at[b, c], r.got_x.at[b, c], r.x_send.at[b, c], r.x_recv.at[b, c], chip_mate
+        )
+
+    def start_sum(b, tile, product, send):
+        routes = (
+            ((1 - chip) * 2 + 1 - core, lambda c, at, v: put(r.stage_core, (b, c, 0), at, v)),
+            (chip * 2 + 1 - core, lambda c, at, v: put(r.stage_core, (b, c, 1), at, v)),
+            ((1 - chip) * 2 + core, lambda c, at, v: put(r.own_fwd, (c,), at, v)),
+            (chip * 2 + core, lambda c, at, v: put(r.own_fin, (b, c), at, v)),
+        )
+
+        def put(ref, index, at, value):
+            ref[(*index, slice(None), at)] = value.astype(ref.dtype)
+
+        def forward_chunk(c):
+            core_copy(b, c).wait_recv()
+            r.stage_x[b, c] = (r.own_fwd[c] + r.got_core[b, c, 0].astype(f32)).astype(bf16)
+            if send:
+                x_copy(b, c).start()
+
+        @pl.loop(0, chunks)
+        def _(c):
+            for t in range(span // 256):
+                n = c * (span // 256) + t
+                tile(n).wait()
+                r.tmp[...] = product(lax.rem(n, 3))
+                for owner, route in routes:
+                    route(c, slice(t * 256, t * 256 + 256), r.tmp[aligned(owner, quarter), :])
+
+                @pl.when(n + 3 < width // 256)
+                def _():
+                    tile(n + 3).start()
+
+            core_copy(b, c).start()
+            pl.when(c > 0)(lambda: forward_chunk(c - 1))
+
+        forward_chunk(chunks - 1)
+
+    def finish_sum(b):
+        for c in range(chunks):
+            x_copy(b, c).wait_recv()
+            r.own_fin[b, c] = (
+                r.own_fin[b, c] + r.got_core[b, c, 1].astype(f32) + r.got_x[b, c].astype(f32)
+            )
+        for c in range(chunks):
+            core_copy(b, c).wait_send()
+            x_copy(b, c).wait_send()
+
+    def back_through_norm(b, values, gain_ref, gain_row, emit):
+        square = jnp.zeros((quarter, 1), f32)
+        inner = jnp.zeros((quarter, 1), f32)
+        for c in range(chunks):
+            at = slice(c * span, (c + 1) * span)
+            v = values[:, at].astype(f32)
+            square = square + jnp.sum(v * v, -1, keepdims=True)
+            inner = inner + jnp.sum(r.own_fin[b, c] * gain_ref[:, at] * v, -1, keepdims=True)
+        inverse = lax.rsqrt(square / width + epsilon)
+        slope = inner / width * (inverse * inverse * inverse)
+        for c in range(chunks):
+            at = slice(c * span, (c + 1) * span)
+            v = values[:, at].astype(f32)
+            dn = r.own_fin[b, c]
+            r.gain_sum[0, gain_row : gain_row + 1, at] = jnp.sum(dn * v * inverse, 0, keepdims=True)
+            emit(at, inverse * dn * gain_ref[:, at] - v * slope)
+
+    def gather(i, src, dst):
+        def copy(slot, src, owner, mate):
+            return remote(
+                src, dst.at[aligned(owner, quarter), :], r.ag_send.at[i, slot],
+                r.ag_recv.at[i, slot], mate,
+            )
+
+        other = chip_mate["tensor"]
+        return (
+            copy(0, src, tensor, chip_mate),
+            copy(1, src, tensor, core_mate),
+            copy(2, dst.at[aligned(other, quarter), :], other, core_mate),
+        )
+
+    if swap:
+        is_end = (place == 0) | (place == 3)
+        is_mid = jnp.logical_not(is_end)
+        beside = place + 1 - 2 * lax.rem(place, 2)
+        low_side = place < 2
+        io_mate, across_mate = {"context": beside}, {"context": 3 - place}
+        plan = (
+            (r.g_hbm.at[:, mine_cols], r.go_hbm, r.hid, r.hid_o, units, r.dwdown_out),
+            (r.n2_hbm.at[:, mine_cols], r.n2_o, r.gg.at[:, 0:lead], r.gg_o.at[0], lead,
+             r.dgu_out.at[:, 0:lead]),
+            (None, None, r.gg.at[:, lead : 2 * lead], r.gg_o.at[1], lead,
+             r.dgu_out.at[:, lead : 2 * lead]),
+            (r.gb.at[:, mine_cols], r.gb_o, r.att_low, r.att_o, heads_width, r.dwout_out),
+            (r.n1_hbm.at[:, mine_cols], r.n1o_hbm, r.gqkv, r.gqkv_o, r.gqkv.shape[1],
+             r.dwqkv_out),
+        )
+
+        def cut_loads(u):
+            own, other = plan[u][:2]
+            return (
+                pltpu.make_async_copy(own, r.cut.at[0:rows], r.cut_sem.at[0]),
+                pltpu.make_async_copy(other, r.cut.at[rows : 2 * rows], r.cut_sem.at[1]),
+            )
+
+        def piece(ref, s, j, u):
+            return ref.at[s, j, :, 0 : plan[u][4]]
+
+        def line_copy(u, j, slot, mate):
+            s = u % 2
+            return remote(
+                piece(r.stage, s, j, u), piece(r.got, s, slot, u), r.line_send.at[s, j],
+                r.line_recv.at[s, slot], mate,
+            )
+
+        def result(u):
+            return pltpu.make_async_copy(
+                r.sums.at[u % 2, :, 0 : plan[u][4]], plan[u][5], r.sums_sem.at[u % 2]
+            )
+
+        def prepare(u, load_next):
+            s = u % 2
+            own, other, width_u = plan[u][2], plan[u][3], plan[u][4]
+            if u >= 2:
+                for j in range(3):
+                    line_copy(u - 2, j, 0, io_mate).wait_send()
+                result(u - 2).wait()
+                pl.when(is_end)(lambda: pl.semaphore_wait(r.io_credit, 1))
+            if plan[u][0] is not None:
+                for copy in cut_loads(u):
+                    copy.wait()
+
+            @pl.loop(0, 4)
+            def _(j):
+                chunk = jnp.where(
+                    j == 0,
+                    jnp.where(low_side, 3, 0),
+                    jnp.where(
+                        j == 1, jnp.where(low_side, 2, 1), jnp.where(j == 2, beside, place)
+                    ),
+                )
+                r.turned[...] = r.cut[:, aligned(chunk, 256)].astype(f32).T.astype(bf16)
+
+                def block(at):
+                    term = dot(r.turned[:, 0:rows], own[:, at]) + dot(
+                        r.turned[:, rows : 2 * rows], other[:, at]
+                    )
+
+                    @pl.when(j < 3)
+                    def _():
+                        r.stage[s, j, :, at] = term.astype(bf16)
+
+                    @pl.when(j == 3)
+                    def _():
+                        r.sums[s, :, at] = term
+
+                @pl.loop(0, width_u // 256)
+                def _(tile):
+                    block(aligned(tile, 256))
+
+                if width_u % 256:
+                    block(slice(width_u - width_u % 256, width_u))
+
+                @pl.when((j < 3) & is_end)
+                def _():
+                    line_copy(u, j, j, io_mate).start()
+
+            if load_next is not None:
+                for copy in cut_loads(load_next):
+                    copy.start()
+
+        def add_in(u, j, slot):
+            width_u, s = plan[u][4], u % 2
+            line_copy(u, 0, slot, io_mate).wait_recv()
+
+            @pl.loop(0, 4)
+            def _(i):
+                at = aligned(i, 64)
+                total = r.stage[s, j, at, 0:width_u].astype(f32)
+                total = total + r.got[s, slot, at, 0:width_u].astype(f32)
+                r.stage[s, j, at, 0:width_u] = total.astype(bf16)
+
+        def pass_on(u, step):
+            @pl.when(is_mid)
+            def _():
+                if step < 2:
+                    add_in(u, step, step)
+                    if u >= 2 and step == 0:
+                        pl.semaphore_wait(r.across_credit, 1)
+                    line_copy(u, step, 3 + step, across_mate).start()
+                else:
+                    add_in(u, 2, 3)
+                    if u >= 2:
+                        pl.semaphore_wait(r.io_credit, 1)
+                    line_copy(u, 2, 0, io_mate).start()
+
+        def complete(u):
+            width_u, s = plan[u][4], u % 2
+
+            def take(slots):
+                for slot in slots:
+                    line_copy(u, 0, slot, io_mate).wait_recv()
+
+                @pl.loop(0, 4)
+                def _(i):
+                    at = aligned(i, 64)
+                    total = r.sums[s, at, 0:width_u]
+                    for slot in slots:
+                        total = total + r.got[s, slot, at, 0:width_u].astype(f32)
+                    r.sums[s, at, 0:width_u] = total
+
+            @pl.when(is_end)
+            def _():
+                take((0,))
+
+            @pl.when(is_mid)
+            def _():
+                take((2, 4))
+
+            result(u).start()
+            if u + 2 < len(plan):
+                pl.semaphore_signal(r.io_credit, inc=1, device_id=io_mate, device_id_type=MESH)
+
+                @pl.when(is_mid)
+                def _():
+                    pl.semaphore_signal(
+                        r.across_credit, inc=1, device_id=across_mate, device_id_type=MESH
+                    )
+
+        late = (
+            pltpu.make_async_copy(r.attlow_hbm, r.att_low, r.late_sem.at[0]),
+            pltpu.make_async_copy(r.atto_hbm, r.att_o, r.late_sem.at[1]),
+        )
+        for copy in (*cut_loads(0), *late):
+            copy.start()
+
+    r.gain_sum[...] = jnp.zeros_like(r.gain_sum)
+
+    loads["gg"].wait()
+    start_sum(0, tile_gu, lambda slot: dot_t(r.gg[...], r.w_rows[slot]), True)
+    loads["hid"].wait()
+    start_sum(1, tile_down, lambda slot: dot(r.hid[...], r.w_cols[slot]), False)
+    for n in range(3):
+        tile_qkv(n).start()
+    finish_sum(0)
+    loads["resid"].wait()
+    loads["g_own"].wait()
+
+    def keep_resid(at, grad):
+        total = r.g_own[:, at].astype(f32) + grad
+        r.grad_resid[:, at] = total
+        r.gb[mine, at] = total.astype(bf16)
+
+    back_through_norm(0, r.resid, r.gain_two, 1, keep_resid)
+    gb_chip, gb_core, gb_onward = gather(0, r.gb.at[mine, :], r.gb)
+    gb_chip.start()
+    gb_core.start()
+    for c in range(chunks):
+        x_copy(1, c).start()
+    gb_chip.wait_recv()
+    gb_onward.start()
+    if swap:
+        swap_hid.wait_recv()
+        prepare(0, None)
+        swap_n2.wait_recv()
+        for copy in cut_loads(1):
+            copy.start()
+    gb_core.wait_recv()
+    gb_onward.wait_recv()
+    if swap:
+        swap_gb.start()
+    else:
+        pltpu.make_async_copy(r.gb, r.gb_out, r.cut_sem.at[0]).start()
+
+    loads["wout"].wait()
+    for i in range(heads_width // 256):
+        at = slice(i * 256, i * 256 + 256)
+        r.ga[:, at] = dot_t(r.gb[...], r.wout[at, :]).astype(bf16)
+    loads["att"].wait()
+
+    @pl.loop(0, heads_width // 128)
+    def _(pair):
+        at = aligned(pair, 128)
+        product = r.ga[:, at].astype(f32).T * r.att[at, :]
+        for e in range(2):
+            r.delta[pair * 2 + e] = jnp.sum(product[64 * e : 64 * e + 64], 0, keepdims=True)
+
+    loads["q"].wait()
+    loads["kv"].wait()
+    r.dq[...] = jnp.zeros_like(r.dq)
+    key_lane = lanes((rows, 128)) < 64
+
+    def back_block(k, first):
+        block = r.kv[k].astype(f32)
+        rolled = pltpu.roll(block, 64, 1)
+        r.keys[0] = jnp.where(key_lane, block, 0.0).astype(bf16)
+        r.keys[1] = jnp.where(key_lane, 0.0, rolled).astype(bf16)
+        r.vals[0] = jnp.where(key_lane, rolled, 0.0).astype(bf16)
+        r.vals[1] = jnp.where(key_lane, 0.0, block).astype(bf16)
+        r.keys_t[...] = block.T[:64].astype(bf16)
+        r.dk[...] = jnp.zeros_like(r.dk)
+        r.dv[...] = jnp.zeros_like(r.dv)
+
+        @pl.loop(0, heads_width // 128)
+        def _(pair):
+            pair_q = r.q[:, aligned(pair, 128)]
+            pair_ga = r.ga[:, aligned(pair, 128)]
+            for e in range(2):
+                head = pair * 2 + e
+                scores = dot_t(r.keys[e], pair_q)
+                key_index = (place - k) * rows + lax.broadcasted_iota(jnp.int32, (rows, rows), 0)
+                allowed = key_index >= r.seg[...]
+                if first:
+                    query_index = place * rows + lax.broadcasted_iota(jnp.int32, (rows, rows), 1)
+                    allowed = allowed & (key_index <= query_index)
+                probs = jnp.where(allowed, jnp.exp(scores - r.lse[head]), 0.0)
+                grad_probs = dot_t(r.vals[e], pair_ga)
+                grad_scores = (probs * (grad_probs - r.delta[head])).astype(bf16)
+                r.dv[e] += dot(probs.astype(bf16), pair_ga)
+                r.dk[e] += dot(grad_scores, pair_q)
+                r.dq[aligned(head, 64), :] += dot(r.keys_t[...], grad_scores)
+
+        return jnp.where(
+            key_lane,
+            r.dk[0] + pltpu.roll(r.dk[1], 64, 1),
+            r.dv[1] + pltpu.roll(r.dv[0], 64, 1),
+        )
+
+    def dkv_copy(k, mate):
+        return remote(
+            r.stage_kv.at[k], r.got_kv.at[k], r.kv_send.at[k], r.kv_recv.at[k], {"context": mate}
+        )
+
+    @pl.loop(0, place)
+    def _(i):
+        k = place - i
+        r.stage_kv[k] = back_block(k, False).astype(bf16)
+        dkv_copy(k, i).start()
+
+    r.dkv[...] = back_block(0, True)
+    if swap:
+        pass_on(0, 0)
+
+    @pl.loop(0, heads_width // 128)
+    def _(pair):
+        at = aligned(pair, 128)
+        turned = turn(r.dq[at, :].T * 0.125, r.cos[...], -r.sin[...])
+        r.gqkv[:, at] = turned.astype(bf16)
+
+    for k in (1, 2, 3):
+
+        @pl.when(place + k < 4)
+        def _():
+            dkv_copy(k, 0).wait_recv()
+            r.dkv[...] += r.got_kv[k].astype(f32)
+
+    r.gqkv[:, heads_width : heads_width + 128] = turn(
+        r.dkv[...], jnp.where(key_lane, r.cos[...], 1.0), jnp.where(key_lane, -r.sin[...], 0.0)
+    ).astype(bf16)
+    if swap:
+        swap_gqkv.start()
+    else:
+        pltpu.make_async_copy(r.gqkv, r.gqkv_out, r.cut_sem.at[1]).start()
+
+    start_sum(
+        0, tile_qkv,
+        lambda slot: dot_t(r.gqkv[...], r.w_rows[slot, :, 0 : r.gqkv.shape[1]]), True,
+    )
+
+    finish_sum(1)
+    for c in range(chunks):
+        at = slice(c * span, (c + 1) * span)
+        r.mixed_own[:, at] = (r.resid[:, at] + r.own_fin[1, c]).astype(bf16)
+    mixed_chip, mixed_core, mixed_onward = gather(1, r.mixed_own, r.mixed_out)
+    mixed_store = pltpu.make_async_copy(r.mixed_own, r.mixed_out.at[mine, :], r.out_sem.at[0])
+    for copy in (mixed_chip, mixed_core, mixed_store):
+        copy.start()
+    if swap:
+        pass_on(0, 1)
+        pass_on(0, 2)
+
+    finish_sum(0)
+    loads["x_own"].wait()
+
+    def keep_tokens(at, grad):
+        r.tokens_own[:, at] = (r.grad_resid[:, at] + grad).astype(bf16)
+
+    back_through_norm(0, r.x_own, r.gain_one, 0, keep_tokens)
+    tokens_chip, tokens_core, tokens_onward = gather(2, r.tokens_own, r.tokens_out)
+    tokens_store = pltpu.make_async_copy(r.tokens_own, r.tokens_out.at[mine, :], r.out_sem.at[1])
+    for copy in (tokens_chip, tokens_core, tokens_store):
+        copy.start()
+
+    for i, mate in enumerate((core_mate, chip_mate)):
+        copy = remote(
+            r.gain_sum.at[i], r.gain_got.at[i], r.gain_send.at[i], r.gain_recv.at[i], mate
+        )
+        copy.start()
+        copy.wait()
+        r.gain_sum[i + 1] = r.gain_sum[i] + r.gain_got[i]
+    if swap:
+        copy = remote(
+            r.gain_sum.at[2, :, theirs_cols], r.gain_half.at[0], r.gain_send.at[2],
+            r.gain_recv.at[2], dp_mate,
+        )
+        copy.start()
+        copy.wait()
+        r.gain_half[1] = r.gain_sum[2, :, mine_cols] + r.gain_half[0]
+        part = half // 4
+        pieces = [
+            remote(
+                r.gain_half.at[1, :, aligned(lax.rem(place + k, 4), part)], r.gain_piece.at[k],
+                r.gain_send.at[2 + k], r.gain_recv.at[2 + k], {"context": lax.rem(place + k, 4)},
+            )
+            for k in (1, 2, 3)
+        ]
+        for copy in pieces:
+            copy.start()
+        for copy in pieces:
+            copy.wait()
+        r.gains_out[...] = (
+            r.gain_half[1, :, aligned(place, part)]
+            + r.gain_piece[1]
+            + r.gain_piece[2]
+            + r.gain_piece[3]
+        )
+    else:
+        r.gains_out[...] = r.gain_sum[2]
+
+    if swap:
+        complete(0)
+        swap_gg[0].wait_recv()
+        prepare(1, None)
+    mixed_chip.wait_recv()
+    mixed_onward.start()
+    tokens_chip.wait_recv()
+    tokens_onward.start()
+    if swap:
+        pass_on(1, 0)
+        swap_gg[1].wait_recv()
+        swap_gb.wait_recv()
+        prepare(2, 3)
+        pass_on(1, 1)
+        pass_on(1, 2)
+        complete(1)
+        for copy in late:
+            copy.wait()
+        prepare(3, 4)
+        pass_on(2, 0)
+        pass_on(2, 1)
+        pass_on(2, 2)
+        complete(2)
+        swap_gqkv.wait_recv()
+        prepare(4, None)
+        for u in (3, 4):
+            for step in range(3):
+                pass_on(u, step)
+            complete(u)
+
+    for copy in (mixed_core, mixed_onward, tokens_core, tokens_onward):
+        copy.wait_recv()
+    for copy in (
+        gb_chip, gb_core, gb_onward, mixed_chip, mixed_core, mixed_onward, tokens_chip,
+        tokens_core, tokens_onward,
+    ):
+        copy.wait_send()
+    mixed_store.wait()
+    tokens_store.wait()
+    for k in (1, 2, 3):
+        pl.when(place >= k)(dkv_copy(k, 0).wait_send)
+    if swap:
+        for copy in (swap_hid, swap_n2, *swap_gg, swap_gb, swap_gqkv):
+            copy.wait_send()
+        for u in (3, 4):
+            for j in range(3):
+                line_copy(u, j, 0, io_mate).wait_send()
+            result(u).wait()
+    else:
+        pltpu.make_async_copy(r.gb, r.gb_out, r.cut_sem.at[0]).wait()
+        pltpu.make_async_copy(r.gqkv, r.gqkv_out, r.cut_sem.at[1]).wait()
+
+
+def backward(swap, inputs, rows, width, units, heads):
+    bf16, f32 = jnp.bfloat16, jnp.float32
+    quarter = rows // 4
+    chunks = 4
+    span = width // chunks
+    wide = heads * HD
+    qkv = wide + 2 * HD
+    outs = {
+        "mixed_out": ((rows, width), bf16),
+        "tokens_out": ((rows, width), bf16),
+        "gains_out": ((8, width // 8 if swap else width), f32),
+    }
+    if swap:
+        outs |= {
+            "dwdown_out": ((width // 8, units), f32),
+            "dgu_out": ((width // 8, 2 * units), f32),
+            "dwout_out": ((width // 8, wide), f32),
+            "dwqkv_out": ((width // 8, qkv), f32),
+            "n2_o": ((rows, width // 2), bf16),
+            "gb_o": ((rows, width // 2), bf16),
+        }
+    else:
+        outs |= {"gb_out": ((rows, width), bf16), "gqkv_out": ((rows, qkv), bf16)}
+    scratch = {
+        "gg": ((rows, 2 * units), bf16),
+        "hid": ((rows, units), bf16),
+        "resid": ((quarter, width), f32),
+        "g_own": ((quarter, width), bf16),
+        "x_own": ((quarter, width), bf16),
+        "wout": ((wide, width), bf16),
+        "q": ((rows, wide), bf16),
+        "kv": ((4, rows, 2 * HD), bf16),
+        "att": ((wide, rows), f32),
+        "w_rows": ((3, 256, 2 * units), bf16),
+        "w_cols": ((3, units, 256), bf16),
+        "tmp": ((rows, 256), f32),
+        "stage_core": ((2, chunks, 2, quarter, span), bf16),
+        "got_core": ((2, chunks, 2, quarter, span), bf16),
+        "own_fwd": ((chunks, quarter, span), f32),
+        "own_fin": ((2, chunks, quarter, span), f32),
+        "stage_x": ((2, chunks, quarter, span), bf16),
+        "got_x": ((2, chunks, quarter, span), bf16),
+        "grad_resid": ((quarter, width), f32),
+        "gb": ((rows, width), bf16),
+        "ga": ((rows, wide), bf16),
+        "mixed_own": ((quarter, width), bf16),
+        "tokens_own": ((quarter, width), bf16),
+        "delta": ((heads, 1, rows), f32),
+        "dq": ((wide, rows), f32),
+        "keys": ((2, rows, 2 * HD), bf16),
+        "vals": ((2, rows, 2 * HD), bf16),
+        "keys_t": ((HD, rows), bf16),
+        "dk": ((2, rows, 2 * HD), f32),
+        "dv": ((2, rows, 2 * HD), f32),
+        "dkv": ((rows, 2 * HD), f32),
+        "stage_kv": ((4, rows, 2 * HD), bf16),
+        "got_kv": ((4, rows, 2 * HD), bf16),
+        "gqkv": ((rows, qkv), bf16),
+        "gain_sum": ((3, 8, width), f32),
+        "gain_got": ((2, 8, width), f32),
+    }
+    if swap:
+        scratch |= {
+            "hid_o": ((rows, units), bf16),
+            "gg_o": ((2, rows, units), bf16),
+            "gqkv_o": ((rows, qkv), bf16),
+            "att_low": ((rows, wide), bf16),
+            "att_o": ((rows, wide), bf16),
+            "cut": ((2 * rows, width // 2), bf16),
+            "turned": ((256, 2 * rows), bf16),
+            "stage": ((2, 3, width // 8, units), bf16),
+            "got": ((2, 5, width // 8, units), bf16),
+            "sums": ((2, width // 8, units), f32),
+            "gain_half": ((2, 8, width // 2), f32),
+            "gain_piece": ((4, 8, width // 8), f32),
+        }
+    sems = {
+        "load_sem": (9,),
+        "w_rows_sem": (3,),
+        "w_cols_sem": (3,),
+        "core_send": (2, chunks),
+        "core_recv": (2, chunks),
+        "x_send": (2, chunks),
+        "x_recv": (2, chunks),
+        "ag_send": (3, 3),
+        "ag_recv": (3, 3),
+        "kv_send": (4,),
+        "kv_recv": (4,),
+        "gain_send": (6,),
+        "gain_recv": (6,),
+        "out_sem": (2,),
+        "cut_sem": (2,),
+    }
+    if swap:
+        sems |= {
+            "dp_send": (6,),
+            "dp_recv": (6,),
+            "line_send": (2, 3),
+            "line_recv": (2, 5),
+            "sums_sem": (2,),
+            "late_sem": (2,),
+        }
+    credits = ["io_credit", "across_credit"] if swap else []
+    names = [*inputs, *outs, *scratch, *sems, *credits]
+    anywhere = pl.BlockSpec(memory_space=pl.ANY)
+    inside = pl.BlockSpec(memory_space=pltpu.VMEM)
+    results = pl.pallas_call(
+        functools.partial(backward_kernel, names, swap),
+        out_shape=[jax.ShapeDtypeStruct(*out) for out in outs.values()],
+        in_specs=[anywhere if name.endswith("_hbm") else inside for name in inputs],
+        out_specs=[inside if name == "gains_out" else anywhere for name in outs],
+        scratch_shapes=[
+            *(pltpu.VMEM(*shape) for shape in scratch.values()),
+            *(pltpu.SemaphoreType.DMA(shape) for shape in sems.values()),
+            *(pltpu.SemaphoreType.REGULAR for _ in credits),
+        ],
+        compiler_params=pltpu.CompilerParams(
+            collective_id=1, has_side_effects=True, vmem_limit_bytes=63 * MIB
+        ),
+        name="backward",
+    )(*inputs.values())
+    return dict(zip(outs, results, strict=True))
 
 
 def pick(array, index, axis):
     return lax.dynamic_index_in_dim(array, index, axis, keepdims=False)
-
-
-def sum_scatter(part):
-    core, chip = lax.axis_index("tensor") % 2, lax.axis_index("tensor") // 2
-    rows, width = part.shape
-    quarters = part.reshape(2, 2, rows // 4, width)
-    got = core_swap(pick(quarters, 1 - core, 1).astype(jnp.bfloat16))
-    pair = pick(quarters, core, 1) + got.astype(jnp.float32)
-    got = chip_swap(pick(pair, 1 - chip, 0).astype(jnp.bfloat16))
-    return pick(pair, chip, 0) + got.astype(jnp.float32)
-
-
-def gather_rows(quarter):
-    core, chip = lax.axis_index("tensor") % 2, lax.axis_index("tensor") // 2
-    rows, width = quarter.shape
-    other = chip_swap(quarter)
-    pair = jnp.where(chip == 0, jnp.stack([quarter, other]), jnp.stack([other, quarter]))
-    other = core_swap(pair)
-    whole = jnp.where(core == 0, jnp.stack([pair, other], 1), jnp.stack([other, pair], 1))
-    return whole.reshape(4 * rows, width)
 
 
 def line_sum(part):
@@ -456,27 +1160,10 @@
     )
 
 
-def weight_grad(left, right, split_left):
-    parts_dp = lax.axis_size("dp")
-    index = lax.axis_index("dp")
-    cut, kept = (left, right) if split_left else (right, left)
-    if parts_dp == 2:
-        halves = cut.reshape(cut.shape[0], 2, cut.shape[1] // 2)
-        swap = [(0, 1), (1, 0)]
-        cut_rows = jnp.concatenate(
-            [pick(halves, index, 1), lax.ppermute(pick(halves, 1 - index, 1), "dp", swap)]
-        )
-        kept_rows = jnp.concatenate([kept, lax.ppermute(kept, "dp", swap)])
-        step = cut_rows.shape[1] // 4
-
-        def part(chunk):
-            columns = lax.dynamic_slice_in_dim(cut_rows, chunk * step, step, 1)
-            pair = (columns, kept_rows) if split_left else (kept_rows, columns)
-            return jnp.einsum("ta,tb->ab", *pair, preferred_element_type=jnp.float32)
-
-        return line_sum(part)
-    whole = jnp.einsum("ta,tb->ab", left, right, preferred_element_type=jnp.float32)
-    axis = 0 if split_left else 1
+def weight_grad(left, right, axis):
+    whole = lax.dot_general(
+        left, right, (((0,), (0,)), ((), ())), preferred_element_type=jnp.float32
+    )
     mine = lax.psum_scatter(
         whole.astype(jnp.bfloat16), "dp", scatter_dimension=axis, tiled=True
     )
@@ -486,12 +1173,6 @@
     )
 
 
-def gain_grad(partial):
-    partial = partial + core_swap(partial)
-    partial = partial + chip_swap(partial)
-    return lax.psum_scatter(partial, ("dp", "context"), scatter_dimension=1, tiled=True)
-
-
 def tables(positions):
     cosine, sine = angles(positions, HD)
     return jnp.concatenate([cosine] * 4, 1), jnp.concatenate([-sine, sine] * 2, 1)
@@ -501,99 +1182,53 @@
     tokens, segments, gain_one, w_query, w_keyval, w_out, gain_two, w_gateup, w_down, cotangent
 ):
     num_seqs, tok_count, model_width = tokens.shape
-    head_dim = HD
     heads_kv = w_keyval.shape[1]
-    heads = w_query.shape[1] // head_dim
+    width_q = w_query.shape[1]
     units = w_down.shape[0]
-    place = lax.axis_index("context")
-    tensor = lax.axis_index("tensor")
-    quarter = tok_count // 4
-
-    def own_rows(array):
-        return lax.dynamic_slice_in_dim(array, tensor * quarter, quarter, 0)
-
-    tokens_flat = tokens.reshape(tok_count, model_width)
-    grad_out = cotangent.reshape(tok_count, model_width)
-    query_index = place * tok_count + jnp.arange(tok_count, dtype=jnp.int32)
+    swap = lax.axis_size("dp") == 2
+    x = tokens.reshape(tok_count, model_width)
+    g = cotangent.reshape(tok_count, model_width)
+    query_index = lax.axis_index("context") * tok_count + jnp.arange(tok_count, dtype=jnp.int32)
     cosine, sine = tables(query_index - segments[0])
-    w_kv = w_keyval.reshape(model_width, 2 * head_dim)
+    w_kv = w_keyval.reshape(model_width, 2 * HD)
+    one, two = gain_one[None], gain_two[None]
     (
-        rot_q, kv, attended_t, log_total, normed_one, normed_two, resid, hidden, grad_gateup, w_gu
+        queries, kv, attended, log_total, normed_one, normed_two, resid, hidden, grad_gateup, w_gu,
+        attended_low, g_other, normed_one_other, attended_other,
     ) = forward(
-        tokens_flat, segments, cosine, sine, gain_one[None], gain_two[None], w_query, w_kv, w_out,
-        w_gateup, w_down, grad_out,
+        swap, x, segments, cosine, sine, one, two, w_query, w_kv, w_out, w_gateup, w_down, g
     )
-    inverse_two = lax.rsqrt(jnp.mean(resid * resid, -1, keepdims=True) + epsilon)
-    grad_normed_two = sum_scatter(
-        jnp.einsum("rf,df->rd", grad_gateup, w_gu, preferred_element_type=jnp.float32)
-    )
-    grad_resid_norm, gain_two_part = norm_back(resid, inverse_two, gain_two, grad_normed_two)
-    grad_resid = own_rows(grad_out).astype(jnp.float32) + grad_resid_norm
-    grad_branch = gather_rows(grad_resid.astype(jnp.bfloat16))
-    down_part = jnp.dot(hidden, w_down, preferred_element_type=jnp.float32)
-    mixed = gather_rows((resid + sum_scatter(down_part)).astype(jnp.bfloat16))
-    sent_wdown = weight_grad(hidden, grad_out, False)
-    sent_gateup = weight_grad(normed_two, grad_gateup, True)
-    attended = attended_t.T
-    sent_wout = weight_grad(attended.astype(jnp.bfloat16), grad_branch, False)
-    grad_attended = jnp.einsum(
-        "rd,ad->ra", grad_branch, w_out, preferred_element_type=jnp.float32
-    ).astype(jnp.bfloat16)
-    delta = jnp.sum(
-        (grad_attended.astype(jnp.float32) * attended).reshape(tok_count, heads, head_dim), -1
-    ).T
-    queries = rot_q.reshape(tok_count, heads, head_dim)
-    grad_heads = grad_attended.reshape(tok_count, heads, head_dim)
-    grad_rot_q = jnp.zeros((tok_count, heads, head_dim), jnp.float32)
-    grad_blocks = []
-    for back in range(4):
-        keys, values = kv[back][:, :head_dim], kv[back][:, head_dim:]
-        index = (place - back) * tok_count + jnp.arange(tok_count, dtype=jnp.int32)
-        allowed = (index[None, :] <= query_index[:, None]) & (
-            index[None, :] >= segments[0][:, None]
-        )
-        raw = jnp.einsum("qhd,pd->hqp", queries, keys, preferred_element_type=jnp.float32)
-        probs = jnp.where(allowed, jnp.exp(jnp.where(allowed, raw, neg_large) - log_total.reshape(heads, tok_count, 1)), 0.0)
-        grad_probs = jnp.einsum("qhd,pd->hqp", grad_heads, values, preferred_element_type=jnp.float32)
-        grad_raw = (probs * (grad_probs - delta[..., None])).astype(jnp.bfloat16)
-        grad_raw = jnp.where(allowed, grad_raw, 0)
-        grad_rot_q = grad_rot_q + 0.125 * jnp.einsum("hqp,pd->qhd", grad_raw, keys, preferred_element_type=jnp.float32)
-        grad_key = jnp.einsum("hqp,qhd->pd", grad_raw, queries, preferred_element_type=jnp.float32)
-        grad_value = jnp.einsum("hqp,qhd->pd", probs.astype(jnp.bfloat16), grad_heads, preferred_element_type=jnp.float32)
-        grad_blocks.append(jnp.concatenate([grad_key, grad_value], -1))
-    grad_kv = grad_blocks[0]
-    for back in range(1, 4):
-        grad_kv = grad_kv + lax.ppermute(
-            grad_blocks[back].astype(jnp.bfloat16),
-            "context",
-            [(i + back, i) for i in range(4 - back)],
-        ).astype(jnp.float32)
-    cos, sin = angles(query_index - segments[0], head_dim)
-    grad_queries = (
-        rotate(grad_rot_q, cos[:, None, :], -sin[:, None, :]).reshape(tok_count, -1).astype(jnp.bfloat16)
-    )
-    grad_keyval = jnp.concatenate(
-        [rotate(grad_kv[..., :head_dim], cos, -sin), grad_kv[..., head_dim:]], -1
-    ).astype(jnp.bfloat16)
-    grad_normed_part = jnp.einsum(
-        "re,de->rd", grad_queries, w_query, preferred_element_type=jnp.float32
-    ) + jnp.einsum("re,de->rd", grad_keyval, w_kv, preferred_element_type=jnp.float32)
-    sent_wqkv = weight_grad(
-        normed_one, jnp.concatenate([grad_queries, grad_keyval], 1), True
-    )
-    grad_normed_one = sum_scatter(grad_normed_part)
-    x_own = own_rows(tokens_flat).astype(jnp.float32)
-    inverse_one = lax.rsqrt(jnp.mean(x_own * x_own, -1, keepdims=True) + epsilon)
-    grad_x_norm, gain_one_part = norm_back(x_own, inverse_one, gain_one, grad_normed_one)
-    grad_tokens = gather_rows((grad_resid + grad_x_norm).astype(jnp.bfloat16))
-    gains = gain_grad(jnp.stack([gain_one_part, gain_two_part]))
-    width_q = w_query.shape[1]
+    inputs = {
+        "seg": segments, "cos": cosine, "sin": sine, "gain_one": one, "gain_two": two,
+        "lse": log_total, "q_hbm": queries, "kv_hbm": kv, "att_hbm": attended,
+        "resid_hbm": resid, "hid_hbm": hidden, "gg_hbm": grad_gateup, "wgu_hbm": w_gu,
+        "wdown_hbm": w_down, "wout_hbm": w_out, "wq_hbm": w_query, "wkv_hbm": w_kv, "x_hbm": x,
+        "g_hbm": g,
+    }
+    if swap:
+        inputs |= {
+            "n1_hbm": normed_one, "n2_hbm": normed_two, "attlow_hbm": attended_low,
+            "go_hbm": g_other, "n1o_hbm": normed_one_other, "atto_hbm": attended_other,
+        }
+    out = backward(swap, inputs, tok_count, model_width, units, width_q // HD)
+    if swap:
+        gains = out["gains_out"]
+        sent_wdown, sent_wout = out["dwdown_out"].T, out["dwout_out"].T
+        sent_gateup, sent_wqkv = out["dgu_out"], out["dwqkv_out"]
+    else:
+        gains = lax.psum_scatter(
+            out["gains_out"], ("dp", "context"), scatter_dimension=1, tiled=True
+        )
+        sent_wdown = weight_grad(hidden, g, 1)
+        sent_gateup = weight_grad(normed_two, grad_gateup, 0)
+        sent_wout = weight_grad(attended_low, out["gb_out"], 1)
+        sent_wqkv = weight_grad(normed_one, out["gqkv_out"], 0)
     return (
-        mixed.reshape(num_seqs, tok_count, model_width),
-        grad_tokens.astype(jnp.float32).reshape(num_seqs, tok_count, model_width),
+        out["mixed_out"].reshape(tokens.shape),
+        out["tokens_out"].astype(jnp.float32).reshape(tokens.shape),
         gains[0],
         sent_wqkv[:, :width_q],
-        sent_wqkv[:, width_q:].reshape(-1, heads_kv, 2 * head_dim),
+        sent_wqkv[:, width_q:].reshape(-1, heads_kv, 2 * HD),
         sent_wout,
         gains[1],
         sent_gateup.reshape(-1, units // 128, 2, 128).transpose(0, 2, 1, 3).reshape(-1, 2, units),

time: 671 us -> 404 us (0.60)
  Pallas kernels: 72.1 us -> 372 us
  waiting for transfers between devices: 155 us -> 0 us
  matrix products: 136 us -> 0 us
  starting transfers between devices: 130 us -> 0 us
  local copies, waits for them, and re-layouts: 113 us -> 22.6 us
  other arithmetic: 37.5 us -> 5.5 us
  between operations: 18.3 us -> 0.7 us
    pallas_call x1 -> x2, Pallas kernels: 72.1 us -> 372 us  [the longest x1 300 us: backward(): pl.pallas_call(functools.partial(backward_kernel, names, swap), out_shape...]
    dot_general x41 -> x0, matrix products: 136 us -> none  [the longest x16 46 us: part(): return jnp.einsum('ta,tb->ab', *pair, preferred_element_type=jnp.float32)]
    ppermute x49 -> x0, starting transfers between devices: 130 us -> none  [the longest x12 72.8 us: inward(): return lax.ppermute(array.astype(jnp.bfloat16), 'context', [(0, 1), (3, 2)])]
    ppermute x49 -> x0, waiting for transfers between devices: 110 us -> none  [the longest x12 52 us: inward(): return lax.ppermute(array.astype(jnp.bfloat16), 'context', [(0, 1), (3, 2)])]
    unnamed x2 -> x0, waiting for transfers between devices: 44.8 us -> none
    dynamic_slice x7 -> x0, local copies, waits for them, and re-layouts: 28.5 us -> none  [the longest x6 27.8 us: pick(): return lax.dynamic_index_in_dim(array, index, axis, keepdims=False)]
    unnamed x190 -> x10, local copies, waits for them, and re-layouts: 37.6 us -> 10.6 us
    convert_element_type x12 -> x0, other arithmetic: 13.1 us -> none  [the longest x8 4.98 us: across(): return lax.ppermute(array.astype(jnp.bfloat16), 'context', [(1, 2), (2, 1)])]
  transfers between devices with their start and end apart: 50 -> 0, of which waited for: 14 -> 0; matrix products, arithmetic and copies ran while one was open for 37% -> 0% of each run, Pallas kernels for 11% -> 0%
where the time goes in v2:
time: 404 us; the launch traced here: 401 us
  Pallas kernels  372 us (92%)
  local copies, waits for them, and re-layouts  22.6 us (6%)
  other arithmetic  5.5 us (1%)
    pallas_call x1, Pallas kernels, backward(): pl.pallas_call(functools.partial(backward_kernel, names, swap), out_shape...  300 us
    pallas_call x1, Pallas kernels, forward(): pl.pallas_call(functools.partial(forward_kernel, swap), out_shape=[jax.Sh...  72.2 us
    unnamed x10, local copies, waits for them, and re-layouts  10.6 us

profile of v2, /device:TPU:24, one launch (start us, length us, event | category | flops | bytes accessed | tf_op | source)
XLA Modules:
  0.0 400.7 jit_solution(16149327436509685280)
XLA Ops:
  0.7 0.7 subtract_convert_fusion
  1.4 1.0 fusion
  2.4 1.3 pad_maximum_fusion
  3.6 72.2 %forward.1 = (bf16[512,512]{1,0:T(8,128)(2,1)}, bf16[4,512,128]{2,1,0:T(8,128)(2,1)}, f32[512,512]{1,0:T(8,128)}, f32[8,1,512]{2,1,0:T(1,128)}, bf16[512,2048]{1...) custom-call(bf16[512,2048]{1,0:T(8,128)(2,1)} %bitcast.21, ...), custom_call_target="tpu_custom_call" | custom-call | tf_op jit(solution)/shard_map/forward/pallas_call | solution.py:362
  75.8 299.6 %backward.1 = (bf16[512,2048]{1,0:T(8,128)(2,1)}, bf16[512,2048]{1,0:T(8,128)(2,1)}, f32[8,256]{1,0:T(8,128)}, f32[256,1408]{1,0:T(8,128)}, f32[256,2816]{1,0:T(...) custom-call(s32[1,512]{1,0:T(1,128)} %refs_0_.1, ...), custom_call_target="tpu_custom_call" | custom-call | tf_op jit(solution)/shard_map/backward/pallas_call | solution.py:1115
  375.5 0.0 copy-start.2
  375.5 1.4 fusion.1
  376.9 1.6 slice.14
  378.5 1.9 slice.13
  380.3 2.0 copy.31
  382.4 0.0 copy-done.2
  382.4 1.5 copy.33
  383.9 3.3 reshape.69
  387.2 3.9 copy.29
  391.1 0.0 copy-start
  391.1 5.7 %copy.32 = f32[256,2,1408]{2,1,0:T(2,128)} copy(f32[256,2,1408]{0,2,1:T(8,128)} %bitcast.20) | data formatting | bytes 5767168
  396.8 0.0 copy-done
  396.8 0.0 copy-start.1
  396.8 2.5 bitcast_convert_fusion
  399.3 0.0 copy-done.1
  399.3 1.3 copy.35
  (1 shorter events, 0.0 us)
Async XLA Ops:
  375.5 6.9 %copy-start.2 = (f32[256,1408]{1,0:T(8,128)S(1)}, f32[256,1408]{1,0:T(8,128)}, u32[]{:S(2)}) copy-start(f32[256,1408]{1,0:T(8,128)} %get-tuple-element.50) | copy-start | bytes 4325380
  391.1 5.7 %copy-start = (bf16[512,2048]{1,0:T(8,128)(2,1)S(1)}, bf16[512,2048]{1,0:T(8,128)(2,1)}, u32[]{:S(2)}) copy-start(bf16[512,2048]{1,0:T(8,128)(2,1)} %get-tuple-element.45) | copy-start | bytes 6291460
  396.8 2.5 copy-start.1

commit v3 on v2

--- a/solution.py
+++ b/solution.py
@@ -52,7 +52,7 @@
     x_hbm, seg_ref, cos_ref, sin_ref, gain_one_ref, gain_two_ref, wq_hbm, wkv_hbm, wout_hbm, raw_hbm,
     wdown_hbm, g_hbm,
     q_out, kv_out, att_out, lse_out, n1_out, n2_out, resid_out, hid_out, gg_out, wgu_out, low_out,
-    g_other, n1_other, low_other,
+    g_other, low_other,
     x, n1, wq, wkv, wout, raw, wdown, g, wgu, q, kv, keys, vals_t, run_max, run_sum, acc, att_low,
     own, stage_core, got_core, stage_x, got_x, resid, n2, gh, hid, gg,
     load_sem, store_sem, kv_send, kv_recv, core_send, core_recv, x_send, x_recv, ag_send, ag_recv,
@@ -126,7 +126,6 @@
     if swap:
         theirs_cols = aligned(1 - side, width // 2)
         swap_start(g_hbm.at[:, theirs_cols], g_other)
-        swap_start(n1.at[:, theirs_cols], n1_other)
 
     def kv_copy(k):
         return pltpu.make_async_remote_copy(
@@ -354,7 +353,6 @@
         ((rows, 2 * units), bf16),
         ((width, 2 * units), bf16),
         ((rows, heads * HD), bf16),
-        ((rows, width // 2), bf16),
         ((rows, width // 2), bf16),
         ((rows, heads * HD), bf16),
     ]
@@ -402,8 +400,8 @@
             dma((chunks,)),
             dma((3,)),
             dma((3,)),
-            dma((3,)),
-            dma((3,)),
+            dma((2,)),
+            dma((2,)),
         ],
         compiler_params=pltpu.CompilerParams(
             collective_id=0, has_side_effects=True, vmem_limit_bytes=60 * MIB
@@ -462,7 +460,7 @@
             pltpu.make_async_copy(
                 r.wkv_hbm.at[at],
                 r.w_rows.at[slot, :, heads_width : heads_width + 128],
-                r.w_cols_sem.at[slot],
+                r.w_kv_sem.at[slot],
             ),
         )
         return types.SimpleNamespace(
@@ -501,18 +499,30 @@
         mine_cols = aligned(side, half)
         lead = r.stage.shape[3]
 
-        def swap_copy(i, src, dst):
-            return remote(src, dst, r.dp_send.at[i], r.dp_recv.at[i], dp_mate)
-
-        swap_hid = swap_copy(0, r.hid_hbm, r.hid_o)
-        swap_n2 = swap_copy(1, r.n2_hbm.at[:, theirs_cols], r.n2_o)
+        def cuts(total):
+            return [(at, min(lead, total - at)) for at in range(0, total, lead)]
+
+        swaps = []
+
+        def swap_copy(src, dst):
+            i = len(swaps)
+            swaps.append(remote(src, dst, r.dp_send.at[i], r.dp_recv.at[i], dp_mate))
+            return swaps[i]
+
+        hid_cuts, gg_cuts = cuts(units), cuts(2 * units)
+        swap_hid = [
+            swap_copy(r.hid_hbm.at[:, at : at + size], r.hid_o.at[i, :, 0:size])
+            for i, (at, size) in enumerate(hid_cuts)
+        ]
+        swap_n2 = swap_copy(r.n2_hbm.at[mine, theirs_cols], r.n2_o.at[mine, :])
         swap_gg = [
-            swap_copy(2 + i, r.gg_hbm.at[:, i * lead : (i + 1) * lead], r.gg_o.at[i])
-            for i in range(2)
+            swap_copy(r.gg_hbm.at[:, at : at + size], r.gg_o.at[i, :, 0:size])
+            for i, (at, size) in enumerate(gg_cuts)
         ]
-        swap_gb = swap_copy(4, r.gb.at[:, theirs_cols], r.gb_o)
-        swap_gqkv = swap_copy(5, r.gqkv, r.gqkv_o)
-        for copy in (swap_hid, swap_n2, *swap_gg):
+        swap_gb = swap_copy(r.gb.at[mine, theirs_cols], r.gb_o.at[mine, :])
+        swap_gqkv = swap_copy(r.gqkv, r.gqkv_o)
+        swap_n1 = swap_copy(r.n1_hbm.at[:, theirs_cols], r.n1_o)
+        for copy in (*swap_hid, swap_n2, *swap_gg):
             copy.start()
 
     chunks = r.own_fin.shape[1]
@@ -611,29 +621,39 @@
         beside = place + 1 - 2 * lax.rem(place, 2)
         low_side = place < 2
         io_mate, across_mate = {"context": beside}, {"context": 3 - place}
-        plan = (
-            (r.g_hbm.at[:, mine_cols], r.go_hbm, r.hid, r.hid_o, units, r.dwdown_out),
-            (r.n2_hbm.at[:, mine_cols], r.n2_o, r.gg.at[:, 0:lead], r.gg_o.at[0], lead,
-             r.dgu_out.at[:, 0:lead]),
-            (None, None, r.gg.at[:, lead : 2 * lead], r.gg_o.at[1], lead,
-             r.dgu_out.at[:, lead : 2 * lead]),
-            (r.gb.at[:, mine_cols], r.gb_o, r.att_low, r.att_o, heads_width, r.dwout_out),
-            (r.n1_hbm.at[:, mine_cols], r.n1o_hbm, r.gqkv, r.gqkv_o, r.gqkv.shape[1],
-             r.dwqkv_out),
-        )
+        plan = []
+        for i, (at, size) in enumerate(hid_cuts):
+            cut = (r.g_hbm.at[:, mine_cols], r.go_hbm) if i == 0 else None
+            plan.append(
+                (cut, r.hid.at[:, at : at + size], r.hid_o.at[i], size,
+                 r.dwdown_out.at[:, at : at + size])
+            )
+        for i, (at, size) in enumerate(gg_cuts):
+            cut = (r.n2_hbm.at[:, mine_cols], r.n2_o) if i == 0 else None
+            plan.append(
+                (cut, r.gg.at[:, at : at + size], r.gg_o.at[i], size,
+                 r.dgu_out.at[:, at : at + size])
+            )
+        cut = (r.gb.at[:, mine_cols], r.gb_o)
+        plan.append((cut, r.att_low, r.att_o, heads_width, r.dwout_out))
+        cut = (r.n1_hbm.at[:, mine_cols], r.n1_o)
+        plan.append((cut, r.gqkv, r.gqkv_o, r.gqkv.shape[1], r.dwqkv_out))
+        sets = r.stage.shape[0]
+        last = len(plan) - 1
+        first_gg = len(hid_cuts)
 
         def cut_loads(u):
-            own, other = plan[u][:2]
+            own, other = plan[u][0]
             return (
                 pltpu.make_async_copy(own, r.cut.at[0:rows], r.cut_sem.at[0]),
                 pltpu.make_async_copy(other, r.cut.at[rows : 2 * rows], r.cut_sem.at[1]),
             )
 
         def piece(ref, s, j, u):
-            return ref.at[s, j, :, 0 : plan[u][4]]
+            return ref.at[s, j, :, 0 : plan[u][3]]
 
         def line_copy(u, j, slot, mate):
-            s = u % 2
+            s = u % sets
             return remote(
                 piece(r.stage, s, j, u), piece(r.got, s, slot, u), r.line_send.at[s, j],
                 r.line_recv.at[s, slot], mate,
@@ -641,16 +661,16 @@
 
         def result(u):
             return pltpu.make_async_copy(
-                r.sums.at[u % 2, :, 0 : plan[u][4]], plan[u][5], r.sums_sem.at[u % 2]
+                r.sums.at[u % sets, :, 0 : plan[u][3]], plan[u][4], r.sums_sem.at[u % sets]
             )
 
-        def prepare(u, load_next):
-            s = u % 2
-            own, other, width_u = plan[u][2], plan[u][3], plan[u][4]
-            if u >= 2:
+        def prepare(u, load_next=None):
+            s = u % sets
+            own, other, width_u = plan[u][1], plan[u][2], plan[u][3]
+            if u >= sets:
                 for j in range(3):
-                    line_copy(u - 2, j, 0, io_mate).wait_send()
-                result(u - 2).wait()
+                    line_copy(u - sets, j, 0, io_mate).wait_send()
+                result(u - sets).wait()
                 pl.when(is_end)(lambda: pl.semaphore_wait(r.io_credit, 1))
             if plan[u][0] is not None:
                 for copy in cut_loads(u):
@@ -696,7 +716,7 @@
                     copy.start()
 
         def add_in(u, j, slot):
-            width_u, s = plan[u][4], u % 2
+            width_u, s = plan[u][3], u % sets
             line_copy(u, 0, slot, io_mate).wait_recv()
 
             @pl.loop(0, 4)
@@ -711,17 +731,17 @@
             def _():
                 if step < 2:
                     add_in(u, step, step)
-                    if u >= 2 and step == 0:
+                    if u >= sets and step == 0:
                         pl.semaphore_wait(r.across_credit, 1)
                     line_copy(u, step, 3 + step, across_mate).start()
                 else:
                     add_in(u, 2, 3)
-                    if u >= 2:
+                    if u >= sets:
                         pl.semaphore_wait(r.io_credit, 1)
                     line_copy(u, 2, 0, io_mate).start()
 
         def complete(u):
-            width_u, s = plan[u][4], u % 2
+            width_u, s = plan[u][3], u % sets
 
             def take(slots):
                 for slot in slots:
@@ -744,7 +764,7 @@
                 take((2, 4))
 
             result(u).start()
-            if u + 2 < len(plan):
+            if u + sets <= last:
                 pl.semaphore_signal(r.io_credit, inc=1, device_id=io_mate, device_id_type=MESH)
 
                 @pl.when(is_mid)
@@ -765,7 +785,9 @@
     loads["gg"].wait()
     start_sum(0, tile_gu, lambda slot: dot_t(r.gg[...], r.w_rows[slot]), True)
     loads["hid"].wait()
-    start_sum(1, tile_down, lambda slot: dot(r.hid[...], r.w_cols[slot]), False)
+    if swap:
+        swap_hid[0].wait_recv()
+        prepare(0)
     for n in range(3):
         tile_qkv(n).start()
     finish_sum(0)
@@ -781,21 +803,26 @@
     gb_chip, gb_core, gb_onward = gather(0, r.gb.at[mine, :], r.gb)
     gb_chip.start()
     gb_core.start()
+    if swap:
+        swap_gb.start()
+    start_sum(1, tile_down, lambda slot: dot(r.hid[...], r.w_cols[slot]), False)
     for c in range(chunks):
         x_copy(1, c).start()
+    if swap:
+        pass_on(0, 0)
+        swap_hid[1].wait_recv()
+        prepare(1)
+        pass_on(0, 1)
     gb_chip.wait_recv()
     gb_onward.start()
     if swap:
-        swap_hid.wait_recv()
-        prepare(0, None)
         swap_n2.wait_recv()
-        for copy in cut_loads(1):
-            copy.start()
+        n2_chip, n2_core, n2_onward = gather(3, r.n2_o.at[mine, :], r.n2_o)
+        n2_chip.start()
+        n2_core.start()
     gb_core.wait_recv()
     gb_onward.wait_recv()
-    if swap:
-        swap_gb.start()
-    else:
+    if not swap:
         pltpu.make_async_copy(r.gb, r.gb_out, r.cut_sem.at[0]).start()
 
     loads["wout"].wait()
@@ -810,6 +837,9 @@
         product = r.ga[:, at].astype(f32).T * r.att[at, :]
         for e in range(2):
             r.delta[pair * 2 + e] = jnp.sum(product[64 * e : 64 * e + 64], 0, keepdims=True)
+
+    if swap:
+        pass_on(0, 2)
 
     loads["q"].wait()
     loads["kv"].wait()
@@ -865,7 +895,17 @@
 
     r.dkv[...] = back_block(0, True)
     if swap:
-        pass_on(0, 0)
+        pass_on(1, 0)
+        pass_on(1, 1)
+        n2_chip.wait_recv()
+        n2_onward.start()
+        n2_core.wait_recv()
+        n2_onward.wait_recv()
+        for copy in cut_loads(first_gg):
+            copy.start()
+        swap_gg[0].wait_recv()
+        prepare(2)
+        complete(0)
 
     @pl.loop(0, heads_width // 128)
     def _(pair):
@@ -885,6 +925,8 @@
     ).astype(bf16)
     if swap:
         swap_gqkv.start()
+        swap_n1.start()
+        pass_on(1, 2)
     else:
         pltpu.make_async_copy(r.gqkv, r.gqkv_out, r.cut_sem.at[1]).start()
 
@@ -892,6 +934,28 @@
         0, tile_qkv,
         lambda slot: dot_t(r.gqkv[...], r.w_rows[slot, :, 0 : r.gqkv.shape[1]]), True,
     )
+    if swap:
+        swap_gg[1].wait_recv()
+        prepare(3)
+        complete(1)
+        pass_on(2, 0)
+
+    finish_sum(0)
+    loads["x_own"].wait()
+
+    def keep_tokens(at, grad):
+        r.tokens_own[:, at] = (r.grad_resid[:, at] + grad).astype(bf16)
+
+    back_through_norm(0, r.x_own, r.gain_one, 0, keep_tokens)
+    tokens_chip, tokens_core, tokens_onward = gather(2, r.tokens_own, r.tokens_out)
+    tokens_store = pltpu.make_async_copy(r.tokens_own, r.tokens_out.at[mine, :], r.out_sem.at[1])
+    for copy in (tokens_chip, tokens_core, tokens_store):
+        copy.start()
+    if swap:
+        pass_on(2, 1)
+        pass_on(2, 2)
+        swap_gg[2].wait_recv()
+        prepare(4)
 
     finish_sum(1)
     for c in range(chunks):
@@ -902,20 +966,18 @@
     for copy in (mixed_chip, mixed_core, mixed_store):
         copy.start()
     if swap:
-        pass_on(0, 1)
-        pass_on(0, 2)
-
-    finish_sum(0)
-    loads["x_own"].wait()
-
-    def keep_tokens(at, grad):
-        r.tokens_own[:, at] = (r.grad_resid[:, at] + grad).astype(bf16)
-
-    back_through_norm(0, r.x_own, r.gain_one, 0, keep_tokens)
-    tokens_chip, tokens_core, tokens_onward = gather(2, r.tokens_own, r.tokens_out)
-    tokens_store = pltpu.make_async_copy(r.tokens_own, r.tokens_out.at[mine, :], r.out_sem.at[1])
-    for copy in (tokens_chip, tokens_core, tokens_store):
-        copy.start()
+        complete(2)
+        pass_on(3, 0)
+        swap_gg[3].wait_recv()
+        for copy in late:
+            copy.wait()
+        prepare(5)
+        swap_gb.wait_recv()
+        gbo_chip, gbo_core, gbo_onward = gather(4, r.gb_o.at[mine, :], r.gb_o)
+        gbo_chip.start()
+        gbo_core.start()
+        pass_on(3, 1)
+        pass_on(3, 2)
 
     for i, mate in enumerate((core_mate, chip_mate)):
         copy = remote(
@@ -942,6 +1004,33 @@
         ]
         for copy in pieces:
             copy.start()
+        complete(3)
+    else:
+        r.gains_out[...] = r.gain_sum[2]
+    tokens_chip.wait_recv()
+    tokens_onward.start()
+    mixed_chip.wait_recv()
+    mixed_onward.start()
+    if swap:
+        gbo_chip.wait_recv()
+        gbo_onward.start()
+        gbo_core.wait_recv()
+        gbo_onward.wait_recv()
+        for copy in cut_loads(last - 1):
+            copy.start()
+        prepare(6)
+        swap_n1.wait_recv()
+        for copy in cut_loads(last):
+            copy.start()
+        for step in range(3):
+            pass_on(4, step)
+        complete(4)
+        swap_gqkv.wait_recv()
+        prepare(7)
+        for u in (5, 6, 7):
+            for step in range(3):
+                pass_on(u, step)
+            complete(u)
         for copy in pieces:
             copy.wait()
         r.gains_out[...] = (
@@ -950,38 +1039,6 @@
             + r.gain_piece[2]
             + r.gain_piece[3]
         )
-    else:
-        r.gains_out[...] = r.gain_sum[2]
-
-    if swap:
-        complete(0)
-        swap_gg[0].wait_recv()
-        prepare(1, None)
-    mixed_chip.wait_recv()
-    mixed_onward.start()
-    tokens_chip.wait_recv()
-    tokens_onward.start()
-    if swap:
-        pass_on(1, 0)
-        swap_gg[1].wait_recv()
-        swap_gb.wait_recv()
-        prepare(2, 3)
-        pass_on(1, 1)
-        pass_on(1, 2)
-        complete(1)
-        for copy in late:
-            copy.wait()
-        prepare(3, 4)
-        pass_on(2, 0)
-        pass_on(2, 1)
-        pass_on(2, 2)
-        complete(2)
-        swap_gqkv.wait_recv()
-        prepare(4, None)
-        for u in (3, 4):
-            for step in range(3):
-                pass_on(u, step)
-            complete(u)
 
     for copy in (mixed_core, mixed_onward, tokens_core, tokens_onward):
         copy.wait_recv()
@@ -995,9 +1052,11 @@
     for k in (1, 2, 3):
         pl.when(place >= k)(dkv_copy(k, 0).wait_send)
     if swap:
-        for copy in (swap_hid, swap_n2, *swap_gg, swap_gb, swap_gqkv):
+        for copy in (
+            *swaps, n2_chip, n2_core, n2_onward, gbo_chip, gbo_core, gbo_onward
+        ):
             copy.wait_send()
-        for u in (3, 4):
+        for u in range(last + 1 - sets, last + 1):
             for j in range(3):
                 line_copy(u, j, 0, io_mate).wait_send()
             result(u).wait()
@@ -1013,6 +1072,7 @@
     span = width // chunks
     wide = heads * HD
     qkv = wide + 2 * HD
+    lead, sets = 768, 3
     outs = {
         "mixed_out": ((rows, width), bf16),
         "tokens_out": ((rows, width), bf16),
@@ -1026,6 +1086,7 @@
             "dwqkv_out": ((width // 8, qkv), f32),
             "n2_o": ((rows, width // 2), bf16),
             "gb_o": ((rows, width // 2), bf16),
+            "n1_o": ((rows, width // 2), bf16),
         }
     else:
         outs |= {"gb_out": ((rows, width), bf16), "gqkv_out": ((rows, qkv), bf16)}
@@ -1069,16 +1130,16 @@
     }
     if swap:
         scratch |= {
-            "hid_o": ((rows, units), bf16),
-            "gg_o": ((2, rows, units), bf16),
+            "hid_o": ((-(-units // lead), rows, lead), bf16),
+            "gg_o": ((-(-2 * units // lead), rows, lead), bf16),
             "gqkv_o": ((rows, qkv), bf16),
             "att_low": ((rows, wide), bf16),
             "att_o": ((rows, wide), bf16),
             "cut": ((2 * rows, width // 2), bf16),
             "turned": ((256, 2 * rows), bf16),
-            "stage": ((2, 3, width // 8, units), bf16),
-            "got": ((2, 5, width // 8, units), bf16),
-            "sums": ((2, width // 8, units), f32),
+            "stage": ((sets, 3, width // 8, lead), bf16),
+            "got": ((sets, 5, width // 8, lead), bf16),
+            "sums": ((sets, width // 8, lead), f32),
             "gain_half": ((2, 8, width // 2), f32),
             "gain_piece": ((4, 8, width // 8), f32),
         }
@@ -1086,12 +1147,13 @@
         "load_sem": (9,),
         "w_rows_sem": (3,),
         "w_cols_sem": (3,),
+        "w_kv_sem": (3,),
         "core_send": (2, chunks),
         "core_recv": (2, chunks),
         "x_send": (2, chunks),
         "x_recv": (2, chunks),
-        "ag_send": (3, 3),
-        "ag_recv": (3, 3),
+        "ag_send": (5, 3),
+        "ag_recv": (5, 3),
         "kv_send": (4,),
         "kv_recv": (4,),
         "gain_send": (6,),
@@ -1101,11 +1163,11 @@
     }
     if swap:
         sems |= {
-            "dp_send": (6,),
-            "dp_recv": (6,),
-            "line_send": (2, 3),
-            "line_recv": (2, 5),
-            "sums_sem": (2,),
+            "dp_send": (10,),
+            "dp_recv": (10,),
+            "line_send": (sets, 3),
+            "line_recv": (sets, 5),
+            "sums_sem": (sets,),
             "late_sem": (2,),
         }
     credits = ["io_credit", "across_credit"] if swap else []
@@ -1130,6 +1192,104 @@
     return dict(zip(outs, results, strict=True))
 
 
+def finish_kernel(
+    down_hbm, gateup_hbm, out_hbm, qkv_hbm, tokens_hbm, mixed_hbm,
+    down_o, gateup_o, out_o, q_o, kv_o, tokens_o, mixed_o,
+    down, gateup, out, qkv, tokens, mixed, down_t, gateup_t, out_t, kv_t, tokens_t,
+    load_sem, store_sem,
+):
+    wide = q_o.shape[1]
+    parts = 4
+    loads, stores = [], []
+
+    def load(src, dst):
+        copy = pltpu.make_async_copy(src, dst, load_sem.at[len(loads)])
+        copy.start()
+        loads.append(copy)
+        return copy
+
+    def store(src, dst):
+        copy = pltpu.make_async_copy(src, dst, store_sem.at[len(stores)])
+        copy.start()
+        stores.append(copy)
+
+    def piece(ref, i):
+        size = ref.shape[0] // parts
+        return ref.at[i * size : (i + 1) * size]
+
+    token_loads = [load(piece(tokens_hbm, i), piece(tokens, i)) for i in range(parts)]
+    gateup_loads = [load(piece(gateup_hbm, i), piece(gateup, i)) for i in range(parts)]
+    load_mixed = load(mixed_hbm, mixed)
+    load_down = load(down_hbm, down)
+    load_qkv = load(qkv_hbm, qkv)
+    load_out = load(out_hbm, out)
+    for i in range(parts):
+        token_loads[i].wait()
+        piece(tokens_t, i)[...] = piece(tokens, i)[...].astype(jnp.float32)
+        store(piece(tokens_t, i), piece(tokens_o, i))
+    for i in range(parts):
+        gateup_loads[i].wait()
+        values, target = piece(gateup, i), piece(gateup_t, i)
+        for b in range(gateup.shape[1] // 256):
+            at = slice(b * 128, b * 128 + 128)
+            target[:, 0, at] = values[:, b * 256 : b * 256 + 128]
+            target[:, 1, at] = values[:, b * 256 + 128 : b * 256 + 256]
+        store(target, piece(gateup_o, i))
+    load_mixed.wait()
+    store(mixed, mixed_o)
+    load_down.wait()
+    for i in range(down.shape[1] // 128):
+        at = slice(i * 128, i * 128 + 128)
+        down_t[at, :] = down[:, at].T
+    store(down_t, down_o)
+    load_qkv.wait()
+    store(qkv.at[:, 0:wide], q_o)
+    kv_t[:, 0, :] = qkv[:, wide:]
+    store(kv_t, kv_o)
+    load_out.wait()
+    for i in range(wide // 128):
+        at = slice(i * 128, i * 128 + 128)
+        out_t[at, :] = out[:, at].T
+    store(out_t, out_o)
+    for copy in stores:
+        copy.wait()
+
+
+def finish(down, gateup, out, qkv, tokens, mixed):
+    depth, units = down.shape
+    wide = out.shape[1]
+    rows, width = tokens.shape
+    bf16, f32 = jnp.bfloat16, jnp.float32
+    outs = [
+        ((units, depth), f32),
+        ((depth, 2, units), f32),
+        ((wide, depth), f32),
+        ((depth, wide), f32),
+        ((depth, 1, 2 * HD), f32),
+        ((rows, width), f32),
+        ((rows, width), bf16),
+    ]
+    scratch = [
+        *((array.shape, array.dtype) for array in (down, gateup, out, qkv, tokens, mixed)),
+        *outs[:3],
+        *outs[4:6],
+    ]
+    anywhere = pl.BlockSpec(memory_space=pl.ANY)
+    return pl.pallas_call(
+        finish_kernel,
+        out_shape=[jax.ShapeDtypeStruct(*entry) for entry in outs],
+        in_specs=[anywhere] * 6,
+        out_specs=[anywhere] * len(outs),
+        scratch_shapes=[
+            *(pltpu.VMEM(*entry) for entry in scratch),
+            pltpu.SemaphoreType.DMA((12,)),
+            pltpu.SemaphoreType.DMA((13,)),
+        ],
+        compiler_params=pltpu.CompilerParams(vmem_limit_bytes=62 * MIB),
+        name="finish",
+    )(down, gateup, out, qkv, tokens, mixed)
+
+
 def pick(array, index, axis):
     return lax.dynamic_index_in_dim(array, index, axis, keepdims=False)
 
@@ -1194,7 +1354,7 @@
     one, two = gain_one[None], gain_two[None]
     (
         queries, kv, attended, log_total, normed_one, normed_two, resid, hidden, grad_gateup, w_gu,
-        attended_low, g_other, normed_one_other, attended_other,
+        attended_low, g_other, attended_other,
     ) = forward(
         swap, x, segments, cosine, sine, one, two, w_query, w_kv, w_out, w_gateup, w_down, g
     )
@@ -1208,13 +1368,16 @@
     if swap:
         inputs |= {
             "n1_hbm": normed_one, "n2_hbm": normed_two, "attlow_hbm": attended_low,
-            "go_hbm": g_other, "n1o_hbm": normed_one_other, "atto_hbm": attended_other,
+            "go_hbm": g_other, "atto_hbm": attended_other,
         }
     out = backward(swap, inputs, tok_count, model_width, units, width_q // HD)
     if swap:
         gains = out["gains_out"]
-        sent_wdown, sent_wout = out["dwdown_out"].T, out["dwout_out"].T
-        sent_gateup, sent_wqkv = out["dgu_out"], out["dwqkv_out"]
+        sent_wdown, sent_gateup, sent_wout, sent_wq, sent_wkv, grad_tokens, mixed = finish(
+            *(out[name] for name in ("dwdown_out", "dgu_out", "dwout_out", "dwqkv_out")),
+            out["tokens_out"],
+            out["mixed_out"],
+        )
     else:
         gains = lax.psum_scatter(
             out["gains_out"], ("dp", "context"), scatter_dimension=1, tiled=True
@@ -1223,15 +1386,18 @@
         sent_gateup = weight_grad(normed_two, grad_gateup, 0)
         sent_wout = weight_grad(attended_low, out["gb_out"], 1)
         sent_wqkv = weight_grad(normed_one, out["gqkv_out"], 0)
+        sent_wq, sent_wkv = sent_wqkv[:, :width_q], sent_wqkv[:, width_q:]
+        sent_gateup = sent_gateup.reshape(-1, units // 128, 2, 128).transpose(0, 2, 1, 3)
+        grad_tokens, mixed = out["tokens_out"].astype(jnp.float32), out["mixed_out"]
     return (
-        out["mixed_out"].reshape(tokens.shape),
-        out["tokens_out"].astype(jnp.float32).reshape(tokens.shape),
+        mixed.reshape(tokens.shape),
+        grad_tokens.reshape(tokens.shape),
         gains[0],
-        sent_wqkv[:, :width_q],
-        sent_wqkv[:, width_q:].reshape(-1, heads_kv, 2 * HD),
+        sent_wq,
+        sent_wkv.reshape(-1, heads_kv, 2 * HD),
         sent_wout,
         gains[1],
-        sent_gateup.reshape(-1, units // 128, 2, 128).transpose(0, 2, 1, 3).reshape(-1, 2, units),
+        sent_gateup.reshape(-1, 2, units),
         sent_wdown,
     )
 

time: 404 us -> 314 us (0.78)
  Pallas kernels: 372 us -> 304 us
  local copies, waits for them, and re-layouts: 22.6 us -> 1.34 us
    pallas_call x1, Pallas kernels: 300 us -> 224 us  [backward(): pl.pallas_call(functools.partial(backward_kernel, names, swap), out_shape...]
    unnamed x10 -> x0, local copies, waits for them, and re-layouts: 10.6 us -> none
    pallas_call x0 -> x1, Pallas kernels: none -> 8.08 us  [finish(): pl.pallas_call(finish_kernel, out_shape=[jax.ShapeDtypeStruct(*entry) for...]
    reshape x2 -> x0, local copies, waits for them, and re-layouts: 7.2 us -> none  [shards(): sent_gateup.reshape(-1, units // 128, 2, 128).transpose(0, 2, 1, 3)]
where the time goes in v3:
time: 314 us; the launch traced here: 309 us
  Pallas kernels  304 us (97%)
    pallas_call x1, Pallas kernels, backward(): pl.pallas_call(functools.partial(backward_kernel, names, swap), out_shape...  224 us
    pallas_call x1, Pallas kernels, forward(): pl.pallas_call(functools.partial(forward_kernel, swap), out_shape=[jax.Sh...  71.7 us
    pallas_call x1, Pallas kernels, finish(): pl.pallas_call(finish_kernel, out_shape=[jax.ShapeDtypeStruct(*entry) for...  8.08 us

profile of v3, /device:TPU:24, one launch (start us, length us, event | category | flops | bytes accessed | tf_op | source)
XLA Modules:
  0.0 308.9 jit_solution(3927422430028246841)
XLA Ops:
  0.7 0.7 subtract_convert_fusion
  1.4 1.0 fusion
  2.4 1.3 pad_maximum_fusion
  3.6 71.7 %forward.1 = (bf16[512,512]{1,0:T(8,128)(2,1)}, bf16[4,512,128]{2,1,0:T(8,128)(2,1)}, f32[512,512]{1,0:T(8,128)}, f32[8,1,512]{2,1,0:T(1,128)}, bf16[512,2048]{1...) custom-call(bf16[512,2048]{1,0:T(8,128)(2,1)} %bitcast.10, ...), custom_call_target="tpu_custom_call" | custom-call | tf_op jit(solution)/shard_map/forward/pallas_call | solution.py:360
  75.3 224.0 %backward.1 = (bf16[512,2048]{1,0:T(8,128)(2,1)}, bf16[512,2048]{1,0:T(8,128)(2,1)}, f32[8,256]{1,0:T(8,128)}, f32[256,1408]{1,0:T(8,128)}, f32[256,2816]{1,0:T(...) custom-call(s32[1,512]{1,0:T(1,128)} %refs_0_.1, ...), custom_call_target="tpu_custom_call" | custom-call | tf_op jit(solution)/shard_map/backward/pallas_call | solution.py:1177
  299.3 1.3 fusion.1
  300.6 8.1 %finish.1 = (f32[1408,256]{1,0:T(8,128)}, f32[256,2,1408]{2,1,0:T(2,128)}, f32[512,256]{1,0:T(8,128)}, f32[256,512]{1,0:T(8,128)}, f32[256,1,128]{2,1,0:T(1,128)...) custom-call(f32[256,1408]{1,0:T(8,128)} %get-tuple-element.49.down_hbm, f32[256,2816]{1,0:T(8,128)} %get-tuple-element.50.gateup_hbm, ...), custom_call_target="tpu_custom_call" | custom-call | tf_op jit(solution)/shard_map/finish/pallas_call | solution.py:1278
  (1 shorter events, 0.0 us)

commit v4 on v0

v4 whole, which is shorter than its diff:
```python
import functools
import types

import jax
import jax.numpy as jnp
import numpy as np
from jax import lax
from jax.experimental import pallas as pl
from jax.experimental.pallas import tpu as pltpu
from jax.sharding import PartitionSpec as P

HD = 64


epsilon = 1e-05
neg_large = -1e30


MESH = pl.DeviceIdType.MESH
MIB = 1 << 20
log2_e = 1.4426950408889634


def dot(left, right):
    return jnp.dot(left, right, preferred_element_type=jnp.float32)


def dot_t(left, right):
    return lax.dot_general(left, right, (((1,), (1,)), ((), ())), preferred_element_type=jnp.float32)


def lanes(shape):
    return lax.broadcasted_iota(jnp.int32, shape, len(shape) - 1)


def turn_of(n, size):
    return n % size if isinstance(n, int) else lax.rem(n, size)


def aligned(index, size):
    if isinstance(index, int):
        return pl.ds(index * size, size)
    return pl.ds(pl.multiple_of(index * size, size), size)


def turn(values, cosine, sine):
    low_half = lax.rem(lanes(values.shape), 64) < 32
    swapped = jnp.where(low_half, pltpu.roll(values, 96, 1), pltpu.roll(values, 32, 1))
    return values * cosine + swapped * sine


def cos_sin(phase):
    count = jnp.floor(phase * 0.6366197723675814 + 0.5)
    rest = phase - count * 1.5703125
    rest = rest - count * 0.0004837512969970703
    rest = rest - count * 7.549789954e-08
    square = rest * rest
    sine = rest + rest * square * (
        -0.16666666666 + square * (0.0083333333333 + square * -0.0001984126984)
    )
    cosine = 1.0 + square * (
        -0.5 + square * (0.041666666666 + square * (-0.0013888888889 + square * 2.48015873e-05))
    )
    place = count - 4.0 * jnp.floor(count * 0.25)
    odd = (place == 1.0) | (place == 3.0)
    first, second = jnp.where(odd, sine, cosine), jnp.where(odd, cosine, sine)
    return (
        jnp.where((place == 1.0) | (place == 2.0), -first, first),
        jnp.where(place >= 2.0, -second, second),
    )


def layer_kernel(names, swap, *refs):
    r = types.SimpleNamespace(**dict(zip(names, refs, strict=True)))
    rows, width = r.x_n2.shape
    quarter = rows // 4
    units = r.hid.shape[1]
    heads_width = r.q.shape[1]
    f32, bf16 = jnp.float32, jnp.bfloat16
    tensor = lax.axis_index("tensor")
    place = lax.axis_index("context")
    core, chip = lax.rem(tensor, 2), lax.div(tensor, 2)
    core_mate = {"tensor": chip * 2 + 1 - core}
    chip_mate = {"tensor": (1 - chip) * 2 + core}
    mates = [core_mate, chip_mate, *({"context": lax.rem(place + k, 4)} for k in (1, 2, 3))]
    if swap:
        side = lax.axis_index("dp")
        dp_mate = {"dp": 1 - side}
        mates.append(dp_mate)
    mine = aligned(tensor, quarter)
    key_lane = lanes((rows, 128)) < 64

    barrier = pltpu.get_barrier_semaphore()
    for mate in mates:
        pl.semaphore_signal(barrier, inc=1, device_id=mate, device_id_type=MESH)

    def remote(src, dst, send, recv, mate):
        return pltpu.make_async_remote_copy(
            src_ref=src, dst_ref=dst, send_sem=send, recv_sem=recv, device_id=mate,
            device_id_type=MESH,
        )

    loads, stores = [], []

    def load(src, dst):
        copy = pltpu.make_async_copy(src, dst, r.load_sem.at[len(loads)])
        loads.append(copy)
        copy.start()
        return copy

    def store_copy(i):
        return pltpu.make_async_copy(*stores[i], r.store_sem.at[i])

    def store(src, dst):
        stores.append((src, dst))
        store_copy(len(stores) - 1).start()

    swaps = []

    def swap_copy(src, dst):
        i = len(swaps)
        swaps.append(remote(src, dst, r.dp_send.at[i], r.dp_recv.at[i], dp_mate))
        return swaps[i]

    if swap:
        half = width // 2
        theirs_cols, mine_cols = aligned(1 - side, half), aligned(side, half)
        lead = r.got.shape[3]

        def cuts(total):
            return [(at, min(lead, total - at)) for at in range(0, total, lead)]

        hid_cuts, gg_cuts = cuts(units), cuts(2 * units)
        row_halves = [aligned(chip, rows // 2), aligned(1 - chip, rows // 2)]
        swap_g = swap_copy(r.g_hbm.at[:, theirs_cols], r.g_o)
        swap_low = swap_copy(r.att_low, r.low_o)
        swap_hid = [
            [
                swap_copy(r.hid.at[at_rows, at : at + size], r.hid_o.at[i, at_rows, 0:size])
                for i, (at, size) in enumerate(hid_cuts)
            ]
            for at_rows in row_halves
        ]
        swap_n2 = swap_copy(r.x_n2.at[mine, theirs_cols], r.n2_o.at[mine, :])
        swap_gg = [
            swap_copy(r.gg.at[:, at : at + size], r.gg_o.at[i, :, 0:size])
            for i, (at, size) in enumerate(gg_cuts)
        ]
        swap_gb = swap_copy(r.n1_gb.at[mine, theirs_cols], r.gb_o.at[mine, :])
        swap_n1 = swap_copy(r.n1_out.at[:, theirs_cols], r.n1_o)

    chunks = r.own_fin.shape[1]
    span = r.own_fin.shape[3]

    def core_copy(b, c):
        return remote(
            r.stage_core.at[b, c], r.got_core.at[b, c], r.core_send.at[b, c],
            r.core_recv.at[b, c], core_mate,
        )

    def x_copy(b, c):
        return remote(
            r.stage_x.at[b, c], r.got_x.at[b, c], r.x_send.at[b, c], r.x_recv.at[b, c], chip_mate
        )

    def start_sum(b, tile, product, send=True):
        def put(ref, index, at, value):
            ref[(*index, slice(None), at)] = value.astype(ref.dtype)

        routes = (
            ((1 - chip) * 2 + 1 - core, lambda c, at, v: put(r.stage_core, (b, c, 0), at, v)),
            (chip * 2 + 1 - core, lambda c, at, v: put(r.stage_core, (b, c, 1), at, v)),
            ((1 - chip) * 2 + core, lambda c, at, v: put(r.own_fwd, (c,), at, v)),
            (chip * 2 + core, lambda c, at, v: put(r.own_fin, (b, c), at, v)),
        )

        def forward_chunk(c):
            core_copy(b, c).wait_recv()
            r.stage_x[b, c] = (r.own_fwd[c] + r.got_core[b, c, 0].astype(f32)).astype(bf16)
            if send:
                x_copy(b, c).start()

        @pl.loop(0, chunks)
        def _(c):
            for t in range(span // 256):
                n = c * (span // 256) + t
                if tile is not None:
                    tile(n).wait()
                r.tmp[...] = product(n)
                for owner, route in routes:
                    route(c, slice(t * 256, t * 256 + 256), r.tmp[aligned(owner, quarter), :])
                if tile is not None:

                    @pl.when(n + 3 < width // 256)
                    def _():
                        tile(n + 3).start()

            core_copy(b, c).start()
            pl.when(c > 0)(lambda: forward_chunk(c - 1))

        forward_chunk(chunks - 1)

    def finish_sum(b):
        for c in range(chunks):
            x_copy(b, c).wait_recv()
            r.own_fin[b, c] = (
                r.own_fin[b, c] + r.got_core[b, c, 1].astype(f32) + r.got_x[b, c].astype(f32)
            )
        for c in range(chunks):
            core_copy(b, c).wait_send()
            x_copy(b, c).wait_send()

    def gather(i, src, dst):
        def copy(slot, src, owner, mate):
            return remote(
                src, dst.at[aligned(owner, quarter), :], r.ag_send.at[i, slot],
                r.ag_recv.at[i, slot], mate,
            )

        other = chip_mate["tensor"]
        return (
            copy(0, src, tensor, chip_mate),
            copy(1, src, tensor, core_mate),
            copy(2, dst.at[aligned(other, quarter), :], other, core_mate),
        )

    def mask(bias, k, first):
        key_index = (place - k) * rows + lax.broadcasted_iota(jnp.int32, (rows, rows), 0)
        allowed = key_index >= r.seg[...]
        if first:
            query_index = place * rows + lax.broadcasted_iota(jnp.int32, (rows, rows), 1)
            allowed = allowed & (key_index <= query_index)
        bias[...] = jnp.where(allowed, 0.0, neg_large)

    def pad_keys(keys, block):
        keys[0] = jnp.where(key_lane, block, 0.0).astype(bf16)
        keys[1] = jnp.where(key_lane, 0.0, pltpu.roll(block, 64, 1)).astype(bf16)

    def kv_copy(k):
        return remote(
            r.kv.at[0], r.kv.at[k], r.kv_send.at[k], r.kv_recv.at[k],
            {"context": lax.rem(place + k, 4)},
        )

    def attention(wgu, raw, wq, wkv, keys, vals_t, bias):
        load_x = load(r.x_hbm, r.x_n2)
        load_wkv = load(r.wkv_hbm, wkv)
        load_wq = load(r.wq_hbm, wq)
        ring = raw.shape[0]

        def raw_copy(i):
            slot = turn_of(i, ring)
            return pltpu.make_async_copy(
                r.wgateup_hbm.at[aligned(i, 128)], raw.at[slot], r.raw_sem.at[slot]
            )

        for i in range(ring):
            raw_copy(i).start()

        position = place * rows + lanes((1, rows)) - r.seg[...]
        cosine, sine = cos_sin(r.freqs[...] * position.astype(f32))
        r.cos[...] = jnp.concatenate([cosine] * 4, 0).T
        r.sin[...] = jnp.concatenate([-sine, sine] * 2, 0).T

        load_x.wait()

        @pl.loop(0, rows // 64)
        def _(i):
            at = aligned(i, 64)
            values = r.x_n2[at, :].astype(f32)
            inverse = lax.rsqrt(jnp.mean(values * values, -1, keepdims=True) + epsilon)
            r.n1_gb[at, :] = (values * inverse * r.gain_one[...]).astype(bf16)

        store(r.n1_gb, r.n1_out)

        load_wkv.wait()
        r.kv[0] = turn(
            dot(r.n1_gb[...], wkv[...]),
            jnp.where(key_lane, r.cos[...], 1.0),
            jnp.where(key_lane, r.sin[...], 0.0),
        ).astype(bf16)
        pl.semaphore_wait(barrier, len(mates))
        for k in (1, 2, 3):
            pl.when(place + k < 4)(kv_copy(k).start)
        if swap:
            swap_g.start()

        load_wq.wait()

        @pl.loop(0, heads_width // 256)
        def _(i):
            wide = dot(r.n1_gb[...], wq[:, aligned(i, 256)])
            for part in range(2):
                turned = turn(wide[:, 128 * part : 128 * part + 128], r.cos[...], r.sin[...])
                at = pl.ds(pl.multiple_of(i * 256 + 128 * part, 128), 128)
                r.q[:, at] = (turned * (0.125 * log2_e)).astype(bf16)

        def attend_block(k, first):
            mask(bias, k, first)
            block = r.kv[k].astype(f32)
            pad_keys(keys, block)
            vals_t[...] = block.T[64:].astype(bf16)

            @pl.loop(0, heads_width // 128)
            def _(pair):
                pair_q = r.q[:, aligned(pair, 128)]
                for e in range(2):
                    head = pair * 2 + e
                    scores = dot_t(keys[e], pair_q) + bias[...]
                    top = jnp.max(scores, 0, keepdims=True)
                    at = aligned(head, 64)
                    if first:
                        weights = jnp.exp2(scores - top)
                        r.run_sum[head] = jnp.sum(weights, 0, keepdims=True)
                        r.att[at, :] = dot(vals_t[...], weights.astype(bf16))
                    else:
                        old = r.lse[head]
                        top = jnp.maximum(top, old)
                        fade = jnp.exp2(old - top)
                        weights = jnp.exp2(scores - top)
                        r.run_sum[head] = r.run_sum[head] * fade + jnp.sum(weights, 0, keepdims=True)
                        r.att[at, :] = r.att[at, :] * fade + dot(vals_t[...], weights.astype(bf16))
                    r.lse[head] = top

        attend_block(0, True)

        row = lax.broadcasted_iota(jnp.int32, (256, 256), 0)
        column = lax.broadcasted_iota(jnp.int32, (256, 256), 1)
        source = jnp.where(row < 128, 2 * row, 2 * row - 255)
        order = (column == source).astype(bf16)

        @pl.loop(0, width // 128)
        def _(i):
            raw_copy(i).wait()
            at = aligned(i, 128)
            split = dot(order, raw[turn_of(i, ring)].reshape(256, units)).astype(bf16)
            for b in range(units // 128):
                wgu[at, 256 * b : 256 * b + 128] = split[:128, 128 * b : 128 * b + 128]
                wgu[at, 256 * b + 128 : 256 * b + 256] = split[128:, 128 * b : 128 * b + 128]

            @pl.when(i + ring < width // 128)
            def _():
                raw_copy(i + ring).start()

        @pl.loop(1, place + 1)
        def _(k):
            kv_copy(k).wait_recv()
            attend_block(k, False)

        for k in (1, 2, 3):
            pl.when(place + k < 4)(kv_copy(k).wait_send)

        @pl.loop(0, heads_width // 128)
        def _(pair):
            for e in range(2):
                head = pair * 2 + e
                at = aligned(head, 64)
                r.att[at, :] = r.att[at, :] * (1.0 / r.run_sum[head])
                r.lse[head] = r.lse[head] + jnp.log2(r.run_sum[head])
            at = aligned(pair, 128)
            r.att_low[:, at] = r.att[at, :].T.astype(bf16)

    def feed_forward(wgu, g, gh, wdown):
        load_g = load(r.g_hbm, g)
        load_wdown = load(r.wdown_hbm, wdown)
        load_wout.wait()
        start_sum(0, None, lambda n: dot(r.att_low[...], r.wout[:, aligned(n, 256)]))
        if swap:
            swap_low.start()

        load_g.wait()
        load_wdown.wait()

        @pl.loop(0, units // 128)
        def _(b):
            at = aligned(b, 128)
            gh[:, at] = dot_t(g[...], wdown[at, :])

        finish_sum(0)
        load_x_own.wait()
        square = jnp.zeros((quarter, 1), f32)
        for c in range(chunks):
            at = slice(c * span, (c + 1) * span)
            part = r.own_fin[0, c] + r.x_own[:, at].astype(f32)
            r.resid[:, at] = part
            square = square + jnp.sum(part * part, -1, keepdims=True)
        inverse = lax.rsqrt(square / width + epsilon)
        r.x_n2[mine, :] = (r.resid[...] * inverse * r.gain_two[...]).astype(bf16)
        to_chip, to_core, onward = gather(5, r.x_n2.at[mine, :], r.x_n2)
        to_chip.start()
        to_core.start()

        def units_of(at, first, last):
            @pl.loop(first, last)
            def _(b):
                wide = dot(r.x_n2[at, :], wgu[:, aligned(b, 256)])
                gate, up = wide[:, :128], wide[:, 128:]
                grad = gh[at, aligned(b, 128)]
                sigmoid = 1.0 / (1.0 + jnp.exp(-gate))
                active = gate * sigmoid
                r.hid[at, aligned(b, 128)] = (active * up).astype(bf16)
                grad_gate = grad * up * (sigmoid * (1.0 + gate * (1.0 - sigmoid)))
                both = jnp.concatenate([grad_gate, grad * active], 1).astype(bf16)
                r.gg[at, aligned(b, 256)] = both

        first_at, second_at = aligned(chip, 2 * quarter), aligned(1 - chip, 2 * quarter)
        blocks = units // 128
        to_core.wait_recv()
        units_of(first_at, 0, blocks)
        if swap:
            for copy in swap_hid[0]:
                copy.start()
        to_chip.wait_recv()
        onward.start()
        onward.wait_recv()
        if swap:
            done = 0
            for copy, (at, size) in zip(swap_hid[1], hid_cuts, strict=True):
                units_of(second_at, done, (at + size) // 128)
                done = (at + size) // 128
                copy.start()
            for copy in (swap_n2, *swap_gg):
                copy.start()
        else:
            units_of(second_at, 0, blocks)
            store(r.x_n2, r.n2_out)
            store(r.hid, r.hid_out)
            store(r.gg, r.gg_out)
            store(r.att_low, r.low_out)
        for copy in (to_chip, to_core, onward):
            copy.wait_send()

        store_copy(0).wait()
        start_sum(0, None, lambda n: dot_t(r.gg[...], wgu[aligned(n, 256), :]))

    def first_half(wgu):
        bf = lambda *shape: pltpu.VMEM(shape, bf16)
        pl.run_scoped(
            functools.partial(attention, wgu),
            raw=bf(4, 128, 2, units),
            wq=bf(width, heads_width),
            wkv=bf(width, 128),
            keys=bf(2, rows, 128),
            vals_t=bf(64, rows),
            bias=pltpu.VMEM((rows, rows), f32),
        )
        pl.run_scoped(
            functools.partial(feed_forward, wgu),
            g=bf(rows, width),
            gh=pltpu.VMEM((rows, units), f32),
            wdown=bf(units, width),
        )

    load_wout = load(r.wout_hbm, r.wout)
    load_x_own = load(r.x_hbm.at[mine, :], r.x_own)
    load_g_own = load(r.g_hbm.at[mine, :], r.g_own)
    pl.run_scoped(first_half, pltpu.VMEM((width, 2 * units), bf16))

    def second_half(**scoped):
        vars(r).update(scoped)

        def tile_down(n):
            slot = turn_of(n, 3)
            return pltpu.make_async_copy(
                r.wdown_hbm.at[:, aligned(n, 256)], r.w_cols.at[slot], r.w_cols_sem.at[slot]
            )

        def tile_qkv(n):
            slot = turn_of(n, 3)
            at = aligned(n, 256)
            copies = (
                pltpu.make_async_copy(
                    r.wq_hbm.at[at], r.w_rows.at[slot, :, 0:heads_width], r.w_rows_sem.at[slot]
                ),
                pltpu.make_async_copy(
                    r.wkv_hbm.at[at],
                    r.w_rows.at[slot, :, heads_width : heads_width + 128],
                    r.w_kv_sem.at[slot],
                ),
            )
            return types.SimpleNamespace(
                start=lambda: [copy.start() for copy in copies],
                wait=lambda: [copy.wait() for copy in copies],
            )

        def back_through_norm(b, values, gain_ref, gain_row, emit):
            square = jnp.zeros((quarter, 1), f32)
            inner = jnp.zeros((quarter, 1), f32)
            for c in range(chunks):
                at = slice(c * span, (c + 1) * span)
                v = values[:, at].astype(f32)
                square = square + jnp.sum(v * v, -1, keepdims=True)
                inner = inner + jnp.sum(r.own_fin[b, c] * gain_ref[:, at] * v, -1, keepdims=True)
            inverse = lax.rsqrt(square / width + epsilon)
            slope = inner / width * (inverse * inverse * inverse)
            for c in range(chunks):
                at = slice(c * span, (c + 1) * span)
                v = values[:, at].astype(f32)
                dn = r.own_fin[b, c]
                r.gain_sum[0, gain_row : gain_row + 1, at] = jnp.sum(
                    dn * v * inverse, 0, keepdims=True
                )
                emit(at, inverse * dn * gain_ref[:, at] - v * slope)

        if swap:
            is_end = (place == 0) | (place == 3)
            is_mid = jnp.logical_not(is_end)
            beside = place + 1 - 2 * lax.rem(place, 2)
            low_side = place < 2
            io_mate, across_mate = {"context": beside}, {"context": 3 - place}
            swap_gqkv = swap_copy(r.gqkv, r.gqkv_o)
            plan = []
            for i, (at, size) in enumerate(hid_cuts):
                cut = (r.g_hbm.at[:, mine_cols], r.g_o) if i == 0 else None
                plan.append(
                    (cut, r.hid.at[:, at : at + size], r.hid_o.at[i], size,
                     r.dwdown_out.at[:, at : at + size])
                )
            for i, (at, size) in enumerate(gg_cuts):
                cut = (r.x_n2.at[:, mine_cols], r.n2_o) if i == 0 else None
                plan.append(
                    (cut, r.gg.at[:, at : at + size], r.gg_o.at[i], size,
                     r.dgu_out.at[:, at : at + size])
                )
            cut = (r.n1_gb.at[:, mine_cols], r.gb_o)
            plan.append((cut, r.att_low, r.att_o, heads_width, r.dwout_out))
            cut = (r.n1_out.at[:, mine_cols], r.n1_o)
            plan.append((cut, r.gqkv, r.gqkv_o, r.gqkv.shape[1], r.dwqkv_out))
            sets = r.stage.shape[0]
            last = len(plan) - 1
            first_gg = len(hid_cuts)

            def cut_loads(u):
                own, other = plan[u][0]
                return (
                    pltpu.make_async_copy(own, r.cut.at[0:rows], r.cut_sem.at[0]),
                    pltpu.make_async_copy(other, r.cut.at[rows : 2 * rows], r.cut_sem.at[1]),
                )

            def piece(ref, s, j, u):
                return ref.at[s, j, :, 0 : plan[u][3]]

            def line_copy(u, j, slot, mate):
                s = u % sets
                return remote(
                    piece(r.stage, s, j, u), piece(r.got, s, slot, u), r.line_send.at[s, j],
                    r.line_recv.at[s, slot], mate,
                )

            def result(u):
                return pltpu.make_async_copy(
                    r.sums.at[u % sets, :, 0 : plan[u][3]], plan[u][4], r.sums_sem.at[u % sets]
                )

            def prepare(u):
                s = u % sets
                own, other, width_u = plan[u][1], plan[u][2], plan[u][3]
                if u >= sets:
                    for j in range(3):
                        line_copy(u - sets, j, 0, io_mate).wait_send()
                    result(u - sets).wait()
                    pl.when(is_end)(lambda: pl.semaphore_wait(r.io_credit, 1))
                if plan[u][0] is not None:
                    for copy in cut_loads(u):
                        copy.wait()

                @pl.loop(0, 4)
                def _(j):
                    chunk = jnp.where(
                        j == 0,
                        jnp.where(low_side, 3, 0),
                        jnp.where(
                            j == 1, jnp.where(low_side, 2, 1), jnp.where(j == 2, beside, place)
                        ),
                    )
                    r.turned[...] = r.cut[:, aligned(chunk, 256)].astype(f32).T.astype(bf16)

                    def block(at):
                        term = dot(r.turned[:, 0:rows], own[:, at]) + dot(
                            r.turned[:, rows : 2 * rows], other[:, at]
                        )

                        @pl.when(j < 3)
                        def _():
                            r.stage[s, j, :, at] = term.astype(bf16)

                        @pl.when(j == 3)
                        def _():
                            r.sums[s, :, at] = term

                    @pl.loop(0, width_u // 256)
                    def _(tile):
                        block(aligned(tile, 256))

                    if width_u % 256:
                        block(slice(width_u - width_u % 256, width_u))

                    @pl.when((j < 3) & is_end)
                    def _():
                        line_copy(u, j, j, io_mate).start()

            def add_in(u, j, slot):
                width_u, s = plan[u][3], u % sets
                line_copy(u, 0, slot, io_mate).wait_recv()

                @pl.loop(0, 4)
                def _(i):
                    at = aligned(i, 64)
                    total = r.stage[s, j, at, 0:width_u].astype(f32)
                    total = total + r.got[s, slot, at, 0:width_u].astype(f32)
                    r.stage[s, j, at, 0:width_u] = total.astype(bf16)

            def pass_on(u, step):
                @pl.when(is_mid)
                def _():
                    if step < 2:
                        add_in(u, step, step)
                        if u >= sets and step == 0:
                            pl.semaphore_wait(r.across_credit, 1)
                        line_copy(u, step, 3 + step, across_mate).start()
                    else:
                        add_in(u, 2, 3)
                        if u >= sets:
                            pl.semaphore_wait(r.io_credit, 1)
                        line_copy(u, 2, 0, io_mate).start()

            def complete(u):
                width_u, s = plan[u][3], u % sets

                def take(slots):
                    for slot in slots:
                        line_copy(u, 0, slot, io_mate).wait_recv()

                    @pl.loop(0, 4)
                    def _(i):
                        at = aligned(i, 64)
                        total = r.sums[s, at, 0:width_u]
                        for slot in slots:
                            total = total + r.got[s, slot, at, 0:width_u].astype(f32)
                        r.sums[s, at, 0:width_u] = total

                @pl.when(is_end)
                def _():
                    take((0,))

                @pl.when(is_mid)
                def _():
                    take((2, 4))

                result(u).start()
                if u + sets <= last:
                    pl.semaphore_signal(r.io_credit, inc=1, device_id=io_mate, device_id_type=MESH)

                    @pl.when(is_mid)
                    def _():
                        pl.semaphore_signal(
                            r.across_credit, inc=1, device_id=across_mate, device_id_type=MESH
                        )

            swap_g.wait_recv()
            for copy in cut_loads(0):
                copy.start()
        for n in range(3):
            tile_down(n).start()
            tile_qkv(n).start()
        r.gain_sum[...] = jnp.zeros_like(r.gain_sum)

        if swap:
            swap_hid[0][0].wait_recv()
            swap_hid[1][0].wait_recv()
            prepare(0)
        finish_sum(0)
        load_g_own.wait()
        for i in range(1, len(stores)):
            store_copy(i).wait()

        def keep_resid(at, grad):
            total = r.g_own[:, at].astype(f32) + grad
            r.grad_resid[:, at] = total
            r.n1_gb[mine, at] = total.astype(bf16)

        back_through_norm(0, r.resid, r.gain_two, 1, keep_resid)
        gb_chip, gb_core, gb_onward = gather(0, r.n1_gb.at[mine, :], r.n1_gb)
        gb_chip.start()
        gb_core.start()
        if swap:
            swap_gb.start()
        start_sum(1, tile_down, lambda n: dot(r.hid[...], r.w_cols[turn_of(n, 3)]), False)
        for c in range(chunks):
            x_copy(1, c).start()
        if swap:
            pass_on(0, 0)
            swap_hid[0][1].wait_recv()
            swap_hid[1][1].wait_recv()
            prepare(1)
            pass_on(0, 1)
        gb_chip.wait_recv()
        gb_onward.start()
        if swap:
            swap_n2.wait_recv()
            n2_chip, n2_core, n2_onward = gather(3, r.n2_o.at[mine, :], r.n2_o)
            n2_chip.start()
            n2_core.start()
        gb_core.wait_recv()
        gb_onward.wait_recv()
        if swap:
            swap_low.wait_recv()
            late = pltpu.make_async_copy(r.low_o, r.att_o, r.late_sem)
            late.start()
        else:
            late = pltpu.make_async_copy(r.n1_gb, r.gb_out, r.late_sem)
            late.start()

        for i in range(heads_width // 256):
            at = slice(i * 256, i * 256 + 256)
            r.ga[:, at] = dot_t(r.n1_gb[...], r.wout[at, :]).astype(bf16)

        @pl.loop(0, heads_width // 128)
        def _(pair):
            at = aligned(pair, 128)
            product = r.ga[:, at].astype(f32).T * r.att[at, :]
            for e in range(2):
                r.delta[pair * 2 + e] = jnp.sum(product[64 * e : 64 * e + 64], 0, keepdims=True)

        if swap:
            pass_on(0, 2)

        r.dq[...] = jnp.zeros_like(r.dq)

        def back_block(k, first):
            mask(r.bias, k, first)
            block = r.kv[k].astype(f32)
            rolled = pltpu.roll(block, 64, 1)
            pad_keys(r.keys, block)
            r.vals[0] = jnp.where(key_lane, rolled, 0.0).astype(bf16)
            r.vals[1] = jnp.where(key_lane, 0.0, block).astype(bf16)
            r.keys_t[...] = block.T[:64].astype(bf16)
            r.dk[...] = jnp.zeros_like(r.dk)
            r.dv[...] = jnp.zeros_like(r.dv)

            @pl.loop(0, heads_width // 128)
            def _(pair):
                pair_q = r.q[:, aligned(pair, 128)]
                pair_ga = r.ga[:, aligned(pair, 128)]
                for e in range(2):
                    head = pair * 2 + e
                    probs = jnp.exp2(dot_t(r.keys[e], pair_q) + r.bias[...] - r.lse[head])
                    grad_probs = dot_t(r.vals[e], pair_ga)
                    grad_scores = (probs * (grad_probs - r.delta[head])).astype(bf16)
                    r.dv[e] += dot(probs.astype(bf16), pair_ga)
                    r.dk[e] += dot(grad_scores, pair_q)
                    r.dq[aligned(head, 64), :] += dot(r.keys_t[...], grad_scores)

            return jnp.where(
                key_lane,
                (r.dk[0] + pltpu.roll(r.dk[1], 64, 1)) * (1.0 / log2_e),
                r.dv[1] + pltpu.roll(r.dv[0], 64, 1),
            )

        def dkv_copy(k, mate):
            return remote(
                r.stage_kv.at[k], r.got_kv.at[k], r.dkv_send.at[k], r.dkv_recv.at[k],
                {"context": mate},
            )

        @pl.loop(0, place)
        def _(i):
            k = place - i
            r.stage_kv[k] = back_block(k, False).astype(bf16)
            dkv_copy(k, i).start()

        r.dkv[...] = back_block(0, True)
        if swap:
            pass_on(1, 0)
            pass_on(1, 1)
            n2_chip.wait_recv()
            n2_onward.start()
            n2_core.wait_recv()
            n2_onward.wait_recv()
            for copy in cut_loads(first_gg):
                copy.start()
            swap_gg[0].wait_recv()
            prepare(2)
            complete(0)

        @pl.loop(0, heads_width // 128)
        def _(pair):
            at = aligned(pair, 128)
            turned = turn(r.dq[at, :].T * 0.125, r.cos[...], -r.sin[...])
            r.gqkv[:, at] = turned.astype(bf16)

        for k in (1, 2, 3):

            @pl.when(place + k < 4)
            def _():
                dkv_copy(k, 0).wait_recv()
                r.dkv[...] += r.got_kv[k].astype(f32)

        r.gqkv[:, heads_width : heads_width + 128] = turn(
            r.dkv[...], jnp.where(key_lane, r.cos[...], 1.0), jnp.where(key_lane, -r.sin[...], 0.0)
        ).astype(bf16)
        if swap:
            swap_gqkv.start()
            swap_n1.start()
            pass_on(1, 2)
        else:
            gqkv_store = pltpu.make_async_copy(r.gqkv, r.gqkv_out, r.cut_sem.at[1])
            gqkv_store.start()

        start_sum(0, tile_qkv, lambda n: dot_t(r.gqkv[...], r.w_rows[turn_of(n, 3)]))
        if swap:
            swap_gg[1].wait_recv()
            prepare(3)
            complete(1)
            pass_on(2, 0)

        finish_sum(0)

        def keep_tokens(at, grad):
            r.tokens_own[:, at] = (r.grad_resid[:, at] + grad).astype(bf16)

        back_through_norm(0, r.x_own, r.gain_one, 0, keep_tokens)
        tokens_chip, tokens_core, tokens_onward = gather(2, r.tokens_own, r.tokens_out)
        tokens_store = pltpu.make_async_copy(
            r.tokens_own, r.tokens_out.at[mine, :], r.out_sem.at[1]
        )
        for copy in (tokens_chip, tokens_core, tokens_store):
            copy.start()
        if swap:
            pass_on(2, 1)
            pass_on(2, 2)
            swap_gg[2].wait_recv()
            prepare(4)

        finish_sum(1)
        for c in range(chunks):
            at = slice(c * span, (c + 1) * span)
            r.mixed_own[:, at] = (r.resid[:, at] + r.own_fin[1, c]).astype(bf16)
        mixed_chip, mixed_core, mixed_onward = gather(1, r.mixed_own, r.mixed_out)
        mixed_store = pltpu.make_async_copy(r.mixed_own, r.mixed_out.at[mine, :], r.out_sem.at[0])
        for copy in (mixed_chip, mixed_core, mixed_store):
            copy.start()
        if swap:
            complete(2)
            pass_on(3, 0)
            swap_gg[3].wait_recv()
            prepare(5)
            swap_gb.wait_recv()
            gbo_chip, gbo_core, gbo_onward = gather(4, r.gb_o.at[mine, :], r.gb_o)
            gbo_chip.start()
            gbo_core.start()
            pass_on(3, 1)
            pass_on(3, 2)

        for i, mate in enumerate((core_mate, chip_mate)):
            copy = remote(
                r.gain_sum.at[i], r.gain_got.at[i], r.gain_send.at[i], r.gain_recv.at[i], mate
            )
            copy.start()
            copy.wait()
            r.gain_sum[i + 1] = r.gain_sum[i] + r.gain_got[i]
        if swap:
            copy = remote(
                r.gain_sum.at[2, :, theirs_cols], r.gain_half.at[0], r.gain_send.at[2],
                r.gain_recv.at[2], dp_mate,
            )
            copy.start()
            copy.wait()
            r.gain_half[1] = r.gain_sum[2, :, mine_cols] + r.gain_half[0]
            part = half // 4
            pieces = [
                remote(
                    r.gain_half.at[1, :, aligned(lax.rem(place + k, 4), part)],
                    r.gain_piece.at[k], r.gain_send.at[2 + k], r.gain_recv.at[2 + k],
                    {"context": lax.rem(place + k, 4)},
                )
                for k in (1, 2, 3)
            ]
            for copy in pieces:
                copy.start()
            complete(3)
        else:
            r.gains_out[...] = r.gain_sum[2]
        tokens_chip.wait_recv()
        tokens_onward.start()
        mixed_chip.wait_recv()
        mixed_onward.start()
        if swap:
            gbo_chip.wait_recv()
            gbo_onward.start()
            gbo_core.wait_recv()
            gbo_onward.wait_recv()
            for copy in cut_loads(last - 1):
                copy.start()
            late.wait()
            prepare(6)
            swap_n1.wait_recv()
            for copy in cut_loads(last):
                copy.start()
            for step in range(3):
                pass_on(4, step)
            complete(4)
            swap_gqkv.wait_recv()
            prepare(7)
            for u in (5, 6, 7):
                for step in range(3):
                    pass_on(u, step)
                complete(u)
            for copy in pieces:
                copy.wait()
            r.gains_out[...] = (
                r.gain_half[1, :, aligned(place, part)]
                + r.gain_piece[1]
                + r.gain_piece[2]
                + r.gain_piece[3]
            )

        for copy in (mixed_core, mixed_onward, tokens_core, tokens_onward):
            copy.wait_recv()
        for copy in (
            gb_chip, gb_core, gb_onward, mixed_chip, mixed_core, mixed_onward, tokens_chip,
            tokens_core, tokens_onward,
        ):
            copy.wait_send()
        mixed_store.wait()
        tokens_store.wait()
        for k in (1, 2, 3):
            pl.when(place >= k)(dkv_copy(k, 0).wait_send)
        if swap:
            for copy in (
                *swaps, n2_chip, n2_core, n2_onward, gbo_chip, gbo_core, gbo_onward
            ):
                copy.wait_send()
            for u in range(last + 1 - sets, last + 1):
                for j in range(3):
                    line_copy(u, j, 0, io_mate).wait_send()
                result(u).wait()
        else:
            late.wait()
            gqkv_store.wait()

    bf = lambda *shape: pltpu.VMEM(shape, bf16)
    fl = lambda *shape: pltpu.VMEM(shape, f32)
    qkv = heads_width + 128
    scoped = {
        "w_rows": bf(3, 256, qkv),
        "w_cols": bf(3, units, 256),
        "bias": fl(rows, rows),
        "ga": bf(rows, heads_width),
        "delta": fl(heads_width // HD, 1, rows),
        "dq": fl(heads_width, rows),
        "keys": bf(2, rows, 128),
        "vals": bf(2, rows, 128),
        "keys_t": bf(HD, rows),
        "dk": fl(2, rows, 128),
        "dv": fl(2, rows, 128),
        "dkv": fl(rows, 128),
        "stage_kv": bf(4, rows, 128),
        "gqkv": bf(rows, qkv),
        "grad_resid": fl(quarter, width),
        "mixed_own": bf(quarter, width),
        "tokens_own": bf(quarter, width),
    }
    if swap:
        scoped |= {
            "att_o": bf(rows, heads_width),
            "cut": bf(2 * rows, width // 2),
            "turned": bf(256, 2 * rows),
            "stage": bf(r.got.shape[0], 3, width // 8, lead),
            "sums": fl(r.got.shape[0], width // 8, lead),
        }
    pl.run_scoped(second_half, **scoped)


def layer(swap, inputs, rows, width, units, heads):
    bf16, f32 = jnp.bfloat16, jnp.float32
    quarter = rows // 4
    chunks = 4
    span = width // chunks
    wide = heads * HD
    qkv = wide + 2 * HD
    lead, sets = 768, 3
    outs = {
        "mixed_out": ((rows, width), bf16),
        "tokens_out": ((rows, width), bf16),
        "gains_out": ((8, width // 8 if swap else width), f32),
        "n1_out": ((rows, width), bf16),
    }
    if swap:
        outs |= {
            "dwdown_out": ((width // 8, units), f32),
            "dgu_out": ((width // 8, 2 * units), f32),
            "dwout_out": ((width // 8, wide), f32),
            "dwqkv_out": ((width // 8, qkv), f32),
            "g_o": ((rows, width // 2), bf16),
            "low_o": ((rows, wide), bf16),
            "n2_o": ((rows, width // 2), bf16),
            "gb_o": ((rows, width // 2), bf16),
            "n1_o": ((rows, width // 2), bf16),
        }
    else:
        outs |= {
            "gb_out": ((rows, width), bf16),
            "gqkv_out": ((rows, qkv), bf16),
            "n2_out": ((rows, width), bf16),
            "hid_out": ((rows, units), bf16),
            "gg_out": ((rows, 2 * units), bf16),
            "low_out": ((rows, wide), bf16),
        }
    scratch = {
        "x_n2": ((rows, width), bf16),
        "n1_gb": ((rows, width), bf16),
        "wout": ((wide, width), bf16),
        "q": ((rows, wide), bf16),
        "kv": ((4, rows, 2 * HD), bf16),
        "att": ((wide, rows), f32),
        "att_low": ((rows, wide), bf16),
        "lse": ((heads, 1, rows), f32),
        "run_sum": ((heads, 1, rows), f32),
        "cos": ((rows, 2 * HD), f32),
        "sin": ((rows, 2 * HD), f32),
        "resid": ((quarter, width), f32),
        "g_own": ((quarter, width), bf16),
        "x_own": ((quarter, width), bf16),
        "hid": ((rows, units), bf16),
        "gg": ((rows, 2 * units), bf16),
        "tmp": ((rows, 256), f32),
        "stage_core": ((2, chunks, 2, quarter, span), bf16),
        "got_core": ((2, chunks, 2, quarter, span), bf16),
        "own_fwd": ((chunks, quarter, span), f32),
        "own_fin": ((2, chunks, quarter, span), f32),
        "stage_x": ((2, chunks, quarter, span), bf16),
        "got_x": ((2, chunks, quarter, span), bf16),
        "got_kv": ((4, rows, 2 * HD), bf16),
        "gain_sum": ((3, 8, width), f32),
        "gain_got": ((2, 8, width), f32),
    }
    if swap:
        scratch |= {
            "hid_o": ((-(-units // lead), rows, lead), bf16),
            "gg_o": ((-(-2 * units // lead), rows, lead), bf16),
            "gqkv_o": ((rows, qkv), bf16),
            "got": ((sets, 5, width // 8, lead), bf16),
            "gain_half": ((2, 8, width // 2), f32),
            "gain_piece": ((4, 8, width // 8), f32),
        }
    sems = {
        "load_sem": (8,),
        "store_sem": (5,),
        "raw_sem": (4,),
        "w_rows_sem": (3,),
        "w_cols_sem": (3,),
        "w_kv_sem": (3,),
        "core_send": (2, chunks),
        "core_recv": (2, chunks),
        "x_send": (2, chunks),
        "x_recv": (2, chunks),
        "ag_send": (6, 3),
        "ag_recv": (6, 3),
        "kv_send": (4,),
        "kv_recv": (4,),
        "dkv_send": (4,),
        "dkv_recv": (4,),
        "gain_send": (6,),
        "gain_recv": (6,),
        "out_sem": (2,),
        "cut_sem": (2,),
        "late_sem": (),
    }
    if swap:
        sems |= {
            "dp_send": (16,),
            "dp_recv": (16,),
            "line_send": (sets, 3),
            "line_recv": (sets, 5),
            "sums_sem": (sets,),
        }
    credits = ["io_credit", "across_credit"] if swap else []
    names = [*inputs, *outs, *scratch, *sems, *credits]
    anywhere = pl.BlockSpec(memory_space=pl.ANY)
    inside = pl.BlockSpec(memory_space=pltpu.VMEM)
    results = pl.pallas_call(
        functools.partial(layer_kernel, names, swap),
        out_shape=[jax.ShapeDtypeStruct(*out) for out in outs.values()],
        in_specs=[anywhere if name.endswith("_hbm") else inside for name in inputs],
        out_specs=[inside if name == "gains_out" else anywhere for name in outs],
        scratch_shapes=[
            *(pltpu.VMEM(*shape) for shape in scratch.values()),
            *(pltpu.SemaphoreType.DMA(shape) for shape in sems.values()),
            *(pltpu.SemaphoreType.REGULAR for _ in credits),
        ],
        compiler_params=pltpu.CompilerParams(
            collective_id=0, has_side_effects=True, vmem_limit_bytes=63 * MIB
        ),
        name="layer",
    )(*inputs.values())
    return dict(zip(outs, results, strict=True))


def finish_kernel(
    down_hbm, gateup_hbm, out_hbm, qkv_hbm, tokens_hbm, mixed_hbm, gains,
    down_o, gateup_o, out_o, q_o, kv_o, tokens_o, mixed_o, gain_one_o, gain_two_o,
    down, gateup, out, qkv, tokens, mixed, down_t, gateup_t, out_t, kv_t, tokens_t,
    load_sem, store_sem,
):
    wide = q_o.shape[1]
    parts = 4
    loads, stores = [], []

    def load(src, dst):
        copy = pltpu.make_async_copy(src, dst, load_sem.at[len(loads)])
        copy.start()
        loads.append(copy)
        return copy

    def store(src, dst):
        copy = pltpu.make_async_copy(src, dst, store_sem.at[len(stores)])
        copy.start()
        stores.append(copy)

    def piece(ref, i):
        size = ref.shape[0] // parts
        return ref.at[i * size : (i + 1) * size]

    gain_one_o[...] = gains[0:1, :]
    gain_two_o[...] = gains[1:2, :]
    token_loads = [load(piece(tokens_hbm, i), piece(tokens, i)) for i in range(parts)]
    gateup_loads = [load(piece(gateup_hbm, i), piece(gateup, i)) for i in range(parts)]
    load_mixed = load(mixed_hbm, mixed)
    load_down = load(down_hbm, down)
    load_qkv = load(qkv_hbm, qkv)
    load_out = load(out_hbm, out)
    for i in range(parts):
        token_loads[i].wait()
        piece(tokens_t, i)[...] = piece(tokens, i)[...].astype(jnp.float32)
        store(piece(tokens_t, i), piece(tokens_o, i))
    for i in range(parts):
        gateup_loads[i].wait()
        values, target = piece(gateup, i), piece(gateup_t, i)
        for b in range(gateup.shape[1] // 256):
            at = slice(b * 128, b * 128 + 128)
            target[:, 0, at] = values[:, b * 256 : b * 256 + 128]
            target[:, 1, at] = values[:, b * 256 + 128 : b * 256 + 256]
        store(target, piece(gateup_o, i))
    load_mixed.wait()
    store(mixed, mixed_o)
    load_down.wait()
    for i in range(down.shape[1] // 128):
        at = slice(i * 128, i * 128 + 128)
        down_t[at, :] = down[:, at].T
    store(down_t, down_o)
    load_qkv.wait()
    store(qkv.at[:, 0:wide], q_o)
    kv_t[:, 0, :] = qkv[:, wide:]
    store(kv_t, kv_o)
    load_out.wait()
    for i in range(wide // 128):
        at = slice(i * 128, i * 128 + 128)
        out_t[at, :] = out[:, at].T
    store(out_t, out_o)
    for copy in stores:
        copy.wait()


def finish(down, gateup, out, qkv, tokens, mixed, gains):
    depth, units = down.shape
    wide = out.shape[1]
    rows, width = tokens.shape
    bf16, f32 = jnp.bfloat16, jnp.float32
    outs = [
        ((units, depth), f32),
        ((depth, 2, units), f32),
        ((wide, depth), f32),
        ((depth, wide), f32),
        ((depth, 1, 2 * HD), f32),
        ((rows, width), f32),
        ((rows, width), bf16),
        ((1, depth), f32),
        ((1, depth), f32),
    ]
    scratch = [
        *((array.shape, array.dtype) for array in (down, gateup, out, qkv, tokens, mixed)),
        *outs[:3],
        *outs[4:6],
    ]
    anywhere = pl.BlockSpec(memory_space=pl.ANY)
    inside = pl.BlockSpec(memory_space=pltpu.VMEM)
    return pl.pallas_call(
        finish_kernel,
        out_shape=[jax.ShapeDtypeStruct(*entry) for entry in outs],
        in_specs=[*[anywhere] * 6, inside],
        out_specs=[*[anywhere] * 7, inside, inside],
        scratch_shapes=[
            *(pltpu.VMEM(*entry) for entry in scratch),
            pltpu.SemaphoreType.DMA((12,)),
            pltpu.SemaphoreType.DMA((13,)),
        ],
        compiler_params=pltpu.CompilerParams(vmem_limit_bytes=62 * MIB),
        name="finish",
    )(down, gateup, out, qkv, tokens, mixed, gains)


def pick(array, index, axis):
    return lax.dynamic_index_in_dim(array, index, axis, keepdims=False)


def line_sum(part):
    place = lax.axis_index("context")
    order = jnp.array([[3, 2, 1, 0], [3, 2, 0, 1], [0, 1, 3, 2], [0, 1, 2, 3]], jnp.int32)[place]
    first, second, third, own = (part(order[i]) for i in range(4))

    def inward(array):
        return lax.ppermute(array.astype(jnp.bfloat16), "context", [(0, 1), (3, 2)])

    def across(array):
        return lax.ppermute(array.astype(jnp.bfloat16), "context", [(1, 2), (2, 1)])

    def outward(array):
        return lax.ppermute(array.astype(jnp.bfloat16), "context", [(1, 0), (2, 3)])

    in_one, in_two, in_three = inward(first), inward(second), inward(third)
    over_two = across(first + in_one.astype(jnp.float32))
    over_three = across(second + in_two.astype(jnp.float32))
    out_three = outward(third + over_two.astype(jnp.float32))
    return (
        own
        + in_three.astype(jnp.float32)
        + over_three.astype(jnp.float32)
        + out_three.astype(jnp.float32)
    )


def weight_grad(left, right, axis):
    whole = lax.dot_general(
        left, right, (((0,), (0,)), ((), ())), preferred_element_type=jnp.float32
    )
    mine = lax.psum_scatter(
        whole.astype(jnp.bfloat16), "dp", scatter_dimension=axis, tiled=True
    )
    step = mine.shape[axis] // 4
    return line_sum(
        lambda chunk: lax.dynamic_slice_in_dim(mine, chunk * step, step, axis).astype(jnp.float32)
    )


def shards(
    tokens, segments, gain_one, w_query, w_keyval, w_out, gain_two, w_gateup, w_down, cotangent
):
    num_seqs, tok_count, model_width = tokens.shape
    heads_kv = w_keyval.shape[1]
    width_q = w_query.shape[1]
    units = w_down.shape[0]
    swap = lax.axis_size("dp") == 2
    freqs = 10000.0 ** (-(np.arange(HD // 2, dtype=np.float32) * 2.0) / HD)
    g = cotangent.reshape(tok_count, model_width)
    inputs = {
        "seg": segments,
        "freqs": jnp.asarray(freqs.astype(np.float32)[:, None]),
        "gain_one": gain_one[None],
        "gain_two": gain_two[None],
        "x_hbm": tokens.reshape(tok_count, model_width),
        "g_hbm": g,
        "wq_hbm": w_query,
        "wkv_hbm": w_keyval.reshape(model_width, 2 * HD),
        "wout_hbm": w_out,
        "wgateup_hbm": w_gateup,
        "wdown_hbm": w_down,
    }
    out = layer(swap, inputs, tok_count, model_width, units, width_q // HD)
    if swap:
        sent_wdown, sent_gateup, sent_wout, sent_wq, sent_wkv, grad_tokens, mixed, *gains = finish(
            *(out[name] for name in ("dwdown_out", "dgu_out", "dwout_out", "dwqkv_out")),
            *(out[name] for name in ("tokens_out", "mixed_out", "gains_out")),
        )
    else:
        gains = lax.psum_scatter(
            out["gains_out"], ("dp", "context"), scatter_dimension=1, tiled=True
        )
        sent_wdown = weight_grad(out["hid_out"], g, 1)
        sent_gateup = weight_grad(out["n2_out"], out["gg_out"], 0)
        sent_wout = weight_grad(out["low_out"], out["gb_out"], 1)
        sent_wqkv = weight_grad(out["n1_out"], out["gqkv_out"], 0)
        sent_wq, sent_wkv = sent_wqkv[:, :width_q], sent_wqkv[:, width_q:]
        sent_gateup = sent_gateup.reshape(-1, units // 128, 2, 128).transpose(0, 2, 1, 3)
        grad_tokens, mixed = out["tokens_out"].astype(jnp.float32), out["mixed_out"]
    return (
        mixed.reshape(tokens.shape),
        grad_tokens.reshape(tokens.shape),
        gains[0].reshape(-1),
        sent_wq,
        sent_wkv.reshape(-1, heads_kv, 2 * HD),
        sent_wout,
        gains[1].reshape(-1),
        sent_gateup.reshape(-1, 2, units),
        sent_wdown,
    )


def solution(mesh):
    return jax.shard_map(
        shards,
        mesh=mesh,
        in_specs=(
            P("dp", "context", None),
            P("dp", "context"),
            P(),
            P(None, "tensor"),
            P(None, "tensor", None),
            P("tensor", None),
            P(),
            P(None, None, "tensor"),
            P("tensor", None),
            P("dp", "context", None),
        ),
        out_specs=(
            P("dp", "context", None),
            P("dp", "context", None),
            P(("dp", "context")),
            P(("dp", "context"), "tensor"),
            P(("dp", "context"), "tensor", None),
            P("tensor", ("dp", "context")),
            P(("dp", "context")),
            P(("dp", "context"), None, "tensor"),
            P("tensor", ("dp", "context")),
        ),
        check_vma=False,
    )
```

time: 1020 us -> 288 us (0.28); the launches traced: 1000 us -> 286 us
  waiting for transfers between devices: 639 us -> 0 us
  Pallas kernels: 0 us -> 285 us
  matrix products: 146 us -> 0 us
  local copies, waits for them, and re-layouts: 69 us -> 0 us
  other arithmetic: 54.8 us -> 0 us
  blocking collectives: 43.7 us -> 0 us
  loops' own time: 31.9 us -> 0 us
  between operations: 15.5 us -> 0.83 us
    reduce_scatter x6 -> x0, waiting for transfers between devices: 449 us -> none  [the longest x1 193 us: shards(): lax.psum_scatter(grad_wgateup.astype(jnp.bfloat16), ('dp', 'context'), sc...]
    pallas_call x0 -> x2, Pallas kernels: none -> 285 us  [the longest x1 276 us: layer(): pl.pallas_call(functools.partial(layer_kernel, names, swap), out_shape=[j...]
    psum x3 -> x0, waiting for transfers between devices: 191 us -> none  [the longest x1 87.3 us: shards(): lax.psum(down_part.astype(jnp.bfloat16), 'tensor').astype(jnp.float32)]
    dot_general x43 -> x0, matrix products: 146 us -> none  [the longest x4 19.2 us: output_compute(): jnp.einsum('kgqp,pkd->qkgd', probs, key_blk[..., head_dim:], preferred_el...]
    slice x48 -> x0, local copies, waits for them, and re-layouts: 34.4 us -> none  [the longest x32 22.9 us: useful(): return (index_blk[0] <= query_index[-1]) & (seg_blk[-1] >= query_seg[0])]
    another operation x15 -> x0, loops' own time: 31.9 us -> none  [the longest x1 10.5 us: attend(): lax.scan(stats_step, (start_max, start_sum), (key_blocks, seg_blocks, ind...]
    all_gather x2 -> x0, blocking collectives: 25.9 us -> none  [the longest x1 15.2 us: shards(): lax.all_gather(rot_kv.reshape(num_seqs, tok_count, heads_kv, 2 * head_dim...]
    reduce_sum x9 -> x0, other arithmetic: 21.3 us -> none  [the longest x4 8.12 us: stats_compute(): jnp.sum(weights, -1)]
  transfers between devices with their start and end apart: 9 -> 0, of which waited for: 9 -> 0; matrix products, arithmetic and copies ran while one was open for 6% -> 0% of each run, Pallas kernels for 0% -> 0%
where the time goes in v4:
time: 288 us; the launch traced here: 286 us
  Pallas kernels  285 us (99%)
    pallas_call x1, Pallas kernels, layer(): pl.pallas_call(functools.partial(layer_kernel, names, swap), out_shape=[j...  276 us
    pallas_call x1, Pallas kernels, finish(): pl.pallas_call(finish_kernel, out_shape=[jax.ShapeDtypeStruct(*entry) for...  9.35 us

profile of v4, /device:TPU:24, one launch (start us, length us, event | category | flops | bytes accessed | tf_op | source)
XLA Modules:
  0.0 285.8 jit_solution(3103933149939906904)
XLA Ops:
  0.6 275.6 %layer.1 = (bf16[512,2048]{1,0:T(8,128)(2,1)}, bf16[512,2048]{1,0:T(8,128)(2,1)}, f32[8,256]{1,0:T(8,128)}, bf16[512,2048]{1,0:T(8,128)(2,1)}, f32[256,1408]{1,0...) custom-call(s32[1,512]{1,0:T(1,128)} %refs_0_.1, ...), custom_call_target="tpu_custom_call" | custom-call | tf_op jit(solution)/shard_map/layer/pallas_call | solution.py:1082
  276.2 9.3 %finish.1 = (f32[1408,256]{1,0:T(8,128)}, f32[256,2,1408]{2,1,0:T(2,128)}, f32[512,256]{1,0:T(8,128)}, f32[256,512]{1,0:T(8,128)}, f32[256,1,128]{2,1,0:T(1,128)...) custom-call(f32[256,1408]{1,0:T(8,128)} %get-tuple-element.25.down_hbm, ...), custom_call_target="tpu_custom_call" | custom-call | tf_op jit(solution)/shard_map/finish/pallas_call | solution.py:1188

commit v5 on v4

--- a/solution.py
+++ b/solution.py
@@ -89,6 +89,9 @@
         mates.append(dp_mate)
     mine = aligned(tensor, quarter)
     key_lane = lanes((rows, 128)) < 64
+    qkv = heads_width + 128
+    bf = lambda *shape: pltpu.VMEM(shape, bf16)
+    fl = lambda *shape: pltpu.VMEM(shape, f32)
 
     barrier = pltpu.get_barrier_semaphore()
     for mate in mates:
@@ -125,29 +128,66 @@
     if swap:
         half = width // 2
         theirs_cols, mine_cols = aligned(1 - side, half), aligned(side, half)
-        lead = r.got.shape[3]
-
-        def cuts(total):
-            return [(at, min(lead, total - at)) for at in range(0, total, lead)]
-
-        hid_cuts, gg_cuts = cuts(units), cuts(2 * units)
-        row_halves = [aligned(chip, rows // 2), aligned(1 - chip, rows // 2)]
-        swap_g = swap_copy(r.g_hbm.at[:, theirs_cols], r.g_o)
+        swap_n1 = swap_copy(r.n1_gb.at[:, theirs_cols], r.n1_o)
         swap_low = swap_copy(r.att_low, r.low_o)
-        swap_hid = [
-            [
-                swap_copy(r.hid.at[at_rows, at : at + size], r.hid_o.at[i, at_rows, 0:size])
-                for i, (at, size) in enumerate(hid_cuts)
-            ]
-            for at_rows in row_halves
-        ]
-        swap_n2 = swap_copy(r.x_n2.at[mine, theirs_cols], r.n2_o.at[mine, :])
-        swap_gg = [
-            swap_copy(r.gg.at[:, at : at + size], r.gg_o.at[i, :, 0:size])
-            for i, (at, size) in enumerate(gg_cuts)
-        ]
-        swap_gb = swap_copy(r.n1_gb.at[mine, theirs_cols], r.gb_o.at[mine, :])
-        swap_n1 = swap_copy(r.n1_out.at[:, theirs_cols], r.n1_o)
+        swap_gb = swap_copy(r.n1_gb.at[:, theirs_cols], r.gb_o)
+        swap_gqkv = swap_copy(r.gqkv, r.gqkv_o)
+
+    low_side = place < 2
+    beside = place + 1 - 2 * lax.rem(place, 2)
+    peers = (beside, jnp.where(low_side, 2, 1), jnp.where(low_side, 3, 0))
+    other_quarter = aligned(chip_mate["tensor"], quarter)
+
+    def line_parts(i):
+        return (mine, other_quarter) if i == 0 else (mine,)
+
+    def line_sent(a, i, part):
+        src, dst = ((r.g_hbm, r.g_z), (r.n2_z.at[place], r.n2_z))[a]
+        step = lax.rem(peers[i] - place + 4, 4)
+        at = line_parts(i)[part]
+        return remote(
+            src.at[at, :], dst.at[place, at, :], r.line_send.at[a, step, part],
+            r.line_recv.at[a, step, part], {"context": peers[i]},
+        )
+
+    def line_got(a, i, part):
+        dst = (r.g_z, r.n2_z)[a].at[peers[i], line_parts(i)[part], :]
+        step = lax.rem(place - peers[i] + 4, 4)
+        return remote(
+            dst, dst, r.line_send.at[a, step, part], r.line_recv.at[a, step, part],
+            {"context": peers[i]},
+        )
+
+    def spread(a, i):
+        block = (r.g_z, r.n2_z)[a].at[peers[i]]
+        slot = 4 + a * 3 + i
+        if i > 0:
+            return gather(slot, block.at[mine, :], block)
+        return tuple(
+            remote(
+                block.at[at, :], block.at[at, :], r.ag_send.at[slot, part],
+                r.ag_recv.at[slot, part], core_mate,
+            )
+            for part, at in enumerate(line_parts(0))
+        )
+
+    def spread_start(a, i):
+        copies = spread(a, i)
+        for part in range(len(line_parts(i))):
+            line_got(a, i, part).wait_recv()
+        for copy in copies[:2]:
+            copy.start()
+
+    def spread_onward(a, i):
+        if i > 0:
+            copies = spread(a, i)
+            copies[0].wait_recv()
+            copies[2].start()
+
+    def spread_wait(a, i):
+        copies = spread(a, i)
+        for copy in copies[1:] if i > 0 else copies:
+            copy.wait_recv()
 
     chunks = r.own_fin.shape[1]
     span = r.own_fin.shape[3]
@@ -163,7 +203,11 @@
             r.stage_x.at[b, c], r.got_x.at[b, c], r.x_send.at[b, c], r.x_recv.at[b, c], chip_mate
         )
 
-    def start_sum(b, tile, product, send=True):
+    def start_sum(b, tile, product, first=False):
+        if not first:
+            pl.semaphore_wait(r.core_credit, 1)
+            pl.semaphore_wait(r.x_credit, 1)
+
         def put(ref, index, at, value):
             ref[(*index, slice(None), at)] = value.astype(ref.dtype)
 
@@ -176,9 +220,9 @@
 
         def forward_chunk(c):
             core_copy(b, c).wait_recv()
-            r.stage_x[b, c] = (r.own_fwd[c] + r.got_core[b, c, 0].astype(f32)).astype(bf16)
-            if send:
-                x_copy(b, c).start()
+            total = r.own_fwd[c].astype(f32) + r.got_core[b, c, 0].astype(f32)
+            r.stage_x[b, c] = total.astype(bf16)
+            x_copy(b, c).start()
 
         @pl.loop(0, chunks)
         def _(c):
@@ -200,7 +244,7 @@
 
         forward_chunk(chunks - 1)
 
-    def finish_sum(b):
+    def finish_sum(b, last=False):
         for c in range(chunks):
             x_copy(b, c).wait_recv()
             r.own_fin[b, c] = (
@@ -209,6 +253,9 @@
         for c in range(chunks):
             core_copy(b, c).wait_send()
             x_copy(b, c).wait_send()
+        if not last:
+            pl.semaphore_signal(r.core_credit, inc=1, device_id=core_mate, device_id_type=MESH)
+            pl.semaphore_signal(r.x_credit, inc=1, device_id=chip_mate, device_id_type=MESH)
 
     def gather(i, src, dst):
         def copy(slot, src, owner, mate):
@@ -240,6 +287,11 @@
         return remote(
             r.kv.at[0], r.kv.at[k], r.kv_send.at[k], r.kv_recv.at[k],
             {"context": lax.rem(place + k, 4)},
+        )
+
+    def dkv_copy(k, mate):
+        return remote(
+            r.kv.at[k], r.got_kv.at[k], r.dkv_send.at[k], r.dkv_recv.at[k], {"context": mate}
         )
 
     def attention(wgu, raw, wq, wkv, keys, vals_t, bias):
@@ -283,7 +335,10 @@
         for k in (1, 2, 3):
             pl.when(place + k < 4)(kv_copy(k).start)
         if swap:
-            swap_g.start()
+            swap_n1.start()
+            for i in range(3):
+                for part in range(len(line_parts(i))):
+                    line_sent(0, i, part).start()
 
         load_wq.wait()
 
@@ -360,11 +415,13 @@
             at = aligned(pair, 128)
             r.att_low[:, at] = r.att[at, :].T.astype(bf16)
 
-    def feed_forward(wgu, g, gh, wdown):
+    def feed_forward(wgu, g, wdown, acc_gu, acc_down, t_n2, t_g):
+        gh = acc_down
+        r.t_n2 = t_n2
         load_g = load(r.g_hbm, g)
         load_wdown = load(r.wdown_hbm, wdown)
         load_wout.wait()
-        start_sum(0, None, lambda n: dot(r.att_low[...], r.wout[:, aligned(n, 256)]))
+        start_sum(0, None, lambda n: dot(r.att_low[...], r.wout[:, aligned(n, 256)]), first=True)
         if swap:
             swap_low.start()
 
@@ -386,55 +443,184 @@
             square = square + jnp.sum(part * part, -1, keepdims=True)
         inverse = lax.rsqrt(square / width + epsilon)
         r.x_n2[mine, :] = (r.resid[...] * inverse * r.gain_two[...]).astype(bf16)
-        to_chip, to_core, onward = gather(5, r.x_n2.at[mine, :], r.x_n2)
+        to_chip, to_core, onward = gather(3, r.x_n2.at[mine, :], r.x_n2)
         to_chip.start()
         to_core.start()
 
-        def units_of(at, first, last):
-            @pl.loop(first, last)
+        def own_to_line(part):
+            at = line_parts(0)[part]
+            return pltpu.make_async_copy(
+                r.x_n2.at[at, :], r.n2_z.at[place, at, :], r.own_sem.at[part]
+            )
+
+        if swap:
+            own_to_line(0).start()
+            own_to_line(0).wait()
+            for i in range(3):
+                line_sent(1, i, 0).start()
+
+        def activations(gate, up, grad):
+            sigmoid = 1.0 / (1.0 + jnp.exp(-gate))
+            active = gate * sigmoid
+            grad_gate = grad * up * (sigmoid * (1.0 + gate * (1.0 - sigmoid)))
+            both = jnp.concatenate([grad_gate, grad * active], 1)
+            return (active * up).astype(bf16), both.astype(bf16)
+
+        def units_of(at):
+            @pl.loop(0, units // 128)
             def _(b):
                 wide = dot(r.x_n2[at, :], wgu[:, aligned(b, 256)])
-                gate, up = wide[:, :128], wide[:, 128:]
-                grad = gh[at, aligned(b, 128)]
-                sigmoid = 1.0 / (1.0 + jnp.exp(-gate))
-                active = gate * sigmoid
-                r.hid[at, aligned(b, 128)] = (active * up).astype(bf16)
-                grad_gate = grad * up * (sigmoid * (1.0 + gate * (1.0 - sigmoid)))
-                both = jnp.concatenate([grad_gate, grad * active], 1).astype(bf16)
-                r.gg[at, aligned(b, 256)] = both
-
-        first_at, second_at = aligned(chip, 2 * quarter), aligned(1 - chip, 2 * quarter)
-        blocks = units // 128
+                hid, gg = activations(wide[:, :128], wide[:, 128:], gh[at, aligned(b, 128)])
+                r.hid[at, aligned(b, 128)] = hid
+                r.gg[at, aligned(b, 256)] = gg
+
         to_core.wait_recv()
-        units_of(first_at, 0, blocks)
-        if swap:
-            for copy in swap_hid[0]:
-                copy.start()
+        units_of(aligned(chip, 2 * quarter))
         to_chip.wait_recv()
         onward.start()
+        if swap:
+            own_to_line(1).start()
+            own_to_line(1).wait()
+            line_sent(1, 0, 1).start()
         onward.wait_recv()
-        if swap:
-            done = 0
-            for copy, (at, size) in zip(swap_hid[1], hid_cuts, strict=True):
-                units_of(second_at, done, (at + size) // 128)
-                done = (at + size) // 128
-                copy.start()
-            for copy in (swap_n2, *swap_gg):
-                copy.start()
-        else:
-            units_of(second_at, 0, blocks)
+        units_of(aligned(1 - chip, 2 * quarter))
+        if not swap:
             store(r.x_n2, r.n2_out)
             store(r.hid, r.hid_out)
             store(r.gg, r.gg_out)
             store(r.att_low, r.low_out)
         for copy in (to_chip, to_core, onward):
             copy.wait_send()
+        if swap:
+            spread_start(0, 1)
+
+        steps = [(at, min(256, units - at)) for at in range(0, units, 256)]
+        whole = units // 256
+
+        def each_step(body):
+            @pl.loop(0, whole)
+            def _(step):
+                body(pl.multiple_of(step * 256, 256), 256, step)
+
+            if units % 256:
+                body(whole * 256, units - whole * 256, whole)
+
+        def turn_block():
+            for t, ref in ((t_n2, r.x_n2), (t_g, g)):
+                for i, owner in enumerate((side, 1 - side)):
+                    columns = aligned(owner * 4 + place, 256)
+                    t[i * 256 : i * 256 + 256, :] = ref[:, columns].astype(f32).T.astype(bf16)
+
+        def own_block():
+            turn_block()
+
+            def body(offset, size, step):
+                gu, down = pl.ds(2 * offset, 2 * size), pl.ds(offset, size)
+                acc_gu[:, gu] = dot(t_n2[...], r.gg[:, gu])
+                acc_down[:, down] = dot(t_g[...], r.hid[:, down])
+
+            each_step(body)
+
+        def block_loads(i):
+            return (
+                pltpu.make_async_copy(r.n2_z.at[peers[i]], r.x_n2, r.block_sem.at[0]),
+                pltpu.make_async_copy(r.g_z.at[peers[i]], g, r.block_sem.at[1]),
+            )
+
+        def exchange(step, size):
+            offset = step * 256
+            gu, down = pl.ds(2 * offset, 2 * size), pl.ds(offset, size)
+            return tuple(
+                remote(
+                    ref.at[0:256, at], ref.at[256:512, at], r.side_send.at[step, i],
+                    r.side_recv.at[step, i], dp_mate,
+                )
+                for i, (ref, at) in enumerate(((r.gg, gu), (r.hid, down)))
+            )
+
+        def other_block(i, last=False):
+            for a in range(2):
+                spread_wait(a, i)
+            for copy in block_loads(i):
+                copy.start()
+            for copy in block_loads(i):
+                copy.wait()
+            turn_block()
+            if last:
+                pl.semaphore_wait(r.side_credit, 1)
+
+            def body(offset, size, step):
+                gu, down = pl.ds(2 * offset, 2 * size), pl.ds(offset, size)
+                wide = dot(r.x_n2[...], wgu[:, gu])
+                grad = dot_t(g[...], wdown[down, :])
+                parts = [
+                    activations(
+                        wide[:, 2 * q : 2 * q + 128],
+                        wide[:, 2 * q + 128 : 2 * q + 256],
+                        grad[:, q : q + 128],
+                    )
+                    for q in range(0, size, 128)
+                ]
+                hid = jnp.concatenate([part[0] for part in parts], 1)
+                gg = jnp.concatenate([part[1] for part in parts], 1)
+                acc_gu[:, gu] += dot(t_n2[...], gg)
+                acc_down[:, down] += dot(t_g[...], hid)
+                if last:
+                    r.gg[0:256, gu] = acc_gu[256:512, gu].astype(bf16)
+                    r.hid[0:256, down] = acc_down[256:512, down].astype(bf16)
+
+                    @pl.when(step < len(steps) - 1)
+                    def _():
+                        for copy in exchange(step, size):
+                            copy.start()
+
+            each_step(body)
+
+        def last_exchange():
+            for copy in exchange(len(steps) - 1, steps[-1][1]):
+                copy.start()
+
+        def own_share(first, stop):
+            for step in range(first, stop):
+                offset, size = steps[step]
+                for copy in exchange(step, size):
+                    copy.wait_recv()
+                gu, down = slice(2 * offset, 2 * (offset + size)), slice(offset, offset + size)
+                acc_gu[0:256, gu] += r.gg[256:512, gu].astype(f32)
+                acc_down[0:256, down] += r.hid[256:512, down].astype(f32)
+                for copy in share_stores(step, offset, size):
+                    copy.start()
+
+        def share_stores(step, offset, size):
+            gu, down = pl.ds(2 * offset, 2 * size), pl.ds(offset, size)
+            return (
+                pltpu.make_async_copy(
+                    acc_gu.at[0:256, gu], r.dgu_out.at[:, gu], r.share_sem.at[step, 0]
+                ),
+                pltpu.make_async_copy(
+                    acc_down.at[0:256, down], r.dwdown_out.at[:, down], r.share_sem.at[step, 1]
+                ),
+            )
+
+        def finish_shares():
+            for step, (offset, size) in enumerate(steps):
+                for copy in exchange(step, size):
+                    copy.wait_send()
+                for copy in share_stores(step, offset, size):
+                    copy.wait()
 
         store_copy(0).wait()
+        if swap:
+            swap_n1.wait_send()
         start_sum(0, None, lambda n: dot_t(r.gg[...], wgu[aligned(n, 256), :]))
+        if swap:
+            own_block()
+            for a in range(2):
+                spread_start(a, 0)
+        r.share_tools = (last_exchange, own_share, finish_shares, len(steps) - 1)
+        rest(wdown, other_block)
 
     def first_half(wgu):
-        bf = lambda *shape: pltpu.VMEM(shape, bf16)
         pl.run_scoped(
             functools.partial(attention, wgu),
             raw=bf(4, 128, 2, units),
@@ -447,269 +633,241 @@
         pl.run_scoped(
             functools.partial(feed_forward, wgu),
             g=bf(rows, width),
-            gh=pltpu.VMEM((rows, units), f32),
             wdown=bf(units, width),
-        )
-
-    load_wout = load(r.wout_hbm, r.wout)
-    load_x_own = load(r.x_hbm.at[mine, :], r.x_own)
-    load_g_own = load(r.g_hbm.at[mine, :], r.g_own)
-    pl.run_scoped(first_half, pltpu.VMEM((width, 2 * units), bf16))
-
-    def second_half(**scoped):
-        vars(r).update(scoped)
-
-        def tile_down(n):
-            slot = turn_of(n, 3)
+            acc_gu=pltpu.VMEM((rows, 2 * units), f32),
+            acc_down=pltpu.VMEM((rows, units), f32),
+            t_n2=bf(512, rows),
+            t_g=bf(512, rows),
+        )
+
+    def slot_qkv(n):
+        return pl.multiple_of(turn_of(n, 3) * qkv, 128)
+
+    def tile_qkv(n):
+        at, first = aligned(n, 256), slot_qkv(n)
+        copies = (
+            pltpu.make_async_copy(
+                r.wq_hbm.at[at],
+                r.wout.at[0:256, pl.ds(first, heads_width)],
+                r.w_rows_sem.at[turn_of(n, 3)],
+            ),
+            pltpu.make_async_copy(
+                r.wkv_hbm.at[at],
+                r.wout.at[0:256, pl.ds(pl.multiple_of(first + heads_width, 128), 128)],
+                r.w_kv_sem.at[turn_of(n, 3)],
+            ),
+        )
+        return types.SimpleNamespace(
+            start=lambda: [copy.start() for copy in copies],
+            wait=lambda: [copy.wait() for copy in copies],
+        )
+
+    def back_through_norm(b, values, gain_ref, gain_row, emit):
+        square = jnp.zeros((quarter, 1), f32)
+        inner = jnp.zeros((quarter, 1), f32)
+        for c in range(chunks):
+            at = slice(c * span, (c + 1) * span)
+            v = values[:, at].astype(f32)
+            square = square + jnp.sum(v * v, -1, keepdims=True)
+            inner = inner + jnp.sum(r.own_fin[b, c] * gain_ref[:, at] * v, -1, keepdims=True)
+        inverse = lax.rsqrt(square / width + epsilon)
+        slope = inner / width * (inverse * inverse * inverse)
+        for c in range(chunks):
+            at = slice(c * span, (c + 1) * span)
+            v = values[:, at].astype(f32)
+            dn = r.own_fin[b, c]
+            r.gain_sum[0, gain_row : gain_row + 1, at] = jnp.sum(
+                dn * v * inverse, 0, keepdims=True
+            )
+            emit(at, inverse * dn * gain_ref[:, at] - v * slope)
+
+    if swap:
+        is_end = (place == 0) | (place == 3)
+        is_mid = jnp.logical_not(is_end)
+        io_mate, across_mate = {"context": beside}, {"context": 3 - place}
+        sets = 2
+
+        def unit(u):
+            if u == 0:
+                cut = (r.n1_gb.at[:, mine_cols], r.gb_o)
+                other = r.other_kept.at[:, 0:heads_width]
+                return (cut, r.att_low, other, heads_width, r.dwout_out)
+            cut = (r.n1_out.at[:, mine_cols], r.n1_o)
+            return (cut, r.gqkv, r.other_kept, qkv, r.dwqkv_out)
+
+        def cut_loads(u):
+            own, other = unit(u)[0]
+            return (
+                pltpu.make_async_copy(own, r.cut.at[0:rows], r.cut_sem.at[0]),
+                pltpu.make_async_copy(other, r.cut.at[rows : 2 * rows], r.cut_sem.at[1]),
+            )
+
+        def piece(ref, s, j, u):
+            return ref.at[s, j, :, 0 : unit(u)[3]]
+
+        def line_copy(u, j, slot, mate):
+            s = u % sets
+            return remote(
+                piece(r.stage, s, j, u), (r.got_out, r.got_qkv)[u].at[slot], r.unit_send.at[s, j],
+                r.unit_recv.at[s, slot], mate,
+            )
+
+        def result(u):
             return pltpu.make_async_copy(
-                r.wdown_hbm.at[:, aligned(n, 256)], r.w_cols.at[slot], r.w_cols_sem.at[slot]
-            )
-
-        def tile_qkv(n):
-            slot = turn_of(n, 3)
-            at = aligned(n, 256)
-            copies = (
-                pltpu.make_async_copy(
-                    r.wq_hbm.at[at], r.w_rows.at[slot, :, 0:heads_width], r.w_rows_sem.at[slot]
-                ),
-                pltpu.make_async_copy(
-                    r.wkv_hbm.at[at],
-                    r.w_rows.at[slot, :, heads_width : heads_width + 128],
-                    r.w_kv_sem.at[slot],
-                ),
-            )
-            return types.SimpleNamespace(
-                start=lambda: [copy.start() for copy in copies],
-                wait=lambda: [copy.wait() for copy in copies],
-            )
-
-        def back_through_norm(b, values, gain_ref, gain_row, emit):
-            square = jnp.zeros((quarter, 1), f32)
-            inner = jnp.zeros((quarter, 1), f32)
-            for c in range(chunks):
-                at = slice(c * span, (c + 1) * span)
-                v = values[:, at].astype(f32)
-                square = square + jnp.sum(v * v, -1, keepdims=True)
-                inner = inner + jnp.sum(r.own_fin[b, c] * gain_ref[:, at] * v, -1, keepdims=True)
-            inverse = lax.rsqrt(square / width + epsilon)
-            slope = inner / width * (inverse * inverse * inverse)
-            for c in range(chunks):
-                at = slice(c * span, (c + 1) * span)
-                v = values[:, at].astype(f32)
-                dn = r.own_fin[b, c]
-                r.gain_sum[0, gain_row : gain_row + 1, at] = jnp.sum(
-                    dn * v * inverse, 0, keepdims=True
+                r.sums.at[u % sets, :, 0 : unit(u)[3]], unit(u)[4], r.sums_sem.at[u % sets]
+            )
+
+        def prepare(u):
+            s = u % sets
+            own, other, width_u = unit(u)[1], unit(u)[2], unit(u)[3]
+            for copy in cut_loads(u):
+                copy.wait()
+
+            @pl.loop(0, 4)
+            def _(j):
+                chunk = jnp.where(
+                    j == 0,
+                    jnp.where(low_side, 3, 0),
+                    jnp.where(
+                        j == 1, jnp.where(low_side, 2, 1), jnp.where(j == 2, beside, place)
+                    ),
                 )
-                emit(at, inverse * dn * gain_ref[:, at] - v * slope)
-
-        if swap:
-            is_end = (place == 0) | (place == 3)
-            is_mid = jnp.logical_not(is_end)
-            beside = place + 1 - 2 * lax.rem(place, 2)
-            low_side = place < 2
-            io_mate, across_mate = {"context": beside}, {"context": 3 - place}
-            swap_gqkv = swap_copy(r.gqkv, r.gqkv_o)
-            plan = []
-            for i, (at, size) in enumerate(hid_cuts):
-                cut = (r.g_hbm.at[:, mine_cols], r.g_o) if i == 0 else None
-                plan.append(
-                    (cut, r.hid.at[:, at : at + size], r.hid_o.at[i], size,
-                     r.dwdown_out.at[:, at : at + size])
-                )
-            for i, (at, size) in enumerate(gg_cuts):
-                cut = (r.x_n2.at[:, mine_cols], r.n2_o) if i == 0 else None
-                plan.append(
-                    (cut, r.gg.at[:, at : at + size], r.gg_o.at[i], size,
-                     r.dgu_out.at[:, at : at + size])
-                )
-            cut = (r.n1_gb.at[:, mine_cols], r.gb_o)
-            plan.append((cut, r.att_low, r.att_o, heads_width, r.dwout_out))
-            cut = (r.n1_out.at[:, mine_cols], r.n1_o)
-            plan.append((cut, r.gqkv, r.gqkv_o, r.gqkv.shape[1], r.dwqkv_out))
-            sets = r.stage.shape[0]
-            last = len(plan) - 1
-            first_gg = len(hid_cuts)
-
-            def cut_loads(u):
-                own, other = plan[u][0]
-                return (
-                    pltpu.make_async_copy(own, r.cut.at[0:rows], r.cut_sem.at[0]),
-                    pltpu.make_async_copy(other, r.cut.at[rows : 2 * rows], r.cut_sem.at[1]),
-                )
-
-            def piece(ref, s, j, u):
-                return ref.at[s, j, :, 0 : plan[u][3]]
-
-            def line_copy(u, j, slot, mate):
-                s = u % sets
-                return remote(
-                    piece(r.stage, s, j, u), piece(r.got, s, slot, u), r.line_send.at[s, j],
-                    r.line_recv.at[s, slot], mate,
-                )
-
-            def result(u):
-                return pltpu.make_async_copy(
-                    r.sums.at[u % sets, :, 0 : plan[u][3]], plan[u][4], r.sums_sem.at[u % sets]
-                )
-
-            def prepare(u):
-                s = u % sets
-                own, other, width_u = plan[u][1], plan[u][2], plan[u][3]
-                if u >= sets:
-                    for j in range(3):
-                        line_copy(u - sets, j, 0, io_mate).wait_send()
-                    result(u - sets).wait()
-                    pl.when(is_end)(lambda: pl.semaphore_wait(r.io_credit, 1))
-                if plan[u][0] is not None:
-                    for copy in cut_loads(u):
-                        copy.wait()
-
-                @pl.loop(0, 4)
-                def _(j):
-                    chunk = jnp.where(
-                        j == 0,
-                        jnp.where(low_side, 3, 0),
-                        jnp.where(
-                            j == 1, jnp.where(low_side, 2, 1), jnp.where(j == 2, beside, place)
-                        ),
+                for i in range(2):
+                    cut = r.cut[i * rows : (i + 1) * rows, aligned(chunk, 256)]
+                    r.t_n2[i * 256 : i * 256 + 256, :] = cut.astype(f32).T.astype(bf16)
+
+                def block(at):
+                    term = dot(r.t_n2[0:256], own[:, at]) + dot(
+                        r.t_n2[256:512], other[:, at]
                     )
-                    r.turned[...] = r.cut[:, aligned(chunk, 256)].astype(f32).T.astype(bf16)
-
-                    def block(at):
-                        term = dot(r.turned[:, 0:rows], own[:, at]) + dot(
-                            r.turned[:, rows : 2 * rows], other[:, at]
-                        )
-
-                        @pl.when(j < 3)
-                        def _():
-                            r.stage[s, j, :, at] = term.astype(bf16)
-
-                        @pl.when(j == 3)
-                        def _():
-                            r.sums[s, :, at] = term
-
-                    @pl.loop(0, width_u // 256)
-                    def _(tile):
-                        block(aligned(tile, 256))
-
-                    if width_u % 256:
-                        block(slice(width_u - width_u % 256, width_u))
-
-                    @pl.when((j < 3) & is_end)
+
+                    @pl.when(j < 3)
                     def _():
-                        line_copy(u, j, j, io_mate).start()
-
-            def add_in(u, j, slot):
-                width_u, s = plan[u][3], u % sets
-                line_copy(u, 0, slot, io_mate).wait_recv()
+                        r.stage[s, j, :, at] = term.astype(bf16)
+
+                    @pl.when(j == 3)
+                    def _():
+                        r.sums[s, :, at] = term
+
+                @pl.loop(0, width_u // 256)
+                def _(tile):
+                    block(aligned(tile, 256))
+
+                if width_u % 256:
+                    block(slice(width_u - width_u % 256, width_u))
+
+                @pl.when((j < 3) & is_end)
+                def _():
+                    line_copy(u, j, j, io_mate).start()
+
+        def add_in(u, j, slot):
+            width_u, s = unit(u)[3], u % sets
+            line_copy(u, 0, slot, io_mate).wait_recv()
+
+            @pl.loop(0, 4)
+            def _(i):
+                at = aligned(i, 64)
+                total = r.stage[s, j, at, 0:width_u].astype(f32)
+                total = total + (r.got_out, r.got_qkv)[u][slot, at, :].astype(f32)
+                r.stage[s, j, at, 0:width_u] = total.astype(bf16)
+
+        def pass_on(u, step):
+            @pl.when(is_mid)
+            def _():
+                if step < 2:
+                    add_in(u, step, step)
+                    line_copy(u, step, 3 + step, across_mate).start()
+                else:
+                    add_in(u, 2, 3)
+                    line_copy(u, 2, 0, io_mate).start()
+
+        def complete(u):
+            width_u, s = unit(u)[3], u % sets
+
+            def take(slots):
+                for slot in slots:
+                    line_copy(u, 0, slot, io_mate).wait_recv()
 
                 @pl.loop(0, 4)
                 def _(i):
                     at = aligned(i, 64)
-                    total = r.stage[s, j, at, 0:width_u].astype(f32)
-                    total = total + r.got[s, slot, at, 0:width_u].astype(f32)
-                    r.stage[s, j, at, 0:width_u] = total.astype(bf16)
-
-            def pass_on(u, step):
-                @pl.when(is_mid)
-                def _():
-                    if step < 2:
-                        add_in(u, step, step)
-                        if u >= sets and step == 0:
-                            pl.semaphore_wait(r.across_credit, 1)
-                        line_copy(u, step, 3 + step, across_mate).start()
-                    else:
-                        add_in(u, 2, 3)
-                        if u >= sets:
-                            pl.semaphore_wait(r.io_credit, 1)
-                        line_copy(u, 2, 0, io_mate).start()
-
-            def complete(u):
-                width_u, s = plan[u][3], u % sets
-
-                def take(slots):
+                    total = r.sums[s, at, 0:width_u]
                     for slot in slots:
-                        line_copy(u, 0, slot, io_mate).wait_recv()
-
-                    @pl.loop(0, 4)
-                    def _(i):
-                        at = aligned(i, 64)
-                        total = r.sums[s, at, 0:width_u]
-                        for slot in slots:
-                            total = total + r.got[s, slot, at, 0:width_u].astype(f32)
-                        r.sums[s, at, 0:width_u] = total
-
-                @pl.when(is_end)
-                def _():
-                    take((0,))
-
-                @pl.when(is_mid)
-                def _():
-                    take((2, 4))
-
-                result(u).start()
-                if u + sets <= last:
-                    pl.semaphore_signal(r.io_credit, inc=1, device_id=io_mate, device_id_type=MESH)
-
-                    @pl.when(is_mid)
-                    def _():
-                        pl.semaphore_signal(
-                            r.across_credit, inc=1, device_id=across_mate, device_id_type=MESH
-                        )
-
-            swap_g.wait_recv()
-            for copy in cut_loads(0):
-                copy.start()
-        for n in range(3):
-            tile_down(n).start()
-            tile_qkv(n).start()
+                        total = total + (r.got_out, r.got_qkv)[u][slot, at, :].astype(f32)
+                    r.sums[s, at, 0:width_u] = total
+
+            @pl.when(is_end)
+            def _():
+                take((0,))
+
+            @pl.when(is_mid)
+            def _():
+                take((2, 4))
+
+            result(u).start()
+
+    def rest(wdown, other_block):
         r.gain_sum[...] = jnp.zeros_like(r.gain_sum)
 
-        if swap:
-            swap_hid[0][0].wait_recv()
-            swap_hid[1][0].wait_recv()
-            prepare(0)
         finish_sum(0)
         load_g_own.wait()
         for i in range(1, len(stores)):
             store_copy(i).wait()
 
         def keep_resid(at, grad):
-            total = r.g_own[:, at].astype(f32) + grad
-            r.grad_resid[:, at] = total
-            r.n1_gb[mine, at] = total.astype(bf16)
+            r.n1_gb[mine, at] = (r.g_own[:, at].astype(f32) + grad).astype(bf16)
 
         back_through_norm(0, r.resid, r.gain_two, 1, keep_resid)
         gb_chip, gb_core, gb_onward = gather(0, r.n1_gb.at[mine, :], r.n1_gb)
         gb_chip.start()
         gb_core.start()
-        if swap:
-            swap_gb.start()
-        start_sum(1, tile_down, lambda n: dot(r.hid[...], r.w_cols[turn_of(n, 3)]), False)
-        for c in range(chunks):
-            x_copy(1, c).start()
-        if swap:
-            pass_on(0, 0)
-            swap_hid[0][1].wait_recv()
-            swap_hid[1][1].wait_recv()
-            prepare(1)
-            pass_on(0, 1)
+        start_sum(0, None, lambda n: dot(r.hid[...], wdown[:, aligned(n, 256)]))
+        if swap:
+            pl.semaphore_signal(r.side_credit, inc=1, device_id=dp_mate, device_id_type=MESH)
+            other_block(0)
         gb_chip.wait_recv()
         gb_onward.start()
         if swap:
-            swap_n2.wait_recv()
-            n2_chip, n2_core, n2_onward = gather(3, r.n2_o.at[mine, :], r.n2_o)
-            n2_chip.start()
-            n2_core.start()
+            spread_onward(0, 1)
+            for a, i in ((1, 1), (0, 2), (1, 2)):
+                spread_start(a, i)
         gb_core.wait_recv()
         gb_onward.wait_recv()
         if swap:
-            swap_low.wait_recv()
-            late = pltpu.make_async_copy(r.low_o, r.att_o, r.late_sem)
-            late.start()
+            swap_gb.start()
         else:
-            late = pltpu.make_async_copy(r.n1_gb, r.gb_out, r.late_sem)
-            late.start()
+            gb_store = pltpu.make_async_copy(r.n1_gb, r.gb_out, r.cut_sem.at[0])
+            gb_store.start()
+        pl.run_scoped(
+            attention_back,
+            ga=bf(rows, heads_width),
+            bias=fl(rows, rows),
+            delta=fl(heads_width // HD, 1, rows),
+            keys=bf(2, rows, 128),
+            vals=bf(2, rows, 128),
+            keys_t=bf(HD, rows),
+            dk=fl(2, rows, 128),
+            dv=fl(2, rows, 128),
+        )
+        for n in range(3):
+            tile_qkv(n).start()
+        last_part = functools.partial(
+            closing, other_block, gb_chip, gb_core, gb_onward
+        )
+        if swap:
+            pl.run_scoped(
+                last_part,
+                other_kept=bf(rows, qkv),
+                cut=bf(2 * rows, width // 2),
+                stage=bf(2, 3, 256, qkv),
+                sums=fl(2, 256, qkv),
+            )
+        else:
+            last_part()
+            gb_store.wait()
+
+    def attention_back(**scoped):
+        vars(r).update(scoped)
 
         for i in range(heads_width // 256):
             at = slice(i * 256, i * 256 + 256)
@@ -722,10 +880,7 @@
             for e in range(2):
                 r.delta[pair * 2 + e] = jnp.sum(product[64 * e : 64 * e + 64], 0, keepdims=True)
 
-        if swap:
-            pass_on(0, 2)
-
-        r.dq[...] = jnp.zeros_like(r.dq)
+        r.att[...] = jnp.zeros_like(r.att)
 
         def back_block(k, first):
             mask(r.bias, k, first)
@@ -749,7 +904,7 @@
                     grad_scores = (probs * (grad_probs - r.delta[head])).astype(bf16)
                     r.dv[e] += dot(probs.astype(bf16), pair_ga)
                     r.dk[e] += dot(grad_scores, pair_q)
-                    r.dq[aligned(head, 64), :] += dot(r.keys_t[...], grad_scores)
+                    r.att[aligned(head, 64), :] += dot(r.keys_t[...], grad_scores)
 
             return jnp.where(
                 key_lane,
@@ -757,36 +912,29 @@
                 r.dv[1] + pltpu.roll(r.dv[0], 64, 1),
             )
 
-        def dkv_copy(k, mate):
-            return remote(
-                r.stage_kv.at[k], r.got_kv.at[k], r.dkv_send.at[k], r.dkv_recv.at[k],
-                {"context": mate},
-            )
-
         @pl.loop(0, place)
         def _(i):
             k = place - i
-            r.stage_kv[k] = back_block(k, False).astype(bf16)
+            r.kv[k] = back_block(k, False).astype(bf16)
             dkv_copy(k, i).start()
 
-        r.dkv[...] = back_block(0, True)
-        if swap:
-            pass_on(1, 0)
-            pass_on(1, 1)
-            n2_chip.wait_recv()
-            n2_onward.start()
-            n2_core.wait_recv()
-            n2_onward.wait_recv()
-            for copy in cut_loads(first_gg):
-                copy.start()
-            swap_gg[0].wait_recv()
-            prepare(2)
-            complete(0)
+        r.tmp[:, 0:128] = back_block(0, True)
+
+    def closing(other_block, gb_chip, gb_core, gb_onward, **scoped):
+        vars(r).update(scoped)
+        last_exchange, own_share, finish_shares, last_step = r.share_tools
+        if swap:
+            spread_onward(1, 1)
+            swap_low.wait_recv()
+            low_load = pltpu.make_async_copy(
+                r.low_o, r.other_kept.at[:, 0:heads_width], r.late_sem
+            )
+            low_load.start()
 
         @pl.loop(0, heads_width // 128)
         def _(pair):
             at = aligned(pair, 128)
-            turned = turn(r.dq[at, :].T * 0.125, r.cos[...], -r.sin[...])
+            turned = turn(r.att[at, :].T * 0.125, r.cos[...], -r.sin[...])
             r.gqkv[:, at] = turned.astype(bf16)
 
         for k in (1, 2, 3):
@@ -794,78 +942,98 @@
             @pl.when(place + k < 4)
             def _():
                 dkv_copy(k, 0).wait_recv()
-                r.dkv[...] += r.got_kv[k].astype(f32)
+                r.tmp[:, 0:128] += r.got_kv[k].astype(f32)
 
         r.gqkv[:, heads_width : heads_width + 128] = turn(
-            r.dkv[...], jnp.where(key_lane, r.cos[...], 1.0), jnp.where(key_lane, -r.sin[...], 0.0)
+            r.tmp[:, 0:128],
+            jnp.where(key_lane, r.cos[...], 1.0),
+            jnp.where(key_lane, -r.sin[...], 0.0),
         ).astype(bf16)
         if swap:
             swap_gqkv.start()
-            swap_n1.start()
-            pass_on(1, 2)
         else:
             gqkv_store = pltpu.make_async_copy(r.gqkv, r.gqkv_out, r.cut_sem.at[1])
             gqkv_store.start()
 
-        start_sum(0, tile_qkv, lambda n: dot_t(r.gqkv[...], r.w_rows[turn_of(n, 3)]))
-        if swap:
-            swap_gg[1].wait_recv()
-            prepare(3)
-            complete(1)
-            pass_on(2, 0)
-
         finish_sum(0)
-
-        def keep_tokens(at, grad):
-            r.tokens_own[:, at] = (r.grad_resid[:, at] + grad).astype(bf16)
-
-        back_through_norm(0, r.x_own, r.gain_one, 0, keep_tokens)
-        tokens_chip, tokens_core, tokens_onward = gather(2, r.tokens_own, r.tokens_out)
-        tokens_store = pltpu.make_async_copy(
-            r.tokens_own, r.tokens_out.at[mine, :], r.out_sem.at[1]
-        )
-        for copy in (tokens_chip, tokens_core, tokens_store):
-            copy.start()
-        if swap:
-            pass_on(2, 1)
-            pass_on(2, 2)
-            swap_gg[2].wait_recv()
-            prepare(4)
-
-        finish_sum(1)
         for c in range(chunks):
             at = slice(c * span, (c + 1) * span)
-            r.mixed_own[:, at] = (r.resid[:, at] + r.own_fin[1, c]).astype(bf16)
-        mixed_chip, mixed_core, mixed_onward = gather(1, r.mixed_own, r.mixed_out)
-        mixed_store = pltpu.make_async_copy(r.mixed_own, r.mixed_out.at[mine, :], r.out_sem.at[0])
-        for copy in (mixed_chip, mixed_core, mixed_store):
+            r.g_own[:, at] = (r.resid[:, at] + r.own_fin[0, c]).astype(bf16)
+        mixed_chip, mixed_core, mixed_onward = gather(1, r.g_own, r.mixed_out)
+        mixed_store = pltpu.make_async_copy(r.g_own, r.mixed_out.at[mine, :], r.out_sem.at[0])
+
+        start_sum(0, tile_qkv, lambda n: dot_t(r.gqkv[...], r.wout[0:256, pl.ds(slot_qkv(n), qkv)]))
+        if swap:
+            spread_onward(0, 2)
+            swap_gb.wait_recv()
+            low_load.wait()
+            for copy in cut_loads(0):
+                copy.start()
+            prepare(0)
+            swap_n1.wait_recv()
+            for copy in cut_loads(1):
+                copy.start()
+            other_block(1)
+            spread_onward(1, 2)
+            pass_on(0, 0)
+            swap_gqkv.wait_recv()
+            gqkv_load = pltpu.make_async_copy(r.gqkv_o, r.other_kept, r.late_sem)
+            gqkv_load.start()
+            gqkv_load.wait()
+            prepare(1)
+            pass_on(0, 1)
+            other_block(2, last=True)
+            pass_on(0, 2)
+            pass_on(1, 0)
+
+        finish_sum(0, last=True)
+
+        def keep_tokens(at, grad):
+            r.x_own[:, at] = (r.n1_gb[mine, at].astype(f32) + grad).astype(bf16)
+
+        back_through_norm(0, r.x_own, r.gain_one, 0, keep_tokens)
+        tokens_chip, tokens_core, tokens_onward = gather(2, r.x_own, r.tokens_out)
+        tokens_store = pltpu.make_async_copy(r.x_own, r.tokens_out.at[mine, :], r.out_sem.at[1])
+
+        def gain_copy(i):
+            mate = (core_mate, chip_mate)[i]
+            return remote(
+                r.gain_sum.at[i], r.gain_got.at[i], r.gain_send.at[i], r.gain_recv.at[i], mate
+            )
+
+        def gain_add(i):
+            gain_copy(i).wait()
+            r.gain_sum[i + 1] = r.gain_sum[i] + r.gain_got[i]
+
+        gain_copy(0).start()
+        for copy in (tokens_chip, tokens_core, tokens_store, mixed_chip, mixed_core, mixed_store):
             copy.start()
         if swap:
-            complete(2)
-            pass_on(3, 0)
-            swap_gg[3].wait_recv()
-            prepare(5)
-            swap_gb.wait_recv()
-            gbo_chip, gbo_core, gbo_onward = gather(4, r.gb_o.at[mine, :], r.gb_o)
-            gbo_chip.start()
-            gbo_core.start()
-            pass_on(3, 1)
-            pass_on(3, 2)
-
-        for i, mate in enumerate((core_mate, chip_mate)):
-            copy = remote(
-                r.gain_sum.at[i], r.gain_got.at[i], r.gain_send.at[i], r.gain_recv.at[i], mate
-            )
-            copy.start()
-            copy.wait()
-            r.gain_sum[i + 1] = r.gain_sum[i] + r.gain_got[i]
-        if swap:
-            copy = remote(
+            pass_on(1, 1)
+        gain_add(0)
+        gain_copy(1).start()
+        if swap:
+            complete(0)
+            pass_on(1, 2)
+        gain_add(1)
+        if swap:
+            across = remote(
                 r.gain_sum.at[2, :, theirs_cols], r.gain_half.at[0], r.gain_send.at[2],
                 r.gain_recv.at[2], dp_mate,
             )
-            copy.start()
-            copy.wait()
+            across.start()
+            last_exchange()
+            own_share(0, 2)
+            complete(1)
+        else:
+            r.gains_out[...] = r.gain_sum[2]
+        tokens_chip.wait_recv()
+        tokens_onward.start()
+        mixed_chip.wait_recv()
+        mixed_onward.start()
+        if swap:
+            own_share(2, last_step)
+            across.wait()
             r.gain_half[1] = r.gain_sum[2, :, mine_cols] + r.gain_half[0]
             part = half // 4
             pieces = [
@@ -878,34 +1046,7 @@
             ]
             for copy in pieces:
                 copy.start()
-            complete(3)
-        else:
-            r.gains_out[...] = r.gain_sum[2]
-        tokens_chip.wait_recv()
-        tokens_onward.start()
-        mixed_chip.wait_recv()
-        mixed_onward.start()
-        if swap:
-            gbo_chip.wait_recv()
-            gbo_onward.start()
-            gbo_core.wait_recv()
-            gbo_onward.wait_recv()
-            for copy in cut_loads(last - 1):
-                copy.start()
-            late.wait()
-            prepare(6)
-            swap_n1.wait_recv()
-            for copy in cut_loads(last):
-                copy.start()
-            for step in range(3):
-                pass_on(4, step)
-            complete(4)
-            swap_gqkv.wait_recv()
-            prepare(7)
-            for u in (5, 6, 7):
-                for step in range(3):
-                    pass_on(u, step)
-                complete(u)
+            own_share(last_step, last_step + 1)
             for copy in pieces:
                 copy.wait()
             r.gains_out[...] = (
@@ -927,49 +1068,26 @@
         for k in (1, 2, 3):
             pl.when(place >= k)(dkv_copy(k, 0).wait_send)
         if swap:
-            for copy in (
-                *swaps, n2_chip, n2_core, n2_onward, gbo_chip, gbo_core, gbo_onward
-            ):
+            for copy in (swap_low, swap_gb, swap_gqkv):
                 copy.wait_send()
-            for u in range(last + 1 - sets, last + 1):
+            for a in range(2):
+                for i in range(3):
+                    for copy in spread(a, i):
+                        copy.wait_send()
+                    for part in range(len(line_parts(i))):
+                        line_sent(a, i, part).wait_send()
+            finish_shares()
+            for u in range(2):
                 for j in range(3):
                     line_copy(u, j, 0, io_mate).wait_send()
                 result(u).wait()
         else:
-            late.wait()
             gqkv_store.wait()
 
-    bf = lambda *shape: pltpu.VMEM(shape, bf16)
-    fl = lambda *shape: pltpu.VMEM(shape, f32)
-    qkv = heads_width + 128
-    scoped = {
-        "w_rows": bf(3, 256, qkv),
-        "w_cols": bf(3, units, 256),
-        "bias": fl(rows, rows),
-        "ga": bf(rows, heads_width),
-        "delta": fl(heads_width // HD, 1, rows),
-        "dq": fl(heads_width, rows),
-        "keys": bf(2, rows, 128),
-        "vals": bf(2, rows, 128),
-        "keys_t": bf(HD, rows),
-        "dk": fl(2, rows, 128),
-        "dv": fl(2, rows, 128),
-        "dkv": fl(rows, 128),
-        "stage_kv": bf(4, rows, 128),
-        "gqkv": bf(rows, qkv),
-        "grad_resid": fl(quarter, width),
-        "mixed_own": bf(quarter, width),
-        "tokens_own": bf(quarter, width),
-    }
-    if swap:
-        scoped |= {
-            "att_o": bf(rows, heads_width),
-            "cut": bf(2 * rows, width // 2),
-            "turned": bf(256, 2 * rows),
-            "stage": bf(r.got.shape[0], 3, width // 8, lead),
-            "sums": fl(r.got.shape[0], width // 8, lead),
-        }
-    pl.run_scoped(second_half, **scoped)
+    load_wout = load(r.wout_hbm, r.wout)
+    load_x_own = load(r.x_hbm.at[mine, :], r.x_own)
+    load_g_own = load(r.g_hbm.at[mine, :], r.g_own)
+    pl.run_scoped(first_half, pltpu.VMEM((width, 2 * units), bf16))
 
 
 def layer(swap, inputs, rows, width, units, heads):
@@ -979,7 +1097,6 @@
     span = width // chunks
     wide = heads * HD
     qkv = wide + 2 * HD
-    lead, sets = 768, 3
     outs = {
         "mixed_out": ((rows, width), bf16),
         "tokens_out": ((rows, width), bf16),
@@ -992,9 +1109,10 @@
             "dgu_out": ((width // 8, 2 * units), f32),
             "dwout_out": ((width // 8, wide), f32),
             "dwqkv_out": ((width // 8, qkv), f32),
-            "g_o": ((rows, width // 2), bf16),
+            "g_z": ((4, rows, width), bf16),
+            "n2_z": ((4, rows, width), bf16),
             "low_o": ((rows, wide), bf16),
-            "n2_o": ((rows, width // 2), bf16),
+            "gqkv_o": ((rows, qkv), bf16),
             "gb_o": ((rows, width // 2), bf16),
             "n1_o": ((rows, width // 2), bf16),
         }
@@ -1025,22 +1143,21 @@
         "hid": ((rows, units), bf16),
         "gg": ((rows, 2 * units), bf16),
         "tmp": ((rows, 256), f32),
-        "stage_core": ((2, chunks, 2, quarter, span), bf16),
-        "got_core": ((2, chunks, 2, quarter, span), bf16),
-        "own_fwd": ((chunks, quarter, span), f32),
-        "own_fin": ((2, chunks, quarter, span), f32),
-        "stage_x": ((2, chunks, quarter, span), bf16),
-        "got_x": ((2, chunks, quarter, span), bf16),
+        "stage_core": ((1, chunks, 2, quarter, span), bf16),
+        "got_core": ((1, chunks, 2, quarter, span), bf16),
+        "own_fwd": ((chunks, quarter, span), bf16),
+        "own_fin": ((1, chunks, quarter, span), f32),
+        "stage_x": ((1, chunks, quarter, span), bf16),
+        "got_x": ((1, chunks, quarter, span), bf16),
         "got_kv": ((4, rows, 2 * HD), bf16),
+        "gqkv": ((rows, qkv), bf16),
         "gain_sum": ((3, 8, width), f32),
         "gain_got": ((2, 8, width), f32),
     }
     if swap:
         scratch |= {
-            "hid_o": ((-(-units // lead), rows, lead), bf16),
-            "gg_o": ((-(-2 * units // lead), rows, lead), bf16),
-            "gqkv_o": ((rows, qkv), bf16),
-            "got": ((sets, 5, width // 8, lead), bf16),
+            "got_out": ((5, width // 8, wide), bf16),
+            "got_qkv": ((5, width // 8, qkv), bf16),
             "gain_half": ((2, 8, width // 2), f32),
             "gain_piece": ((4, 8, width // 8), f32),
         }
@@ -1049,14 +1166,13 @@
         "store_sem": (5,),
         "raw_sem": (4,),
         "w_rows_sem": (3,),
-        "w_cols_sem": (3,),
         "w_kv_sem": (3,),
-        "core_send": (2, chunks),
-        "core_recv": (2, chunks),
-        "x_send": (2, chunks),
-        "x_recv": (2, chunks),
-        "ag_send": (6, 3),
-        "ag_recv": (6, 3),
+        "core_send": (1, chunks),
+        "core_recv": (1, chunks),
+        "x_send": (1, chunks),
+        "x_recv": (1, chunks),
+        "ag_send": (10, 3),
+        "ag_recv": (10, 3),
         "kv_send": (4,),
         "kv_recv": (4,),
         "dkv_send": (4,),
@@ -1069,13 +1185,20 @@
     }
     if swap:
         sems |= {
-            "dp_send": (16,),
-            "dp_recv": (16,),
-            "line_send": (sets, 3),
-            "line_recv": (sets, 5),
-            "sums_sem": (sets,),
+            "dp_send": (4,),
+            "dp_recv": (4,),
+            "line_send": (2, 4, 2),
+            "line_recv": (2, 4, 2),
+            "own_sem": (2,),
+            "block_sem": (2,),
+            "side_send": (-(-units // 256), 2),
+            "side_recv": (-(-units // 256), 2),
+            "share_sem": (-(-units // 256), 2),
+            "unit_send": (2, 3),
+            "unit_recv": (2, 5),
+            "sums_sem": (2,),
         }
-    credits = ["io_credit", "across_credit"] if swap else []
+    credits = ["core_credit", "x_credit", *(["side_credit"] if swap else [])]
     names = [*inputs, *outs, *scratch, *sems, *credits]
     anywhere = pl.BlockSpec(memory_space=pl.ANY)
     inside = pl.BlockSpec(memory_space=pltpu.VMEM)
@@ -1090,7 +1213,7 @@
             *(pltpu.SemaphoreType.REGULAR for _ in credits),
         ],
         compiler_params=pltpu.CompilerParams(
-            collective_id=0, has_side_effects=True, vmem_limit_bytes=63 * MIB
+            collective_id=0, has_side_effects=True, vmem_limit_bytes=int(63.5 * MIB)
         ),
         name="layer",
     )(*inputs.values())

time: 288 us -> 264 us (0.917)
  Pallas kernels: 285 us -> 260 us
    pallas_call x1, Pallas kernels: 276 us -> 251 us  [layer(): pl.pallas_call(functools.partial(layer_kernel, names, swap), out_shape=[j...]
where the time goes in v5:
time: 264 us; the launch traced here: 261 us
  Pallas kernels  260 us (98%)
    pallas_call x1, Pallas kernels, layer(): pl.pallas_call(functools.partial(layer_kernel, names, swap), out_shape=[j...  251 us
    pallas_call x1, Pallas kernels, finish(): pl.pallas_call(finish_kernel, out_shape=[jax.ShapeDtypeStruct(*entry) for...  9.35 us

profile of v5, /device:TPU:24, one launch (start us, length us, event | category | flops | bytes accessed | tf_op | source)
XLA Modules:
  0.0 261.3 jit_solution(15473334779078440007)
XLA Ops:
  0.6 251.1 %layer.1 = (bf16[512,2048]{1,0:T(8,128)(2,1)}, bf16[512,2048]{1,0:T(8,128)(2,1)}, f32[8,256]{1,0:T(8,128)}, bf16[512,2048]{1,0:T(8,128)(2,1)}, f32[256,1408]{1,0...) custom-call(s32[1,512]{1,0:T(1,128)} %refs_0_.1, ...), custom_call_target="tpu_custom_call" | custom-call | tf_op jit(solution)/shard_map/layer/pallas_call | solution.py:1205
  251.7 9.3 %finish.1 = (f32[1408,256]{1,0:T(8,128)}, f32[256,2,1408]{2,1,0:T(2,128)}, f32[512,256]{1,0:T(8,128)}, f32[256,512]{1,0:T(8,128)}, f32[256,1,128]{2,1,0:T(1,128)...) custom-call(f32[256,1408]{1,0:T(8,128)} %get-tuple-element.25.down_hbm, ...), custom_call_target="tpu_custom_call" | custom-call | tf_op jit(solution)/shard_map/finish/pallas_call | solution.py:1311

commit v6 on v5

--- a/solution.py
+++ b/solution.py
@@ -82,11 +82,13 @@
     core, chip = lax.rem(tensor, 2), lax.div(tensor, 2)
     core_mate = {"tensor": chip * 2 + 1 - core}
     chip_mate = {"tensor": (1 - chip) * 2 + core}
-    mates = [core_mate, chip_mate, *({"context": lax.rem(place + k, 4)} for k in (1, 2, 3))]
+    tensor_mates = (core_mate, chip_mate, {"tensor": (1 - chip) * 2 + 1 - core})
+    mates = [*tensor_mates, *({"context": lax.rem(place + k, 4)} for k in (1, 2, 3))]
     if swap:
         side = lax.axis_index("dp")
         dp_mate = {"dp": 1 - side}
-        mates.append(dp_mate)
+        mates += [dp_mate]
+        mates += [{"dp": 1 - side, "context": lax.rem(place + k, 4)} for k in (1, 2, 3)]
     mine = aligned(tensor, quarter)
     key_lane = lanes((rows, 128)) < 64
     qkv = heads_width + 128
@@ -133,6 +135,8 @@
         swap_gb = swap_copy(r.n1_gb.at[:, theirs_cols], r.gb_o)
         swap_gqkv = swap_copy(r.gqkv, r.gqkv_o)
 
+    is_end = (place == 0) | (place == 3)
+    is_mid = jnp.logical_not(is_end)
     low_side = place < 2
     beside = place + 1 - 2 * lax.rem(place, 2)
     peers = (beside, jnp.where(low_side, 2, 1), jnp.where(low_side, 3, 0))
@@ -157,6 +161,18 @@
             dst, dst, r.line_send.at[a, step, part], r.line_recv.at[a, step, part],
             {"context": peers[i]},
         )
+
+    def handed_on(a, i):
+        block = (r.g_z, r.n2_z)[a].at[peers[i], mine, :]
+        return remote(
+            block, block, r.hand_send.at[a, i - 1], r.hand_recv.at[a, i - 1], {"context": beside}
+        )
+
+    def hand_on(a, i):
+        @pl.when(is_mid)
+        def _():
+            line_got(a, i, 0).wait_recv()
+            handed_on(a, i).start()
 
     def spread(a, i):
         block = (r.g_z, r.n2_z)[a].at[peers[i]]
@@ -173,8 +189,11 @@
 
     def spread_start(a, i):
         copies = spread(a, i)
-        for part in range(len(line_parts(i))):
-            line_got(a, i, part).wait_recv()
+        if i > 0:
+            pl.when(is_end)(handed_on(a, i).wait_recv)
+        else:
+            for part in range(2):
+                line_got(a, 0, part).wait_recv()
         for copy in copies[:2]:
             copy.start()
 
@@ -240,8 +259,9 @@
                         tile(n + 3).start()
 
             core_copy(b, c).start()
-            pl.when(c > 0)(lambda: forward_chunk(c - 1))
-
+            pl.when(c > 1)(lambda: forward_chunk(c - 2))
+
+        forward_chunk(chunks - 2)
         forward_chunk(chunks - 1)
 
     def finish_sum(b, last=False):
@@ -336,9 +356,8 @@
             pl.when(place + k < 4)(kv_copy(k).start)
         if swap:
             swap_n1.start()
-            for i in range(3):
-                for part in range(len(line_parts(i))):
-                    line_sent(0, i, part).start()
+            for i, part in ((0, 0), (0, 1), (1, 0)):
+                line_sent(0, i, part).start()
 
         load_wq.wait()
 
@@ -433,6 +452,9 @@
             at = aligned(b, 128)
             gh[:, at] = dot_t(g[...], wdown[at, :])
 
+        if swap:
+            hand_on(0, 1)
+
         finish_sum(0)
         load_x_own.wait()
         square = jnp.zeros((quarter, 1), f32)
@@ -456,13 +478,13 @@
         if swap:
             own_to_line(0).start()
             own_to_line(0).wait()
-            for i in range(3):
-                line_sent(1, i, 0).start()
+            line_sent(1, 0, 0).start()
+            pl.when(is_mid)(line_sent(1, 1, 0).start)
 
         def activations(gate, up, grad):
-            sigmoid = 1.0 / (1.0 + jnp.exp(-gate))
+            sigmoid = 0.5 * jnp.tanh(0.5 * gate) + 0.5
             active = gate * sigmoid
-            grad_gate = grad * up * (sigmoid * (1.0 + gate * (1.0 - sigmoid)))
+            grad_gate = (grad * up) * (sigmoid + active * (1.0 - sigmoid))
             both = jnp.concatenate([grad_gate, grad * active], 1)
             return (active * up).astype(bf16), both.astype(bf16)
 
@@ -482,6 +504,7 @@
             own_to_line(1).start()
             own_to_line(1).wait()
             line_sent(1, 0, 1).start()
+            pl.when(is_end)(line_sent(1, 1, 0).start)
         onward.wait_recv()
         units_of(aligned(1 - chip, 2 * quarter))
         if not swap:
@@ -492,7 +515,7 @@
         for copy in (to_chip, to_core, onward):
             copy.wait_send()
         if swap:
-            spread_start(0, 1)
+            hand_on(0, 2)
 
         steps = [(at, min(256, units - at)) for at in range(0, units, 256)]
         whole = units // 256
@@ -538,11 +561,13 @@
                 for i, (ref, at) in enumerate(((r.gg, gu), (r.hid, down)))
             )
 
-        def other_block(i, last=False):
+        def block_start(i):
             for a in range(2):
                 spread_wait(a, i)
             for copy in block_loads(i):
                 copy.start()
+
+        def other_block(i, last=False):
             for copy in block_loads(i):
                 copy.wait()
             turn_block()
@@ -551,20 +576,24 @@
 
             def body(offset, size, step):
                 gu, down = pl.ds(2 * offset, 2 * size), pl.ds(offset, size)
-                wide = dot(r.x_n2[...], wgu[:, gu])
-                grad = dot_t(g[...], wdown[down, :])
-                parts = [
-                    activations(
-                        wide[:, 2 * q : 2 * q + 128],
-                        wide[:, 2 * q + 128 : 2 * q + 256],
-                        grad[:, q : q + 128],
-                    )
-                    for q in range(0, size, 128)
-                ]
-                hid = jnp.concatenate([part[0] for part in parts], 1)
-                gg = jnp.concatenate([part[1] for part in parts], 1)
-                acc_gu[:, gu] += dot(t_n2[...], gg)
-                acc_down[:, down] += dot(t_g[...], hid)
+                terms = []
+                for h in range(2):
+                    at = slice(h * 256, h * 256 + 256)
+                    wide = dot(r.x_n2[at, :], wgu[:, gu])
+                    grad = dot_t(g[at, :], wdown[down, :])
+                    parts = [
+                        activations(
+                            wide[:, 2 * q : 2 * q + 128],
+                            wide[:, 2 * q + 128 : 2 * q + 256],
+                            grad[:, q : q + 128],
+                        )
+                        for q in range(0, size, 128)
+                    ]
+                    hid = jnp.concatenate([part[0] for part in parts], 1)
+                    gg = jnp.concatenate([part[1] for part in parts], 1)
+                    terms.append((dot(t_n2[:, at], gg), dot(t_g[:, at], hid)))
+                acc_gu[:, gu] += terms[0][0] + terms[1][0]
+                acc_down[:, down] += terms[0][1] + terms[1][1]
                 if last:
                     r.gg[0:256, gu] = acc_gu[256:512, gu].astype(bf16)
                     r.hid[0:256, down] = acc_down[256:512, down].astype(bf16)
@@ -615,10 +644,10 @@
         start_sum(0, None, lambda n: dot_t(r.gg[...], wgu[aligned(n, 256), :]))
         if swap:
             own_block()
-            for a in range(2):
-                spread_start(a, 0)
+            hand_on(1, 1)
+            spread_start(0, 0)
         r.share_tools = (last_exchange, own_share, finish_shares, len(steps) - 1)
-        rest(wdown, other_block)
+        rest(wdown, block_start, other_block)
 
     def first_half(wgu):
         pl.run_scoped(
@@ -682,8 +711,6 @@
             emit(at, inverse * dn * gain_ref[:, at] - v * slope)
 
     if swap:
-        is_end = (place == 0) | (place == 3)
-        is_mid = jnp.logical_not(is_end)
         io_mate, across_mate = {"context": beside}, {"context": 3 - place}
         sets = 2
 
@@ -806,7 +833,8 @@
 
             result(u).start()
 
-    def rest(wdown, other_block):
+    def rest(wdown, block_start, other_block):
+        r.wdown = wdown
         r.gain_sum[...] = jnp.zeros_like(r.gain_sum)
 
         finish_sum(0)
@@ -821,16 +849,20 @@
         gb_chip, gb_core, gb_onward = gather(0, r.n1_gb.at[mine, :], r.n1_gb)
         gb_chip.start()
         gb_core.start()
-        start_sum(0, None, lambda n: dot(r.hid[...], wdown[:, aligned(n, 256)]))
+        if swap:
+            spread_start(1, 0)
+        start_sum(0, None, lambda n: dot(r.hid[...], r.wdown[:, aligned(n, 256)]))
         if swap:
             pl.semaphore_signal(r.side_credit, inc=1, device_id=dp_mate, device_id_type=MESH)
+            block_start(0)
             other_block(0)
+            hand_on(1, 2)
         gb_chip.wait_recv()
         gb_onward.start()
         if swap:
-            spread_onward(0, 1)
-            for a, i in ((1, 1), (0, 2), (1, 2)):
-                spread_start(a, i)
+            spread_start(0, 1)
+            spread_start(1, 1)
+            spread_start(0, 2)
         gb_core.wait_recv()
         gb_onward.wait_recv()
         if swap:
@@ -852,7 +884,7 @@
         for n in range(3):
             tile_qkv(n).start()
         last_part = functools.partial(
-            closing, other_block, gb_chip, gb_core, gb_onward
+            closing, block_start, other_block, gb_chip, gb_core, gb_onward
         )
         if swap:
             pl.run_scoped(
@@ -920,11 +952,12 @@
 
         r.tmp[:, 0:128] = back_block(0, True)
 
-    def closing(other_block, gb_chip, gb_core, gb_onward, **scoped):
+    def closing(block_start, other_block, gb_chip, gb_core, gb_onward, **scoped):
         vars(r).update(scoped)
         last_exchange, own_share, finish_shares, last_step = r.share_tools
         if swap:
-            spread_onward(1, 1)
+            spread_onward(0, 1)
+            spread_start(1, 2)
             swap_low.wait_recv()
             low_load = pltpu.make_async_copy(
                 r.low_o, r.other_kept.at[:, 0:heads_width], r.late_sem
@@ -955,6 +988,11 @@
             gqkv_store = pltpu.make_async_copy(r.gqkv, r.gqkv_out, r.cut_sem.at[1])
             gqkv_store.start()
 
+        if swap:
+            spread_onward(1, 1)
+            swap_gb.wait_recv()
+            for copy in cut_loads(0):
+                copy.start()
         finish_sum(0)
         for c in range(chunks):
             at = slice(c * span, (c + 1) * span)
@@ -964,26 +1002,24 @@
 
         start_sum(0, tile_qkv, lambda n: dot_t(r.gqkv[...], r.wout[0:256, pl.ds(slot_qkv(n), qkv)]))
         if swap:
+            block_start(1)
             spread_onward(0, 2)
-            swap_gb.wait_recv()
             low_load.wait()
-            for copy in cut_loads(0):
-                copy.start()
             prepare(0)
             swap_n1.wait_recv()
             for copy in cut_loads(1):
                 copy.start()
             other_block(1)
             spread_onward(1, 2)
-            pass_on(0, 0)
             swap_gqkv.wait_recv()
             gqkv_load = pltpu.make_async_copy(r.gqkv_o, r.other_kept, r.late_sem)
             gqkv_load.start()
             gqkv_load.wait()
             prepare(1)
+            block_start(2)
+            pass_on(0, 0)
+            other_block(2, last=True)
             pass_on(0, 1)
-            other_block(2, last=True)
-            pass_on(0, 2)
             pass_on(1, 0)
 
         finish_sum(0, last=True)
@@ -995,66 +1031,57 @@
         tokens_chip, tokens_core, tokens_onward = gather(2, r.x_own, r.tokens_out)
         tokens_store = pltpu.make_async_copy(r.x_own, r.tokens_out.at[mine, :], r.out_sem.at[1])
 
-        def gain_copy(i):
-            mate = (core_mate, chip_mate)[i]
-            return remote(
-                r.gain_sum.at[i], r.gain_got.at[i], r.gain_send.at[i], r.gain_recv.at[i], mate
-            )
-
-        def gain_add(i):
-            gain_copy(i).wait()
-            r.gain_sum[i + 1] = r.gain_sum[i] + r.gain_got[i]
-
-        gain_copy(0).start()
+        across_tensor = [
+            remote(
+                r.gain_sum.at[0], r.gain_got.at[i], r.gain_send.at[i], r.gain_recv.at[i], mate
+            )
+            for i, mate in enumerate(tensor_mates)
+        ]
+        for copy in across_tensor:
+            copy.start()
         for copy in (tokens_chip, tokens_core, tokens_store, mixed_chip, mixed_core, mixed_store):
             copy.start()
         if swap:
             pass_on(1, 1)
-        gain_add(0)
-        gain_copy(1).start()
-        if swap:
+        for copy in across_tensor:
+            copy.wait()
+        r.gain_sum[1] = (r.gain_sum[0] + r.gain_got[0]) + (r.gain_got[1] + r.gain_got[2])
+        if swap:
+            part = width // 8
+            pieces = []
+            for i in range(1, 8):
+                to_side = side if i < 4 else 1 - side
+                to_place = lax.rem(place + i, 4)
+                pieces.append(
+                    remote(
+                        r.gain_sum.at[1, :, aligned(to_side * 4 + to_place, part)],
+                        r.gain_piece.at[i], r.gain_send.at[2 + i], r.gain_recv.at[2 + i],
+                        {"dp": to_side, "context": to_place},
+                    )
+                )
+            for copy in pieces:
+                copy.start()
+            last_exchange()
+            pass_on(0, 2)
+        else:
+            r.gains_out[...] = r.gain_sum[1]
+        tokens_chip.wait_recv()
+        tokens_onward.start()
+        if swap:
+            pass_on(1, 2)
             complete(0)
-            pass_on(1, 2)
-        gain_add(1)
-        if swap:
-            across = remote(
-                r.gain_sum.at[2, :, theirs_cols], r.gain_half.at[0], r.gain_send.at[2],
-                r.gain_recv.at[2], dp_mate,
-            )
-            across.start()
-            last_exchange()
+        mixed_chip.wait_recv()
+        mixed_onward.start()
+        if swap:
             own_share(0, 2)
             complete(1)
-        else:
-            r.gains_out[...] = r.gain_sum[2]
-        tokens_chip.wait_recv()
-        tokens_onward.start()
-        mixed_chip.wait_recv()
-        mixed_onward.start()
-        if swap:
-            own_share(2, last_step)
-            across.wait()
-            r.gain_half[1] = r.gain_sum[2, :, mine_cols] + r.gain_half[0]
-            part = half // 4
-            pieces = [
-                remote(
-                    r.gain_half.at[1, :, aligned(lax.rem(place + k, 4), part)],
-                    r.gain_piece.at[k], r.gain_send.at[2 + k], r.gain_recv.at[2 + k],
-                    {"context": lax.rem(place + k, 4)},
-                )
-                for k in (1, 2, 3)
-            ]
-            for copy in pieces:
-                copy.start()
-            own_share(last_step, last_step + 1)
+            own_share(2, last_step + 1)
             for copy in pieces:
                 copy.wait()
-            r.gains_out[...] = (
-                r.gain_half[1, :, aligned(place, part)]
-                + r.gain_piece[1]
-                + r.gain_piece[2]
-                + r.gain_piece[3]
-            )
+            total = r.gain_sum[1, :, aligned(side * 4 + place, part)]
+            for i in range(1, 8):
+                total = total + r.gain_piece[i]
+            r.gains_out[...] = total
 
         for copy in (mixed_core, mixed_onward, tokens_core, tokens_onward):
             copy.wait_recv()
@@ -1074,8 +1101,10 @@
                 for i in range(3):
                     for copy in spread(a, i):
                         copy.wait_send()
-                    for part in range(len(line_parts(i))):
-                        line_sent(a, i, part).wait_send()
+                for i, part in ((0, 0), (0, 1), (1, 0)):
+                    line_sent(a, i, part).wait_send()
+                for i in (1, 2):
+                    pl.when(is_mid)(handed_on(a, i).wait_send)
             finish_shares()
             for u in range(2):
                 for j in range(3):
@@ -1151,15 +1180,14 @@
         "got_x": ((1, chunks, quarter, span), bf16),
         "got_kv": ((4, rows, 2 * HD), bf16),
         "gqkv": ((rows, qkv), bf16),
-        "gain_sum": ((3, 8, width), f32),
-        "gain_got": ((2, 8, width), f32),
+        "gain_sum": ((2, 8, width), f32),
+        "gain_got": ((3, 8, width), f32),
     }
     if swap:
         scratch |= {
             "got_out": ((5, width // 8, wide), bf16),
             "got_qkv": ((5, width // 8, qkv), bf16),
-            "gain_half": ((2, 8, width // 2), f32),
-            "gain_piece": ((4, 8, width // 8), f32),
+            "gain_piece": ((8, 8, width // 8), f32),
         }
     sems = {
         "load_sem": (8,),
@@ -1177,8 +1205,8 @@
         "kv_recv": (4,),
         "dkv_send": (4,),
         "dkv_recv": (4,),
-        "gain_send": (6,),
-        "gain_recv": (6,),
+        "gain_send": (10,),
+        "gain_recv": (10,),
         "out_sem": (2,),
         "cut_sem": (2,),
         "late_sem": (),
@@ -1189,6 +1217,8 @@
             "dp_recv": (4,),
             "line_send": (2, 4, 2),
             "line_recv": (2, 4, 2),
+            "hand_send": (2, 2),
+            "hand_recv": (2, 2),
             "own_sem": (2,),
             "block_sem": (2,),
             "side_send": (-(-units // 256), 2),

time: 264 us -> 242 us (0.917)
  Pallas kernels: 260 us -> 241 us
    pallas_call x1, Pallas kernels: 251 us -> 231 us  [layer(): pl.pallas_call(functools.partial(layer_kernel, names, swap), out_shape=[j...]
where the time goes in v6:
time: 242 us
  Pallas kernels  241 us (100%)
    pallas_call x1, Pallas kernels, layer(): pl.pallas_call(functools.partial(layer_kernel, names, swap), out_shape=[j...  231 us
    pallas_call x1, Pallas kernels, finish(): pl.pallas_call(finish_kernel, out_shape=[jax.ShapeDtypeStruct(*entry) for...  9.35 us

profile of v6, /device:TPU:24, one launch (start us, length us, event | category | flops | bytes accessed | tf_op | source)
XLA Modules:
  0.0 241.6 jit_solution(3698224977638024660)
XLA Ops:
  0.6 231.4 %layer.1 = (bf16[512,2048]{1,0:T(8,128)(2,1)}, bf16[512,2048]{1,0:T(8,128)(2,1)}, f32[8,256]{1,0:T(8,128)}, bf16[512,2048]{1,0:T(8,128)(2,1)}, f32[256,1408]{1,0...) custom-call(s32[1,512]{1,0:T(1,128)} %refs_0_.1, ...), custom_call_target="tpu_custom_call" | custom-call | tf_op jit(solution)/shard_map/layer/pallas_call | solution.py:1235
  232.0 9.3 %finish.1 = (f32[1408,256]{1,0:T(8,128)}, f32[256,2,1408]{2,1,0:T(2,128)}, f32[512,256]{1,0:T(8,128)}, f32[256,512]{1,0:T(8,128)}, f32[256,1,128]{2,1,0:T(1,128)...) custom-call(f32[256,1408]{1,0:T(8,128)} %get-tuple-element.25.down_hbm, ...), custom_call_target="tpu_custom_call" | custom-call | tf_op jit(solution)/shard_map/finish/pallas_call | solution.py:1341

commit v7 on v6

--- a/solution.py
+++ b/solution.py
@@ -107,10 +107,11 @@
 
     loads, stores = [], []
 
-    def load(src, dst):
+    def load(src, dst, now=True):
         copy = pltpu.make_async_copy(src, dst, r.load_sem.at[len(loads)])
         loads.append(copy)
-        copy.start()
+        if now:
+            copy.start()
         return copy
 
     def store_copy(i):
@@ -328,6 +329,9 @@
 
         for i in range(ring):
             raw_copy(i).start()
+
+        for copy in (load_wout, load_x_own, load_g_own):
+            copy.start()
 
         position = place * rows + lanes((1, rows)) - r.seg[...]
         cosine, sine = cos_sin(r.freqs[...] * position.astype(f32))
@@ -520,8 +524,18 @@
         steps = [(at, min(256, units - at)) for at in range(0, units, 256)]
         whole = units // 256
 
-        def each_step(body):
-            @pl.loop(0, whole)
+        def each_step(body, pause=None):
+            first = 0
+            if pause is not None:
+                first = (whole + 1) // 2
+
+                @pl.loop(0, first)
+                def _(step):
+                    body(pl.multiple_of(step * 256, 256), 256, step)
+
+                pause()
+
+            @pl.loop(first, whole)
             def _(step):
                 body(pl.multiple_of(step * 256, 256), 256, step)
 
@@ -567,7 +581,7 @@
             for copy in block_loads(i):
                 copy.start()
 
-        def other_block(i, last=False):
+        def other_block(i, last=False, pause=None):
             for copy in block_loads(i):
                 copy.wait()
             turn_block()
@@ -603,7 +617,7 @@
                         for copy in exchange(step, size):
                             copy.start()
 
-            each_step(body)
+            each_step(body, pause)
 
         def last_exchange():
             for copy in exchange(len(steps) - 1, steps[-1][1]):
@@ -855,14 +869,19 @@
         if swap:
             pl.semaphore_signal(r.side_credit, inc=1, device_id=dp_mate, device_id_type=MESH)
             block_start(0)
-            other_block(0)
+
+            def pause():
+                gb_chip.wait_recv()
+                gb_onward.start()
+                spread_start(0, 1)
+                spread_start(1, 1)
+
+            other_block(0, pause=pause)
             hand_on(1, 2)
-        gb_chip.wait_recv()
-        gb_onward.start()
-        if swap:
-            spread_start(0, 1)
-            spread_start(1, 1)
             spread_start(0, 2)
+        else:
+            gb_chip.wait_recv()
+            gb_onward.start()
         gb_core.wait_recv()
         gb_onward.wait_recv()
         if swap:
@@ -962,7 +981,6 @@
             low_load = pltpu.make_async_copy(
                 r.low_o, r.other_kept.at[:, 0:heads_width], r.late_sem
             )
-            low_load.start()
 
         @pl.loop(0, heads_width // 128)
         def _(pair):
@@ -988,11 +1006,6 @@
             gqkv_store = pltpu.make_async_copy(r.gqkv, r.gqkv_out, r.cut_sem.at[1])
             gqkv_store.start()
 
-        if swap:
-            spread_onward(1, 1)
-            swap_gb.wait_recv()
-            for copy in cut_loads(0):
-                copy.start()
         finish_sum(0)
         for c in range(chunks):
             at = slice(c * span, (c + 1) * span)
@@ -1002,25 +1015,28 @@
 
         start_sum(0, tile_qkv, lambda n: dot_t(r.gqkv[...], r.wout[0:256, pl.ds(slot_qkv(n), qkv)]))
         if swap:
-            block_start(1)
-            spread_onward(0, 2)
-            low_load.wait()
-            prepare(0)
+            spread_onward(1, 1)
             swap_n1.wait_recv()
             for copy in cut_loads(1):
                 copy.start()
+            block_start(1)
+            spread_onward(0, 2)
             other_block(1)
             spread_onward(1, 2)
             swap_gqkv.wait_recv()
             gqkv_load = pltpu.make_async_copy(r.gqkv_o, r.other_kept, r.late_sem)
             gqkv_load.start()
             gqkv_load.wait()
+            block_start(2)
             prepare(1)
-            block_start(2)
-            pass_on(0, 0)
+            swap_gb.wait_recv()
+            for copy in (*cut_loads(0), low_load):
+                copy.start()
             other_block(2, last=True)
-            pass_on(0, 1)
+            low_load.wait()
+            prepare(0)
             pass_on(1, 0)
+            pass_on(1, 1)
 
         finish_sum(0, last=True)
 
@@ -1042,7 +1058,7 @@
         for copy in (tokens_chip, tokens_core, tokens_store, mixed_chip, mixed_core, mixed_store):
             copy.start()
         if swap:
-            pass_on(1, 1)
+            pass_on(0, 0)
         for copy in across_tensor:
             copy.wait()
         r.gain_sum[1] = (r.gain_sum[0] + r.gain_got[0]) + (r.gain_got[1] + r.gain_got[2])
@@ -1062,20 +1078,22 @@
             for copy in pieces:
                 copy.start()
             last_exchange()
-            pass_on(0, 2)
+            pass_on(1, 2)
         else:
             r.gains_out[...] = r.gain_sum[1]
         tokens_chip.wait_recv()
         tokens_onward.start()
         if swap:
-            pass_on(1, 2)
-            complete(0)
+            pass_on(0, 1)
+            complete(1)
         mixed_chip.wait_recv()
         mixed_onward.start()
         if swap:
-            own_share(0, 2)
-            complete(1)
-            own_share(2, last_step + 1)
+            own_share(0, 1)
+            pass_on(0, 2)
+            own_share(1, 3)
+            complete(0)
+            own_share(3, last_step + 1)
             for copy in pieces:
                 copy.wait()
             total = r.gain_sum[1, :, aligned(side * 4 + place, part)]
@@ -1113,9 +1131,9 @@
         else:
             gqkv_store.wait()
 
-    load_wout = load(r.wout_hbm, r.wout)
-    load_x_own = load(r.x_hbm.at[mine, :], r.x_own)
-    load_g_own = load(r.g_hbm.at[mine, :], r.g_own)
+    load_wout = load(r.wout_hbm, r.wout, False)
+    load_x_own = load(r.x_hbm.at[mine, :], r.x_own, False)
+    load_g_own = load(r.g_hbm.at[mine, :], r.g_own, False)
     pl.run_scoped(first_half, pltpu.VMEM((width, 2 * units), bf16))
 
 

time: 242 us -> 238 us (0.983)
  Pallas kernels: 241 us -> 237 us
    pallas_call x1, Pallas kernels: 231 us -> 227 us  [layer(): pl.pallas_call(functools.partial(layer_kernel, names, swap), out_shape=[j...]
where the time goes in v7:
time: 238 us; the launch traced here: 237 us
  Pallas kernels  237 us (100%)
    pallas_call x1, Pallas kernels, layer(): pl.pallas_call(functools.partial(layer_kernel, names, swap), out_shape=[j...  227 us
    pallas_call x1, Pallas kernels, finish(): pl.pallas_call(finish_kernel, out_shape=[jax.ShapeDtypeStruct(*entry) for...  9.35 us

profile of v7, /device:TPU:24, one launch (start us, length us, event | category | flops | bytes accessed | tf_op | source)
XLA Modules:
  0.0 237.5 jit_solution(278199584143401063)
XLA Ops:
  0.6 227.2 %layer.1 = (bf16[512,2048]{1,0:T(8,128)(2,1)}, bf16[512,2048]{1,0:T(8,128)(2,1)}, f32[8,256]{1,0:T(8,128)}, bf16[512,2048]{1,0:T(8,128)(2,1)}, f32[256,1408]{1,0...) custom-call(s32[1,512]{1,0:T(1,128)} %refs_0_.1, ...), custom_call_target="tpu_custom_call" | custom-call | tf_op jit(solution)/shard_map/layer/pallas_call | solution.py:1253
  227.9 9.3 %finish.1 = (f32[1408,256]{1,0:T(8,128)}, f32[256,2,1408]{2,1,0:T(2,128)}, f32[512,256]{1,0:T(8,128)}, f32[256,512]{1,0:T(8,128)}, f32[256,1,128]{2,1,0:T(1,128)...) custom-call(f32[256,1408]{1,0:T(8,128)} %get-tuple-element.25.down_hbm, ...), custom_call_target="tpu_custom_call" | custom-call | tf_op jit(solution)/shard_map/finish/pallas_call | solution.py:1359
